TPU v7x, 32 devices: a whole 2x2x4 slice. The times are simulated.
32 devices in a mesh: fsdp: 8 (over z, x), dp: 4 (over y, core).
Axes of the slice: x: 2, y: 2, z: 4, core: 2. Of those that a mesh axis runs over, the one named last changes fastest.
Arguments:
- inputs: bfloat16 [32768, 1024], P(('fsdp', 'dp')), may hold values from -6 to 6
- encoder: bfloat16 [32768, 1024], P(('fsdp', 'dp')), may hold values from -6 to 6
- cotangent: bfloat16 [32768, 1024], P(('fsdp', 'dp')), may hold values from -6 to 6
- buckets: int32 [32], P(('fsdp', 'dp')), may hold values from 0 to 2, as said below
- lengths: int32 [32, 4], P(('fsdp', 'dp')), may hold values from 0 to 1024, as said below
- self_query: bfloat16 [1024, 1024], P('fsdp'), may hold values from -0.1875 to 0.1875
- self_key: bfloat16 [1024, 1024], P('fsdp'), may hold values from -0.1875 to 0.1875
- self_value: bfloat16 [1024, 1024], P('fsdp'), may hold values from -0.1875 to 0.1875
- self_output: bfloat16 [1024, 1024], P('fsdp'), may hold values from -1.5 to 1.5
- cross_query: bfloat16 [1024, 1024], P('fsdp'), may hold values from -0.1875 to 0.1875
- cross_key: bfloat16 [1024, 1024], P('fsdp'), may hold values from -0.1875 to 0.1875
- cross_value: bfloat16 [1024, 1024], P('fsdp'), may hold values from -0.1875 to 0.1875
- cross_output: bfloat16 [1024, 1024], P('fsdp'), may hold values from -1.5 to 1.5
- fc_first: bfloat16 [1024, 4096], P('fsdp'), may hold values from -0.1875 to 0.1875
- fc_second: bfloat16 [4096, 1024], P('fsdp'), may hold values from -0.09375 to 0.09375
- norm_gains: float32 [3, 1024], replicated, may hold values from 0.5 to 1.5
- down_master: float32 [1024, 512], replicated, may hold values from -0.1875 to 0.1875
- up_master: float32 [512, 1024], replicated, may hold values from -0.0625 to 0.0625
- down_first: float32 [1024, 512], replicated, may hold values from -48 to 48
- down_second: float32 [1024, 512], replicated, may hold values from 2.62144 to 42.5984
- up_first: float32 [512, 1024], replicated, may hold values from -128 to 128
- up_second: float32 [512, 1024], replicated, may hold values from 22.9376 to 360.448
Outputs:
- outputs: bfloat16 [32768, 1024], P(('fsdp', 'dp'))
- input_grad: bfloat16 [32768, 1024], P(('fsdp', 'dp'))
- encoder_grad: bfloat16 [32768, 1024], P(('fsdp', 'dp'))
- down_grad: float32 [1024, 512], replicated
- up_grad: float32 [512, 1024], replicated
- down_first_new: float32 [1024, 512], replicated
- down_second_new: float32 [1024, 512], replicated
- up_first_new: float32 [512, 1024], replicated
- up_second_new: float32 [512, 1024], replicated
- down_master_new: float32 [1024, 512], replicated
- up_master_new: float32 [512, 1024], replicated
- down_weight: bfloat16 [1024, 512], replicated
- up_weight: bfloat16 [512, 1024], replicated
Inputs may be any that keep to these rules, and one draw needn't show every extreme that they name: `buckets`: bucket 0 holds four items of 256 slots, bucket 1 two of 512, bucket 2 one of 1024; item i of a block takes its slots i * S to (i + 1) * S - 1. 32 // 6 blocks hold bucket 0, as many hold bucket 1, the rest bucket 2. `lengths`: for the items that a block's bucket has, the length lies between max(1, S // 4) and the item size S; the other entries are 0. Some item fills all 1024 slots of its block.
All inputs are finite; a program needn't handle non-finite values.
Results may differ from a plain program's by a relative error of at most 0.02.
Values may be sent and summed in bfloat16 or wider, within the bound.
No kernel may reach another device: no remote copies, remote signals or barrier semaphores. Data moves between devices by JAX's collectives and lax.ppermute only.
A program may use at most 320 MiB of HBM per device.

v0:
```python
import functools
import math

import jax
import jax.numpy as jnp
from jax import lax
from jax.experimental import pallas as pl
from jax.experimental.pallas import tpu as pltpu
from jax.sharding import PartitionSpec as P

HEAD_DIM = 64
PAIR = 2 * HEAD_DIM
STEP = 10
SLOTS = 4

epsilon_norm = 1e-05
beta_first = 0.9
beta_second = 0.999
learn_rate = 0.05
weight_decay = 0.01
epsilon_adam = 1e-08

f32, bf16 = jnp.float32, jnp.bfloat16
query_scale = HEAD_DIM ** (-0.5) * math.log2(math.e)
forbidden = -(2.0**100)
score_limit = 64.0

params = pltpu.CompilerParams(vmem_limit_bytes=63 * 2**20)


def contract(left, right, left_dim, right_dim):
    return lax.dot_general(
        left, right, (((left_dim,), (right_dim,)), ((), ())), preferred_element_type=f32
    )


def start_loading(pieces, table_ref, wanted, store, sems, start=0):
    count = len(pieces) // 3

    def copies(group, slot, i):
        for p, piece in enumerate(pieces[group * count : (group + 1) * count]):
            rows = piece.shape[1]
            at = pl.multiple_of(table_ref[0, p], 16)
            pltpu.make_async_copy(
                piece.at[i], store.at[slot, pl.ds(at, rows)], sems.at[slot]
            ).start()

    for slot, (kind, i) in list(enumerate(wanted))[start:]:
        if kind is None:
            copies(0, slot, i)
        else:
            pl.when(table_ref[3, 0] == kind)(functools.partial(copies, 1, slot, i))
            pl.when(table_ref[3, 0] != kind)(functools.partial(copies, 2, slot, i))


def loaded(store, sems, slot):
    pltpu.make_async_copy(store.at[slot], store.at[slot], sems.at[slot]).wait()


def loaded_once(store, sems, slot):
    @pl.when(pl.program_id(0) == 0)
    def wait():
        loaded(store, sems, slot)


def cost(microseconds):
    return pl.CostEstimate(flops=int(microseconds * 1.15e9), bytes_accessed=10**5, transcendentals=0)


def share_spec(share, rows):
    return pl.BlockSpec(share.shape[:2] + (rows,), lambda i: (0, 0, i))


def in_place():
    return pl.BlockSpec(memory_space=pl.ANY)


def stores(count, width):
    return [pltpu.VMEM((count, width, width), bf16), pltpu.SemaphoreType.DMA((count,))]


smem = functools.partial(pl.BlockSpec, memory_space=pltpu.SMEM)


def spread(share_ref, width):
    pairs, two, rows = share_ref.shape
    rest = share_ref[...].reshape(pairs * two, rows)
    member = (
        lax.broadcasted_iota(jnp.int32, (pairs * two, width), 0)
        == lax.broadcasted_iota(jnp.int32, (pairs * two, width), 1) >> 6
    ).astype(bf16)
    parts = []
    for i in range(3):
        parts.append(rest.astype(bf16))
        rest = rest - parts[-1].astype(f32)
    return contract(jnp.concatenate(parts, axis=0), jnp.concatenate([member] * 3, axis=0), 0, 0)


def normalise(values):
    centre = values - jnp.mean(values, axis=-1, keepdims=True)
    inverse = lax.rsqrt(jnp.mean(centre * centre, axis=-1, keepdims=True) + epsilon_norm)
    return centre * inverse, inverse


def normalise_back(scaled, normal, inverse):
    return inverse * (
        scaled
        - jnp.mean(scaled, axis=-1, keepdims=True)
        - normal * jnp.mean(scaled * normal, axis=-1, keepdims=True)
    )


def gelu_and_slope(u):
    bell = jnp.exp2(u * u * (-0.5 * math.log2(math.e)) - 0.5 * math.log2(2.0 * math.pi))
    below = 0.5 + 0.5 * lax.erf(u * math.sqrt(0.5))
    return u * below, below + u * bell


def head_squares(values):
    width = values.shape[1]
    member = (
        lax.broadcasted_iota(jnp.int32, (width, PAIR), 0) >> 6
        == lax.broadcasted_iota(jnp.int32, (width, PAIR), 1)
    ).astype(bf16)
    return jnp.max(contract(values * values, member, 1, 0), axis=0, keepdims=True)


def project_kernel(wanted, scale, squared, count, x_ref, table_ref, *refs):
    pieces = refs[:count]
    out_ref, square_ref, store, sems = refs[-4:]
    step = pl.program_id(0)

    @pl.when(step == 0)
    def begin():
        start_loading(pieces, table_ref, wanted[:1], store, sems)
        loaded(store, sems, 0)
        start_loading(pieces, table_ref, wanted, store, sems, 1)
        out = contract(x_ref[...], store[0], 1, 0)
        out_ref[0] = (out if scale == 1.0 else out * scale).astype(bf16)

    @pl.when(step > 0)
    def more():
        loaded(store, sems, step)
        out_ref[0] = contract(x_ref[...], store[step], 1, 0).astype(bf16)

    @pl.when(step < squared)
    def squares():
        square_ref[0] = jnp.broadcast_to(head_squares(out_ref[0]), square_ref.shape[1:])

    @pl.when(step >= squared)
    def no_squares():
        square_ref[0] = jnp.zeros(square_ref.shape[1:], f32)


def project(x, table, pieces, wanted, scale, squared, sooner=()):
    tokens, width = x.shape
    count = len(wanted)
    return pl.pallas_call(
        functools.partial(project_kernel, wanted, scale, squared, len(pieces)),
        grid=(count,),
        in_specs=[pl.BlockSpec((tokens, width), lambda i: (0, 0)), smem()]
        + [in_place() for piece in (*pieces, *sooner)],
        out_specs=[
            pl.BlockSpec((1, tokens, width), lambda i: (i, 0, 0)),
            pl.BlockSpec((1, 8, PAIR), lambda i: (i, 0, 0)),
        ],
        out_shape=[
            jax.ShapeDtypeStruct((count, tokens, width), bf16),
            jax.ShapeDtypeStruct((count, 8, PAIR), f32),
        ],
        scratch_shapes=stores(count, width),
        compiler_params=params,
        cost_estimate=cost(4 * count),
        name="project",
    )(x, table, *pieces, *sooner)


def low_half(rows):
    return lax.broadcasted_iota(jnp.int32, (rows, PAIR), 1) < HEAD_DIM


def choose(head, low):
    if head == 0:
        return lambda own, other: jnp.where(low, own, other)
    return lambda own, other: jnp.where(low, other, own)


def item_shift(bucket, tokens):
    return bucket + (tokens.bit_length() - 1 - 2)


def item_length(item, lengths_ref):
    length = jnp.zeros_like(item)
    for slot in range(SLOTS):
        length = jnp.where(item == slot, lengths_ref[0, slot], length)
    return length


def attend_kernel(
    causal, q_at, k_at, start, bucket_ref, lengths_ref, qsq_ref, ksq_ref, q_ref, k_ref, v_ref, *refs
):
    out_ref, weight_ref, share_ref, done_ref, qmark, kmark = refs[-6:]
    done_ref[...] = jnp.zeros_like(done_ref)
    tokens = q_ref.shape[-2]
    low = low_half(tokens)
    pair = pl.program_id(0) + start

    @pl.when(pl.program_id(0) == 0)
    def marks():
        shift = item_shift(bucket_ref[0], tokens)
        lane = lax.broadcasted_iota(jnp.int32, (tokens, PAIR), 1) & (HEAD_DIM - 1)
        row = lax.broadcasted_iota(jnp.int32, (tokens, PAIR), 0)
        item = row >> shift
        own = lane == item
        qmark[...] = jnp.where(own, 1.0, 0.0).astype(bf16)
        allowed = own & (row - (item << shift) < item_length(item, lengths_ref))
        kmark[...] = jnp.where((lane < SLOTS) & ~allowed, forbidden, 0.0).astype(bf16)

    q, k, v = q_ref[0], k_ref[0], v_ref[0]
    one = jnp.ones((tokens, PAIR), bf16)

    def operands(head):
        own = choose(head, low)
        return own(q, qmark[...]), own(k, kmark[...]), own(v, one)

    def finish(sums):
        even, odd = sums
        even_share, odd_share = 1.0 / even[HEAD_DIM : HEAD_DIM + 8], 1.0 / odd[:8]
        out = jnp.concatenate(
            [even[:HEAD_DIM] * even_share[:1], odd[HEAD_DIM:] * odd_share[:1]], axis=0
        )
        out_ref[...] = out.astype(bf16).T
        share_ref[0, 0:1] = even_share[:1]
        share_ref[0, 1:2] = odd_share[:1]

    bound = score_limit * score_limit
    small = (
        qsq_ref[q_at, 0, 2 * pair] * ksq_ref[k_at, 0, 2 * pair] <= bound
    ) & (qsq_ref[q_at, 0, 2 * pair + 1] * ksq_ref[k_at, 0, 2 * pair + 1] <= bound)

    @pl.when(small)
    def direct():
        sums = []
        for head in range(2):
            queries, keys, values = operands(head)
            if not causal:
                weight = jnp.exp2(contract(keys, queries, 1, 1)).astype(bf16)
                weight_ref[head] = weight
                sums.append(contract(values, weight, 0, 0))
                continue
            step = tokens // 2
            before = lax.broadcasted_iota(jnp.int32, (step, step), 0) <= lax.broadcasted_iota(
                jnp.int32, (step, step), 1
            )
            nothing = jnp.zeros((), bf16)
            top = jnp.exp2(contract(keys[:step], queries, 1, 1)).astype(bf16)
            top = jnp.concatenate(
                [jnp.where(before, top[:, :step], nothing), top[:, step:]], axis=1
            )
            weight_ref[head, :step] = top
            total = contract(values[:step], top, 0, 0)
            low_part = jnp.exp2(contract(keys[step:], queries[step:], 1, 1)).astype(bf16)
            low_part = jnp.where(before, low_part, nothing)
            weight_ref[head, step:, step:] = low_part
            rest = contract(values[step:], low_part, 0, 0)
            sums.append(jnp.concatenate([total[:, :step], total[:, step:] + rest], axis=1))
        finish(sums)

    @pl.when(jnp.logical_not(small))
    def shifted():
        sums = []
        for head in range(2):
            queries, keys, values = operands(head)
            scores = contract(keys, queries, 1, 1)
            if causal:
                before = lax.broadcasted_iota(
                    jnp.int32, scores.shape, 0
                ) <= lax.broadcasted_iota(jnp.int32, scores.shape, 1)
                scores = jnp.where(before, scores, forbidden)
            scores = scores - jnp.max(scores, axis=0, keepdims=True)
            weight = jnp.exp2(scores).astype(bf16)
            weight_ref[head] = weight
            sums.append(contract(values, weight, 0, 0))
        finish(sums)


def attend(bucket, lengths, q_pack, k_pack, v_pack, causal, start, stop, so_far=(), sooner=()):
    (q, q_squares, q_at), (k, k_squares, k_at), (v, unused, v_at) = q_pack, k_pack, v_pack
    tokens, width = q.shape[1:]
    pairs = width // PAIR
    pair_spec = lambda at: pl.BlockSpec((1, tokens, PAIR), lambda j: (at, 0, start + j))
    flat_spec = pl.BlockSpec((tokens, PAIR), lambda j: (0, start + j))
    return pl.pallas_call(
        functools.partial(attend_kernel, causal, q_at, k_at, start),
        grid=(stop - start,),
        in_specs=[smem(), smem(), smem(), smem(), pair_spec(q_at), pair_spec(k_at), pair_spec(v_at)]
        + [in_place() for array in (*so_far, *sooner)],
        out_specs=[
            flat_spec,
            pl.BlockSpec((2, tokens, tokens), lambda j: (start + j, 0, 0)),
            pl.BlockSpec((1, 2, tokens), lambda j: (start + j, 0, 0)),
            pl.BlockSpec((8, PAIR), lambda j: (0, 0)),
        ],
        out_shape=[
            jax.ShapeDtypeStruct((tokens, width), bf16),
            jax.ShapeDtypeStruct((2 * pairs, tokens, tokens), bf16),
            jax.ShapeDtypeStruct((pairs, 2, tokens), f32),
            jax.ShapeDtypeStruct((8, PAIR), f32),
        ],
        input_output_aliases={7 + i: i for i in range(len(so_far))},
        scratch_shapes=[pltpu.VMEM((tokens, PAIR), bf16), pltpu.VMEM((tokens, PAIR), bf16)],
        compiler_params=params,
        cost_estimate=cost(0.05 * (stop - start)),
        name="attend",
    )(bucket, lengths, q_squares, k_squares, q, k, v, *so_far, *sooner)


def attend_back_kernel(
    causal, q_ref, k_ref, v_ref, grad_ref, out_ref, weight_ref, dq_ref, dk_ref, dv_ref
):
    tokens = q_ref.shape[-2]
    low = low_half(tokens)
    q, k, v, grad = q_ref[0], k_ref[0], v_ref[0], grad_ref[...]
    nothing = jnp.zeros((tokens, PAIR), bf16)
    minus = jnp.full((tokens, PAIR), -1.0, bf16)
    swap = (
        (lax.broadcasted_iota(jnp.int32, (PAIR, PAIR), 0) < HEAD_DIM)
        != (lax.broadcasted_iota(jnp.int32, (PAIR, PAIR), 1) < HEAD_DIM)
    ).astype(bf16)
    product = grad.astype(f32) * out_ref[...].astype(f32)
    high = product.astype(bf16)
    centre = contract(high, swap, 1, 0) + contract((product - high.astype(f32)).astype(bf16), swap, 1, 0)
    high = centre.astype(bf16)
    rest = (centre - high.astype(f32)).astype(bf16)
    lane = lax.broadcasted_iota(jnp.int32, (tokens, PAIR), 1) & (HEAD_DIM - 1)
    centre = jnp.where(lane == 0, high, jnp.where(lane == 1, rest, nothing))

    step = tokens // 2 if causal else tokens
    dq_turned = None
    for tile in range(tokens // step):
        at = tile * step
        rows = slice(at, at + step)
        dk = dv = None
        turned = []
        for head in range(2):
            own = choose(head, low)
            weight = weight_ref[head, rows, at:]
            dweight = contract(own(v, minus)[rows], own(grad, centre)[at:], 1, 1)
            dscore = weight * dweight.astype(bf16)
            dv_own = contract(weight, own(grad, nothing)[at:], 1, 0)
            dk_own = contract(dscore, own(q, nothing)[at:], 1, 0)
            dv = dv_own if head == 0 else dv + dv_own
            dk = dk_own if head == 0 else dk + dk_own
            turned.append(contract(k[rows], dscore, 0, 0)[head * HEAD_DIM : (head + 1) * HEAD_DIM])
        dv_ref[rows] = dv.astype(bf16)
        dk_ref[rows] = (dk * math.log(2.0)).astype(bf16)
        turned = jnp.concatenate(turned, axis=0)
        if tile == 0:
            dq_turned = turned
        else:
            dq_turned = jnp.concatenate([dq_turned[:, :at], dq_turned[:, at:] + turned], axis=1)
    dq_ref[...] = (dq_turned * HEAD_DIM ** (-0.5)).T.astype(bf16)


def attend_back(q_pack, k_pack, v_pack, grad, out, weight, causal):
    (q, unused, q_at), (k, unused, k_at), (v, unused, v_at) = q_pack, k_pack, v_pack
    tokens, width = q.shape[1:]
    pairs = width // PAIR
    pair_spec = lambda at: pl.BlockSpec((1, tokens, PAIR), lambda j: (at, 0, j))
    flat_spec = pl.BlockSpec((tokens, PAIR), lambda j: (0, j))
    return pl.pallas_call(
        functools.partial(attend_back_kernel, causal),
        grid=(pairs,),
        in_specs=[
            pair_spec(q_at),
            pair_spec(k_at),
            pair_spec(v_at),
            flat_spec,
            flat_spec,
            pl.BlockSpec((2, tokens, tokens), lambda j: (j, 0, 0)),
        ],
        out_specs=[flat_spec] * 3,
        out_shape=[jax.ShapeDtypeStruct((tokens, width), bf16)] * 3,
        compiler_params=params,
        cost_estimate=cost(0.2),
        name="attend_back",
    )(q, k, v, grad, out, weight)


def first_kernel(wanted, count, table_ref, x_ref, out_ref, gains_ref, *refs):
    pieces = refs[:count]
    first_ref, inverse_ref, q_ref, square_ref, store, sems = refs[-6:]
    step = pl.program_id(0)

    @pl.when(step == 0)
    def load():
        start_loading(pieces, table_ref, wanted, store, sems)

    loaded_once(store, sems, 0)
    z = x_ref[...].astype(f32) + contract(out_ref[...], store[0], 1, 0)
    normal, inverse = normalise(z)
    first = normal * gains_ref[0:1]
    first_ref[...] = first
    inverse_ref[...] = jnp.broadcast_to(inverse, inverse_ref.shape)
    loaded_once(store, sems, 1)
    q = (contract(first.astype(bf16), store[1], 1, 0) * query_scale).astype(bf16)
    q_ref[0] = q
    squares = jnp.broadcast_to(head_squares(q), square_ref.shape[1:])

    @pl.when(step == 0)
    def begin():
        square_ref[0] = squares

    @pl.when(step > 0)
    def more():
        square_ref[0] = jnp.maximum(square_ref[0], squares)


def after_self(x, out, gains, table, pieces, wanted, sooner):
    tokens, width = x.shape
    rows = tokens // 4
    tile = pl.BlockSpec((rows, width), lambda i: (i, 0))
    return pl.pallas_call(
        functools.partial(first_kernel, wanted, len(pieces)),
        grid=(tokens // rows,),
        in_specs=[smem(), tile, tile, pl.BlockSpec(gains.shape, lambda i: (0, 0))]
        + [in_place() for piece in (*pieces, *sooner)],
        out_specs=[
            tile,
            pl.BlockSpec((rows, PAIR), lambda i: (i, 0)),
            pl.BlockSpec((1, rows, width), lambda i: (0, i, 0)),
            pl.BlockSpec((1, 8, PAIR), lambda i: (0, 0, 0)),
        ],
        out_shape=[
            jax.ShapeDtypeStruct((tokens, width), f32),
            jax.ShapeDtypeStruct((tokens, PAIR), f32),
            jax.ShapeDtypeStruct((1, tokens, width), bf16),
            jax.ShapeDtypeStruct((1, 8, PAIR), f32),
        ],
        scratch_shapes=stores(len(wanted), width),
        compiler_params=params,
        cost_estimate=cost(0.2),
        name="after_self",
    )(table, x, out, gains, *pieces, *sooner)


def load_feed(feed_pieces, table_ref, kinds, feed_store, feed_sems):
    blocks = feed_store.shape[2]
    for kind in kinds:
        for p, piece in enumerate(feed_pieces):
            rows_at = pl.ds(pl.multiple_of(table_ref[2, p], 16), piece.shape[1])
            pltpu.make_async_copy(
                piece.at[pl.ds(kind * blocks, blocks)],
                feed_store.at[kind, table_ref[1, p], :, rows_at],
                feed_sems.at[kind],
            ).start()


def first_block(feed_store, i):
    return feed_store[0, :, i].reshape(-1, feed_store.shape[-1])


def second_block(feed_store, i):
    devices, blocks = feed_store.shape[1:3]
    return feed_store[1, i * devices // blocks : (i + 1) * devices // blocks].reshape(
        -1, feed_store.shape[-1]
    )


def feed_kernel(
    wanted, count, bucket_ref, lengths_ref, table_ref, first_ref, out_ref, cotangent_ref, gains_ref, down_ref,
    up_ref, *refs,
):
    pieces, feed_pieces = refs[: 3 * count], refs[3 * count : 4 * count]
    (outputs_ref, third_ref, slope_ref, normal_ref, inverse_ref, adapter_ref, down_grad_ref, up_grad_ref,
     down_low, up_low, store, sems, feed_store, feed_sems) = refs[4 * count :]
    rows, width = first_ref.shape
    tokens = rows * pl.num_programs(0)
    step = pl.program_id(0)

    @pl.when(step == 0)
    def begin():
        start_loading(pieces, table_ref, wanted, store, sems)
        load_feed(feed_pieces, table_ref, (0, 1), feed_store, feed_sems)
        down_low[...] = down_ref[...].astype(bf16)
        up_low[...] = up_ref[...].astype(bf16)
        down_grad_ref[...] = jnp.zeros_like(down_grad_ref)
        up_grad_ref[...] = jnp.zeros_like(up_grad_ref)

    loaded_once(store, sems, 0)
    z = first_ref[...] + contract(out_ref[...], store[0], 1, 0)
    second_normal, second_inverse = normalise(z)
    normal_ref[...] = second_normal.astype(bf16)
    inverse_ref[...] = jnp.broadcast_to(second_inverse, inverse_ref.shape)
    second = second_normal * gains_ref[1:2]
    second_low = second.astype(bf16)

    adapter_act, adapter_slope = gelu_and_slope(contract(second_low, down_low[...], 1, 0))
    adapter_act = adapter_act.astype(bf16)
    total = second + 4.0 * contract(adapter_act, up_low[...], 1, 0)
    loaded_once(feed_store, feed_sems, 0)
    loaded_once(feed_store, feed_sems, 1)
    for i in range(feed_store.shape[2]):
        active, slope = gelu_and_slope(contract(second_low, first_block(feed_store, i), 1, 0))
        slope_ref[i] = slope.astype(bf16)
        total += contract(active.astype(bf16), second_block(feed_store, i), 1, 0)

    third_normal, third_inverse = normalise(total)
    outputs_ref[...] = (third_normal * gains_ref[2:3]).astype(bf16)

    shift = item_shift(bucket_ref[0], tokens)
    row = lax.broadcasted_iota(jnp.int32, (rows, 1), 0) + step * rows
    item = row >> shift
    valid = row - (item << shift) < item_length(item, lengths_ref)
    upstream = jnp.where(valid, cotangent_ref[...].astype(f32), 0.0)
    grad_third = normalise_back(upstream * gains_ref[2:3], third_normal, third_inverse)
    third_ref[...] = grad_third

    grad_adapter_out = (4.0 * grad_third).astype(bf16)
    up_grad_ref[...] += contract(adapter_act, grad_adapter_out, 0, 0)
    grad_adapter_pre = (contract(grad_adapter_out, up_low[...], 1, 1) * adapter_slope).astype(bf16)
    adapter_ref[...] = grad_adapter_pre
    down_grad_ref[...] += contract(second_low, grad_adapter_pre, 0, 0)


def feed(bucket, lengths, table, first, out, cotangent, gains, down, up, pieces, output_at, feed_pieces):
    tokens, width = first.shape
    rows = tokens // 4
    chunks, shard_rows = feed_pieces[0].shape[0] // 2, feed_pieces[0].shape[1]
    tile = pl.BlockSpec((rows, width), lambda i: (i, 0))
    fixed = lambda a: pl.BlockSpec(a.shape, lambda i: (0,) * a.ndim, pipeline_mode=pl.Buffered(1))
    return pl.pallas_call(
        functools.partial(feed_kernel, (output_at,), len(feed_pieces)),
        grid=(tokens // rows,),
        in_specs=[smem(), smem(), smem(), tile, tile, tile, fixed(gains), fixed(down), fixed(up)]
        + [in_place() for piece in pieces + feed_pieces],
        out_specs=[
            tile,
            tile,
            pl.BlockSpec((chunks, rows, width), lambda i: (0, i, 0)),
            tile,
            pl.BlockSpec((rows, PAIR), lambda i: (i, 0)),
            pl.BlockSpec((rows, down.shape[1]), lambda i: (i, 0)),
            fixed(down),
            fixed(up),
        ],
        out_shape=[
            jax.ShapeDtypeStruct((tokens, width), bf16),
            jax.ShapeDtypeStruct((tokens, width), f32),
            jax.ShapeDtypeStruct((chunks, tokens, width), bf16),
            jax.ShapeDtypeStruct((tokens, width), bf16),
            jax.ShapeDtypeStruct((tokens, PAIR), f32),
            jax.ShapeDtypeStruct((tokens, down.shape[1]), bf16),
            jax.ShapeDtypeStruct(down.shape, f32),
            jax.ShapeDtypeStruct(up.shape, f32),
        ],
        scratch_shapes=[
            pltpu.VMEM(down.shape, bf16),
            pltpu.VMEM(up.shape, bf16),
            *stores(1, width),
            pltpu.VMEM((2, width // shard_rows, chunks, shard_rows, width), bf16),
            pltpu.SemaphoreType.DMA((2,)),
        ],
        compiler_params=params,
        cost_estimate=cost(0.2),
        name="feed",
    )(bucket, lengths, table, first, out, cotangent, gains, down, up, *pieces, *feed_pieces)


def feed_back_kernel(
    wanted, count, table_ref, third_ref, slope_ref, normal_ref, inverse_ref, adapter_ref, share_ref, gains_ref,
    down_ref, *refs,
):
    pieces, feed_pieces = refs[: 3 * count], refs[3 * count : 4 * count]
    grad_ref, grad_out_ref, down_low, store, sems, feed_store, feed_sems = refs[4 * count :]

    @pl.when(pl.program_id(0) == 0)
    def begin():
        load_feed(feed_pieces, table_ref, (1, 0), feed_store, feed_sems)
        start_loading(pieces, table_ref, wanted, store, sems)
        down_low[...] = down_ref[...].astype(bf16)

    grad_third = third_ref[...]
    grad_feed = grad_third.astype(bf16)
    grad_second = grad_third + contract(adapter_ref[...], down_low[...], 1, 1)
    loaded_once(feed_store, feed_sems, 1)
    loaded_once(feed_store, feed_sems, 0)
    for i in range(feed_store.shape[2]):
        grad_inner = contract(grad_feed, second_block(feed_store, i), 1, 1)
        grad_inner = (grad_inner * slope_ref[i].astype(f32)).astype(bf16)
        grad_second += contract(grad_inner, first_block(feed_store, i), 1, 1)

    grad_pre = normalise_back(
        grad_second * gains_ref[1:2], normal_ref[...].astype(f32), inverse_ref[:, 0:1]
    )
    grad_ref[...] = grad_pre
    loaded_once(store, sems, 0)
    grad_out_ref[...] = (
        contract(grad_pre.astype(bf16), store[0], 1, 1) * spread(share_ref, grad_pre.shape[1])
    ).astype(bf16)


def feed_back(table, third, slope, normal, inverse, adapter, share, gains, down, pieces, output_at, feed_pieces):
    tokens, width = third.shape
    rows = tokens // 4
    chunks, shard_rows = feed_pieces[0].shape[0] // 2, feed_pieces[0].shape[1]
    tile = pl.BlockSpec((rows, width), lambda i: (i, 0))
    fixed = lambda a: pl.BlockSpec(a.shape, lambda i: (0,) * a.ndim, pipeline_mode=pl.Buffered(1))
    return pl.pallas_call(
        functools.partial(feed_back_kernel, (output_at,), len(feed_pieces)),
        grid=(tokens // rows,),
        in_specs=[
            smem(),
            tile,
            pl.BlockSpec((chunks, rows, width), lambda i: (0, i, 0)),
            tile,
            pl.BlockSpec((rows, PAIR), lambda i: (i, 0)),
            pl.BlockSpec((rows, down.shape[1]), lambda i: (i, 0)),
            share_spec(share, rows),
            fixed(gains),
            fixed(down),
        ]
        + [in_place() for piece in pieces + feed_pieces],
        out_specs=[tile, tile],
        out_shape=[
            jax.ShapeDtypeStruct((tokens, width), f32),
            jax.ShapeDtypeStruct((tokens, width), bf16),
        ],
        scratch_shapes=[
            pltpu.VMEM(down.shape, bf16),
            *stores(1, width),
            pltpu.VMEM((2, width // shard_rows, chunks, shard_rows, width), bf16),
            pltpu.SemaphoreType.DMA((2,)),
        ],
        compiler_params=params,
        cost_estimate=cost(0.2),
        name="feed_back",
    )(table, third, slope, normal, inverse, adapter, share, gains, down, *pieces, *feed_pieces)


def cross_back_kernel(
    wanted, table_ref, dq_ref, dk_ref, dv_ref, grad_ref, first_ref, inverse_ref, share_ref, gains_ref,
    *refs,
):
    *pieces, encoder_ref, pre_ref, grad_out_ref, store, sems = refs

    @pl.when(pl.program_id(0) == 0)
    def load():
        start_loading(pieces, table_ref, wanted, store, sems)

    loaded_once(store, sems, 0)
    grad_first = grad_ref[...] + contract(dq_ref[...], store[0], 1, 1)
    loaded_once(store, sems, 1)
    encoder = contract(dk_ref[...], store[1], 1, 1)
    loaded_once(store, sems, 2)
    encoder_ref[...] = (encoder + contract(dv_ref[...], store[2], 1, 1)).astype(bf16)
    gain = gains_ref[0:1]
    grad_pre = normalise_back(grad_first * gain, first_ref[...] / gain, inverse_ref[:, 0:1])
    pre_ref[...] = grad_pre
    loaded_once(store, sems, 3)
    grad_out_ref[...] = (
        contract(grad_pre.astype(bf16), store[3], 1, 1) * spread(share_ref, grad_pre.shape[1])
    ).astype(bf16)


def after_cross_back(dq, dk, dv, grad, first, inverse, share, gains, table, pieces, wanted):
    tokens, width = first.shape
    rows = tokens // 4
    tile = pl.BlockSpec((rows, width), lambda i: (i, 0))
    return pl.pallas_call(
        functools.partial(cross_back_kernel, wanted),
        grid=(tokens // rows,),
        in_specs=[smem()]
        + [tile] * 5
        + [pl.BlockSpec((rows, PAIR), lambda i: (i, 0)), share_spec(share, rows), pl.BlockSpec(gains.shape, lambda i: (0, 0))]
        + [in_place() for piece in pieces],
        out_specs=[tile] * 3,
        out_shape=[
            jax.ShapeDtypeStruct((tokens, width), bf16),
            jax.ShapeDtypeStruct((tokens, width), f32),
            jax.ShapeDtypeStruct((tokens, width), bf16),
        ],
        scratch_shapes=stores(len(wanted), width),
        compiler_params=params,
        cost_estimate=cost(0.2),
        name="after_cross_back",
    )(table, dq, dk, dv, grad, first, inverse, share, gains, *pieces)


def input_kernel(wanted, table_ref, dq_ref, dk_ref, dv_ref, pre_ref, *refs):
    *pieces, out_ref, store, sems = refs

    @pl.when(pl.program_id(0) == 0)
    def load():
        start_loading(pieces, table_ref, wanted, store, sems)

    total = pre_ref[...]
    for slot, ref in enumerate((dq_ref, dk_ref, dv_ref)):
        loaded_once(store, sems, slot)
        total += contract(ref[...], store[slot], 1, 1)
    out_ref[...] = total.astype(bf16)


def input_gradient(dq, dk, dv, pre, table, pieces, wanted):
    tokens, width = pre.shape
    rows = tokens // 4
    tile = pl.BlockSpec((rows, width), lambda i: (i, 0))
    return pl.pallas_call(
        functools.partial(input_kernel, wanted),
        grid=(tokens // rows,),
        in_specs=[smem()] + [tile] * 4 + [in_place() for piece in pieces],
        out_specs=tile,
        out_shape=jax.ShapeDtypeStruct((tokens, width), bf16),
        scratch_shapes=stores(len(wanted), width),
        compiler_params=params,
        cost_estimate=cost(0.2),
        name="input_gradient",
    )(table, dq, dk, dv, pre, *pieces)


def adamw(master, first_moment, second_moment, gradient):
    first_new = beta_first * first_moment + (1.0 - beta_first) * gradient
    second_new = beta_second * second_moment + (1.0 - beta_second) * gradient * gradient
    first_hat = first_new / (1.0 - beta_first**STEP)
    second_hat = second_new / (1.0 - beta_second**STEP)
    master_new = master - learn_rate * (
        first_hat / (jnp.sqrt(second_hat) + epsilon_adam) + weight_decay * master
    )
    return (first_new, second_new, master_new)


def pack_kernel(*refs):
    *shards, out_ref = refs
    for i, shard in enumerate(shards):
        out_ref[i] = shard[...]


def pack(shards):
    return pl.pallas_call(
        pack_kernel,
        out_shape=jax.ShapeDtypeStruct((len(shards),) + shards[0].shape, bf16),
        compiler_params=params,
        cost_estimate=cost(2),
        name="pack",
    )(*shards)


def pack_pair_kernel(table_ref, *refs):
    *shards, own_ref, other_ref = refs
    half = len(shards) // 2

    def both(first_ref, second_ref):
        for i in range(half):
            first_ref[i] = shards[i][...]
            second_ref[i] = shards[half + i][...]

    pl.when(table_ref[3, 0] == 0)(functools.partial(both, own_ref, other_ref))
    pl.when(table_ref[3, 0] != 0)(functools.partial(both, other_ref, own_ref))


def pack_pair(table, shards):
    shape = jax.ShapeDtypeStruct((len(shards) // 2,) + shards[0].shape, bf16)
    vmem = pl.BlockSpec(memory_space=pltpu.VMEM)
    return pl.pallas_call(
        pack_pair_kernel,
        in_specs=[smem()] + [vmem] * len(shards),
        out_specs=[vmem, vmem],
        out_shape=[shape, shape],
        compiler_params=params,
        cost_estimate=cost(2),
        name="pack_pair",
    )(table, *shards)


def pack_feed_kernel(first_ref, second_ref, out_ref):
    blocks, rows, width = out_ref.shape
    blocks //= 2
    for i in range(blocks):
        out_ref[i] = first_ref[:, i * width : (i + 1) * width]
        out_ref[blocks + i] = second_ref[i * rows : (i + 1) * rows]


def pack_feed(first, second):
    rows, width = first.shape[0], second.shape[1]
    blocks = (first.size + second.size) // (rows * width)
    return pl.pallas_call(
        pack_feed_kernel,
        out_shape=jax.ShapeDtypeStruct((blocks, rows, width), bf16),
        compiler_params=params,
        cost_estimate=cost(3),
        name="pack_feed",
    )(first, second)


def after_kernel(*refs):
    done_ref = refs[-1]
    done_ref[0] = 0


def after(values, *sooner):
    if not sooner:
        return values
    return pl.pallas_call(
        after_kernel,
        in_specs=[in_place()] * (1 + len(sooner)),
        out_specs=[in_place(), smem()],
        out_shape=[jax.ShapeDtypeStruct(values.shape, values.dtype), jax.ShapeDtypeStruct((1,), jnp.int32)],
        input_output_aliases={0: 0},
        compiler_params=params,
        cost_estimate=cost(0.01),
        name="after",
    )(values, *sooner)[0]


AXES = ("fsdp", "dp")


def ring_order(size):
    return list(range(0, size, 2)) + list(range(size - 1, 0, -2))


class Links:
    def __init__(self, shard_rows):
        self.size, self.parts = lax.axis_size("fsdp"), lax.axis_size("dp")
        order = ring_order(self.size)
        after = {order[i]: order[(i + 1) % self.size] for i in range(self.size)}
        before = {later: sooner for sooner, later in after.items()}
        every = [(f, d) for f in range(self.size) for d in range(self.parts)]
        flat = lambda f, d: f * self.parts + d
        self.onward = [(flat(f, d), flat((before if d % 2 else after)[f], d)) for f, d in every]
        self.sibling = [(flat(f, d), flat(f, d ^ 1)) for f, d in every]
        self.across = [(flat(f, d), flat(f, d ^ 2)) for f, d in every]
        self.core = lax.axis_index("dp") % 2
        self.hops = self.size // 2

        rows, table = shard_rows, []
        for f, d in every:
            place, core, plane = order.index(f), d % 2, d // 2 % 2
            toward = 1 - 2 * core
            shards, inside = [f], [0]
            for hop in range(1, self.hops + 1):
                for sign in (-1, 1):
                    shards.append(order[(place + sign * toward * hop) % self.size])
                    late = core if sign == -1 else 1 - core
                    inside.append(late * (rows // 2) if hop == self.hops else 0)
            first = [shard * rows + at for shard, at in zip(shards, inside)]
            table.append([first, shards, inside, [plane] * len(first)])
        self.table = lax.dynamic_index_in_dim(
            jnp.array(table, jnp.int32), lax.axis_index(AXES), 0, keepdims=False
        )

    def send(self, values, pairs):
        return lax.ppermute(values, AXES, pairs)

    def last(self, values):
        half = values.shape[1] // 2
        return lax.dynamic_slice_in_dim(values, self.core * half, half, 1)


class Gather:
    def __init__(self, links, own, other=None):
        self.links, self.moving, self.count, self.quarter, self.pieces = links, own, 0, 0, []
        self.rest = [] if other is None else [other]

    def share(self, *sooner):
        self.moving = after(self.moving, *sooner)
        self.shared = self.moving
        self.pieces.append(self.moving)
        if self.count:
            self.pieces.append(self.links.send(self.moving, self.links.sibling))
            if self.rest:
                self.crossed = self.links.send(self.moving, self.links.across)
                if self.count < self.links.hops:
                    self.hand_over()

    def hand_over(self, *sooner):
        crossed = after(self.crossed, *sooner)
        self.rest += [crossed, self.links.send(crossed, self.links.sibling)]

    def hop(self, *sooner, chained=False):
        links = self.links
        self.quarter += 1
        while self.count < self.quarter * links.hops // 4:
            if chained and len(self.pieces) > 1:
                sooner = (*sooner, self.pieces[-1], *self.rest[2:][-1:])
            self.share(*sooner)
            sooner = ()
            self.count += 1
            moving = links.last(self.moving) if self.count == links.hops else self.moving
            self.moving = links.send(moving, links.onward)


def body(
    inputs, encoder, cotangent, buckets, lengths, self_query, self_key, self_value, self_output,
    cross_query, cross_key, cross_value, cross_output, fc_first, fc_second, norm_gains,
    down_master, up_master, down_first, down_second, up_first, up_second,
):
    rows, width = self_query.shape
    links = Links(rows)
    table = links.table
    sq, sk, sv, so = ((None, i) for i in range(4))
    ck, cv, cq, co = (0, 0), (0, 1), (1, 0), (1, 1)
    one = Gather(links, pack((self_query, self_key, self_value, self_output)))
    two = Gather(links, *pack_pair(table, (cross_key, cross_value, cross_query, cross_output)))
    two_own = two.moving
    one.hop(chained=True)
    two.hop(chained=True)
    one.hop(two_own, chained=True)
    two.hop(chained=True)
    for quarter in range(2):
        one.hop(chained=True)
        two.hop(chained=True)
    one.share()
    two.share()
    late = Gather(links, pack_feed(fc_first, fc_second))
    late.hop(one.moving, two.moving)

    qkv, squares = project(inputs, table, one.pieces * 3, (sq, sk, sv), query_scale, 2, (late.shared,))
    two.hand_over(squares)
    pieces = one.pieces + two.pieces + two.rest
    kv, kv_squares = project(encoder, table, two.pieces + two.pieces + two.rest, (ck, cv), 1.0, 1, (squares,))
    self_packs = [(qkv, squares, 0), (qkv, squares, 1), (qkv, None, 2)]
    half = width // PAIR // 2
    late.hop(squares, kv_squares)
    *self_half, done = attend(buckets, lengths, *self_packs, True, 0, half, (), (late.shared,))
    self_out, self_weight, self_share, done = attend(
        buckets, lengths, *self_packs, True, half, 2 * half, self_half
    )
    late.hop(done)
    first, first_inverse, query_cross, query_squares = after_self(
        inputs, self_out, norm_gains, table, pieces, (so, cq), (late.shared,)
    )
    cross_packs = [(query_cross, query_squares, 0), (kv, kv_squares, 0), (kv, None, 1)]
    *cross_half, done = attend(buckets, lengths, *cross_packs, False, 0, half)
    late.hop(done)
    cross_out, cross_weight, cross_share, done = attend(
        buckets, lengths, *cross_packs, False, half, 2 * half, cross_half, (late.shared,)
    )
    late.share(done)

    outputs, grad_third, slope, second_normal, second_inverse, adapter, down_local, up_local = feed(
        buckets, lengths, table, first, cross_out, cotangent, norm_gains, down_master, up_master, pieces, co,
        late.pieces,
    )
    down_grad, up_grad = lax.psum((down_local, up_local), ("fsdp", "dp"))

    grad_cross_pre, grad_cross_out = feed_back(
        table, grad_third, slope, second_normal, second_inverse, adapter, cross_share, norm_gains, down_master,
        pieces, co, late.pieces,
    )
    dq, dk, dv = attend_back(*cross_packs, grad_cross_out, cross_out, cross_weight, False)
    encoder_grad, grad_self_pre, grad_self_out = after_cross_back(
        dq, dk, dv, grad_cross_pre, first, first_inverse, self_share, norm_gains, table, pieces, (cq, ck, cv, so)
    )
    dq, dk, dv = attend_back(*self_packs, grad_self_out, self_out, self_weight, True)
    input_grad = input_gradient(dq, dk, dv, grad_self_pre, table, pieces, (sq, sk, sv))

    down_first_new, down_second_new, down_master_new = adamw(
        down_master, down_first, down_second, down_grad
    )
    up_first_new, up_second_new, up_master_new = adamw(up_master, up_first, up_second, up_grad)
    return (
        outputs,
        input_grad,
        encoder_grad,
        down_grad,
        up_grad,
        down_first_new,
        down_second_new,
        up_first_new,
        up_second_new,
        down_master_new,
        up_master_new,
        down_master_new.astype(bf16),
        up_master_new.astype(bf16),
    )


def solution(mesh):
    tokens, matrix = P(("fsdp", "dp"), None), P("fsdp", None)
    return jax.shard_map(
        body,
        mesh=mesh,
        in_specs=(tokens, tokens, tokens, P(("fsdp", "dp")), tokens) + (matrix,) * 10 + (P(),) * 7,
        out_specs=(tokens,) * 3 + (P(),) * 10,
        check_vma=False,
    )
```

profile of v0, /device:TPU:0, one launch (start us, length us, event | category | flops | bytes accessed | tf_op | source)
XLA Modules:
  0.0 404.4 jit_solution(4348157863855608290)
XLA Ops:
  7.2 2.2 pack.1.refs_0_.refs_9_.refs_18_
  9.5 3.0 collective-permute-start
  13.7 2.3 pack_pair.1
  17.6 7.9 %collective-permute-done.refs_0_ = bf16[4,128,1024]{2,1,0:T(8,128)(2,1)} collective-permute-done((bf16[4,128,1024]{2,1,0:T(8,128)(2,1)}, bf16[4,128,1024]{2,1,0:T(8,128)(2,1)}, u32[]{:S(2)}, u32[]{:S(2)}) %collective-permute-start) | collective-permute-done | bytes 1048608 | tf_op jit(solution)/shard_map/ppermute | solution.py:853
  26.1 2.2 collective-permute-start.2
  28.2 2.9 collective-permute-done.8.refs_1_.refs_10_
  31.1 2.1 collective-permute-start.11
  34.7 9.9 %collective-permute-done.11.refs_19_ = bf16[2,128,1024]{2,1,0:T(8,128)(2,1)} collective-permute-done((bf16[2,128,1024]{2,1,0:T(8,128)(2,1)}, bf16[2,128,1024]{2,1,0:T(8,128)(2,1)}, u32[]{:S(2)}, u32[]{:S(2)}) %collective-permute-start.11) | collective-permute-done | bytes 524320 | tf_op jit(solution)/shard_map/ppermute | solution.py:853
  49.3 2.1 collective-permute-start.15
  53.0 9.9 %collective-permute-done.15.refs_21_ = bf16[2,128,1024]{2,1,0:T(8,128)(2,1)} collective-permute-done((bf16[2,128,1024]{2,1,0:T(8,128)(2,1)}, bf16[2,128,1024]{2,1,0:T(8,128)(2,1)}, u32[]{:S(2)}, u32[]{:S(2)}) %collective-permute-start.15) | collective-permute-done | bytes 524320 | tf_op jit(solution)/shard_map/ppermute | solution.py:853
  63.4 1.9 constant_dynamic-slice_fusion.2
  70.1 4.7 %collective-permute-done.6.refs_1_.refs_7_.refs_16_.refs_25_ = bf16[4,64,1024]{2,1,0:T(8,128)(2,1)} collective-permute-done((bf16[4,64,1024]{2,1,0:T(8,128)(2,1)}, bf16[4,64,1024]{2,1,0:T(8,128)(2,1)}, u32[]{:S(2)}, u32[]{:S(2)}) %collective-permute-start.6) | collective-permute-done | bytes 524320 | tf_op jit(solution)/shard_map/ppermute | solution.py:853
  77.6 3.0 pack_feed.1.refs_0_
  86.4 13.0 %project.2 = (bf16[3,1024,1024]{2,1,0:T(8,128)(2,1)}, f32[3,8,128]{2,1,0:T(8,128)}) custom-call(bf16[1024,1024]{1,0:T(8,128)(2,1)} %x_ref.5, s32[4,9]{1,0:T(4,128)} %dynamic-slice_bitcast_fusion.table_ref, bf16[4,128,1024]{2,1,0:T(8,128)(2,1)} %pack.1.refs_0_.refs_9_.refs_18_, bf16[4,128,1024]{2,1,0:T(8,128)(2,1)} %get-tuple-element.69.refs_1_.refs_10_.refs_19_, ...), custom_call_target="tpu_custom_call" | custom-call | flops 13799999488 | bytes 100000 | tf_op jit(solution)/shard_map/project/pallas_call | solution.py:158
  103.2 9.9 %project.3 = (bf16[2,1024,1024]{2,1,0:T(8,128)(2,1)}, f32[2,8,128]{2,1,0:T(8,128)}) custom-call(bf16[1024,1024]{1,0:T(8,128)(2,1)} %x_ref.4, s32[4,9]{1,0:T(4,128)} %dynamic-slice_bitcast_fusion.table_ref, bf16[2,128,1024]{2,1,0:T(8,128)(2,1)} %get-tuple-element.68.refs_1_.refs_0_.refs_9_, bf16[2,128,1024]{2,1,0:T(8,128)(2,1)} %collective-permute-done.8.refs_1_.refs_10_, ...), custom_call_target="tpu_custom_call" | custom-call | flops 9200000000 | bytes 100000 | tf_op jit(solution)/shard_map/project/pallas_call | solution.py:158
  116.2 15.4 %attend.4 = (bf16[1024,1024]{1,0:T(8,128)(2,1)}, bf16[16,1024,1024]{2,1,0:T(8,128)(2,1)}, f32[8,2,1024]{2,1,0:T(2,128)}, f32[8,128]{1,0:T(8,128)}) custom-call(s32[1]{0:T(128)S(6)} %copy.72.bucket_ref, s32[1,4]{1,0:T(1,128)} %lengths_ref.9, f32[3,8,128]{2,1,0:T(8,128)} %get-tuple-element.75.refs_1_.refs_27_.qsq_ref.ksq_ref, ...), custom_call_target="tpu_custom_call" | custom-call | flops 230000000 | bytes 100000 | tf_op jit(solution)/shard_map/attend/pallas_call | solution.py:293
  131.6 15.4 %attend.5 = (bf16[1024,1024]{1,0:T(8,128)(2,1)}, bf16[16,1024,1024]{2,1,0:T(8,128)(2,1)}, f32[8,2,1024]{2,1,0:T(2,128)}, f32[8,128]{1,0:T(8,128)}) custom-call(s32[1]{0:T(128)S(6)} %copy.72.bucket_ref, s32[1,4]{1,0:T(1,128)} %lengths_ref.9, ...), custom_call_target="tpu_custom_call", output_to_operand_aliasing={{0}: (7, {}), {1}: (8, {}), {2}: (9, {})} | custom-call | flops 230000000 | bytes 100000 | tf_op jit(solution)/shard_map/attend/pallas_call | solution.py:293
  147.8 11.8 %after_self.1 = (f32[1024,1024]{1,0:T(8,128)}, f32[1024,128]{1,0:T(8,128)}, bf16[1,1024,1024]{2,1,0:T(8,128)(2,1)}, f32[1,8,128]{2,1,0:T(8,128)}) custom-call(s32[4,9]{1,0:T(4,128)} %dynamic-slice_bitcast_fusion.table_ref, bf16[1024,1024]{1,0:T(8,128)(2,1)} %x_ref.5, bf16[1024,1024]{1,0:T(8,128)(2,1)} %get-tuple-element.84.out_ref, f32[3,1024]{1,0:T(4,128)} %gains_ref.7, ...), custom_call_target="tpu_custom_call" | custom-call | flops 230000000 | bytes 100000 | tf_op jit(solution)/shard_map/after_self/pallas_call | solution.py:423
  159.6 12.1 %attend.6 = (bf16[1024,1024]{1,0:T(8,128)(2,1)}, bf16[16,1024,1024]{2,1,0:T(8,128)(2,1)}, f32[8,2,1024]{2,1,0:T(2,128)}, f32[8,128]{1,0:T(8,128)}) custom-call(s32[1]{0:T(128)S(6)} %copy.72.bucket_ref, s32[1,4]{1,0:T(1,128)} %lengths_ref.9, f32[1,8,128]{2,1,0:T(8,128)} %get-tuple-element.88.qsq_ref, f32[2,8,128]{2,1,0:T(8,128)} %get-tuple-element.79.refs_2_.ksq_ref, ...), custom_call_target="tpu_custom_call" | custom-call | flops 230000000 | bytes 100000 | tf_op jit(solution)/shard_map/attend/pallas_call | solution.py:293
  171.7 2.5 collective-permute-done.26.refs_0_
  174.7 2.3 constant_dynamic-slice_fusion
  178.5 12.1 %attend.7 = (bf16[1024,1024]{1,0:T(8,128)(2,1)}, bf16[16,1024,1024]{2,1,0:T(8,128)(2,1)}, f32[8,2,1024]{2,1,0:T(2,128)}, f32[8,128]{1,0:T(8,128)}) custom-call(s32[1]{0:T(128)S(6)} %copy.72.bucket_ref, s32[1,4]{1,0:T(1,128)} %lengths_ref.9, f32[1,8,128]{2,1,0:T(8,128)} %get-tuple-element.88.qsq_ref, ...), custom_call_target="tpu_custom_call", output_to_operand_aliasing={{0}: (7, {}), {1}: (8, {}), {2}: (9, {})} | custom-call | flops 230000000 | bytes 100000 | tf_op jit(solution)/shard_map/attend/pallas_call | solution.py:293
  190.6 1.9 collective-permute-done.30.refs_0_
  193.1 3.0 collective-permute-done.31.refs_35_
  196.1 45.7 %feed.1 = (bf16[1024,1024]{1,0:T(8,128)(2,1)}, f32[1024,1024]{1,0:T(8,128)}, bf16[4,1024,1024]{2,1,0:T(8,128)(2,1)}, bf16[1024,1024]{1,0:T(8,128)(2,1)}, f32[102...) custom-call(s32[1]{0:T(128)S(6)} %copy.72.bucket_ref, ...), custom_call_target="tpu_custom_call" | custom-call | flops 230000000 | bytes 100000 | tf_op jit(solution)/shard_map/feed/pallas_call | solution.py:532
  241.9 35.7 %feed_back.1 = (f32[1024,1024]{1,0:T(8,128)}, bf16[1024,1024]{1,0:T(8,128)(2,1)}) custom-call(s32[4,9]{1,0:T(4,128)} %dynamic-slice_bitcast_fusion.table_ref, f32[1024,1024]{1,0:T(8,128)} %get-tuple-element.100.third_ref, bf16[4,1024,1024]{2,1,0:T(8,128)(2,1)} %get-tuple-element.101.slope_ref, bf16[1024,1024]{1,0:T(8,128)(2,1)} %get-tuple-element.102.normal_ref, ...), custom_call_target="tpu_custom_call" | custom-call | flops 230000000 | bytes 100000 | tf_op jit(solution)/shard_map/feed_back/pallas_call | solution.py:609
  277.5 39.6 %attend_back.2 = (bf16[1024,1024]{1,0:T(8,128)(2,1)}, bf16[1024,1024]{1,0:T(8,128)(2,1)}, bf16[1024,1024]{1,0:T(8,128)(2,1)}) custom-call(bf16[1,1024,1024]{2,1,0:T(8,128)(2,1)} %get-tuple-element.89.q_ref, bf16[2,1024,1024]{2,1,0:T(8,128)(2,1)} %get-tuple-element.90.k_ref.v_ref, bf16[2,1024,1024]{2,1,0:T(8,128)(2,1)} %get-tuple-element.90.k_ref.v_ref, ...), custom_call_target="tpu_custom_call" | custom-call | flops 230000000 | bytes 100000 | tf_op jit(solution)/shard_map/attend_back/pallas_call | solution.py:371
  317.2 19.4 %after_cross_back.1 = (bf16[1024,1024]{1,0:T(8,128)(2,1)}, f32[1024,1024]{1,0:T(8,128)}, bf16[1024,1024]{1,0:T(8,128)(2,1)}) custom-call(s32[4,9]{1,0:T(4,128)} %dynamic-slice_bitcast_fusion.table_ref, bf16[1024,1024]{1,0:T(8,128)(2,1)} %get-tuple-element.108.dq_ref, bf16[1024,1024]{1,0:T(8,128)(2,1)} %get-tuple-element.109.dk_ref, ...), custom_call_target="tpu_custom_call" | custom-call | flops 230000000 | bytes 100000 | tf_op jit(solution)/shard_map/after_cross_back/pallas_call | solution.py:670
  336.6 32.7 %attend_back.3 = (bf16[1024,1024]{1,0:T(8,128)(2,1)}, bf16[1024,1024]{1,0:T(8,128)(2,1)}, bf16[1024,1024]{1,0:T(8,128)(2,1)}) custom-call(bf16[3,1024,1024]{2,1,0:T(8,128)(2,1)} %get-tuple-element.76.q_ref.k_ref.v_ref, bf16[3,1024,1024]{2,1,0:T(8,128)(2,1)} %get-tuple-element.76.q_ref.k_ref.v_ref, ...), custom_call_target="tpu_custom_call" | custom-call | flops 230000000 | bytes 100000 | tf_op jit(solution)/shard_map/attend_back/pallas_call | solution.py:371
  369.2 12.6 %input_gradient.1 = bf16[1024,1024]{1,0:T(8,128)(2,1)} custom-call(s32[4,9]{1,0:T(4,128)} %dynamic-slice_bitcast_fusion.table_ref, bf16[1024,1024]{1,0:T(8,128)(2,1)} %get-tuple-element.116.dq_ref, bf16[1024,1024]{1,0:T(8,128)(2,1)} %get-tuple-element.117.dk_ref, bf16[1024,1024]{1,0:T(8,128)(2,1)} %get-tuple-element.118.dv_ref, ...), custom_call_target="tpu_custom_call" | custom-call | flops 230000000 | bytes 100000 | tf_op jit(solution)/shard_map/input_gradient/pallas_call | solution.py:708
  382.3 7.8 %fusion.4 = (bf16[1024,512]{1,0:T(8,128)(2,1)}, f32[1024,512]{1,0:T(8,128)}, f32[1024,512]{1,0:T(8,128)}, f32[1024,512]{1,0:T(8,128)}) fusion(f32[1024,512]{1,0:T(8,128)} %down_ref.3, f32[1024,512]{1,0:T(8,128)} %get-tuple-element.136, f32[1024,512]{1,0:T(8,128)} %param.42, f32[1024,512]{1,0:T(8,128)} %param.41), kind=kLoop, calls=%fused_computation.13 | loop fusion | flops 8388608 | bytes 15728640 | tf_op jit(solution)/shard_map/convert_element_type | solution.py:974
  390.2 4.2 %fusion.2 = (bf16[512,1024]{1,0:T(8,128)(2,1)}, f32[512,1024]{1,0:T(8,128)}, f32[512,1024]{1,0:T(8,128)}, f32[512,1024]{1,0:T(8,128)}) fusion(f32[512,1024]{1,0:T(8,128)S(1)} %copy-done.4, f32[512,1024]{1,0:T(8,128)S(1)} %copy-done.5, f32[512,1024]{1,0:T(8,128)S(1)} %copy-done.8, f32[512,1024]{1,0:T(8,128)S(1)} %copy-done.9), kind=kLoop, calls=%fused_computation.12 | loop fusion | flops 8388608 | bytes 15728640 | tf_op jit(solution)/shard_map/convert_element_type | solution.py:975
  (90 shorter events, 37.9 us)
Async XLA Ops:
  7.2 375.1 %all-reduce.3.cloned.1.call-start = ((), (), s32[]{:S(2)}) async-start(), calls=%async_computation | async-start | bytes 8388608 | tf_op jit(solution)/shard_map/psum | solution.py:945
  9.5 16.0 %collective-permute-start = (bf16[4,128,1024]{2,1,0:T(8,128)(2,1)}, bf16[4,128,1024]{2,1,0:T(8,128)(2,1)}, u32[]{:S(2)}, u32[]{:S(2)}) collective-permute-start(bf16[4,128,1024]{2,1,0:T(8,128)(2,1)} %pack.1.refs_0_.refs_9_.refs_18_), channel_id=1, source_target_pairs={{0,8},{1,5},{2,10},{3,7},{4,0},{5,13},{6,2},{7,15},{8,16},{9,1},{1... | collective-permute-start | bytes 3145736 | tf_op jit(solution)/shard_map/ppermute | solution.py:853
  16.0 15.1 %collective-permute-start.8 = (bf16[2,128,1024]{2,1,0:T(8,128)(2,1)}, bf16[2,128,1024]{2,1,0:T(8,128)(2,1)}, u32[]{:S(2)}, u32[]{:S(2)}) collective-permute-start(bf16[2,128,1024]{2,1,0:T(8,128)(2,1)} %get-tuple-element.68.refs_1_.refs_0_.refs_9_), channel_id=1, source_target_pairs={{0,8},{1,5},{2,10},{3,7},{4,0},{5,13},{6,2},{7,15},{8,16},{9,1},{1... | collective-permute-start | bytes 1572872 | tf_op jit(solution)/shard_map/ppermute | solution.py:853
  26.0 18.6 %collective-permute-start.1 = (bf16[4,128,1024]{2,1,0:T(8,128)(2,1)}, bf16[4,128,1024]{2,1,0:T(8,128)(2,1)}, u32[]{:S(2)}, u32[]{:S(2)}) collective-permute-start(bf16[4,128,1024]{2,1,0:T(8,128)(2,1)} %get-tuple-element.69.refs_1_.refs_10_.refs_19_), channel_id=1, source_target_pairs={{0,1},{1,0},{2,3},{3,2},{4,5},{5,4},{6,7},{7,6},{8,9},{9,8},{10,11... | collective-permute-start | bytes 3145736 | tf_op jit(solution)/shard_map/ppermute | solution.py:853
  26.1 18.5 %collective-permute-start.2 = (bf16[4,128,1024]{2,1,0:T(8,128)(2,1)}, bf16[4,128,1024]{2,1,0:T(8,128)(2,1)}, u32[]{:S(2)}, u32[]{:S(2)}) collective-permute-start(bf16[4,128,1024]{2,1,0:T(8,128)(2,1)} %get-tuple-element.69.refs_1_.refs_10_.refs_19_), channel_id=1, source_target_pairs={{0,8},{1,5},{2,10},{3,7},{4,0},{5,13},{6,2},{7,15},{8,16},{9,1},{1... | collective-permute-start | bytes 3145736 | tf_op jit(solution)/shard_map/ppermute | solution.py:853
  31.1 13.5 %collective-permute-start.11 = (bf16[2,128,1024]{2,1,0:T(8,128)(2,1)}, bf16[2,128,1024]{2,1,0:T(8,128)(2,1)}, u32[]{:S(2)}, u32[]{:S(2)}) collective-permute-start(bf16[2,128,1024]{2,1,0:T(8,128)(2,1)} %collective-permute-done.8.refs_1_.refs_10_), channel_id=1, source_target_pairs={{0,2},{1,3},{2,0},{3,1},{4,6},{5,7},{6,4},{7,5},{8,10},{9,11},{10,... | collective-permute-start | bytes 1572872 | tf_op jit(solution)/shard_map/ppermute | solution.py:853
  33.2 14.8 %collective-permute-start.9 = (bf16[2,128,1024]{2,1,0:T(8,128)(2,1)}, bf16[2,128,1024]{2,1,0:T(8,128)(2,1)}, u32[]{:S(2)}, u32[]{:S(2)}) collective-permute-start(bf16[2,128,1024]{2,1,0:T(8,128)(2,1)} %collective-permute-done.8.refs_1_.refs_10_), channel_id=1, source_target_pairs={{0,8},{1,5},{2,10},{3,7},{4,0},{5,13},{6,2},{7,15},{8,16},{9,1},{1... | collective-permute-start | bytes 1572872 | tf_op jit(solution)/shard_map/ppermute | solution.py:853
  34.7 13.2 %collective-permute-start.10 = (bf16[2,128,1024]{2,1,0:T(8,128)(2,1)}, bf16[2,128,1024]{2,1,0:T(8,128)(2,1)S(1)}, u32[]{:S(2)}, u32[]{:S(2)}) collective-permute-start(bf16[2,128,1024]{2,1,0:T(8,128)(2,1)} %collective-permute-done.8.refs_1_.refs_10_), channel_id=1, source_target_pairs={{0,1},{1,0},{2,3},{3,2},{4,5},{5,4},{6,7},{7,6},{8,9},{9,8},{10,11... | collective-permute-start | bytes 1572872 | tf_op jit(solution)/shard_map/ppermute | solution.py:853
  44.6 3.4 collective-permute-start.12
  45.1 17.7 %collective-permute-start.3 = (bf16[4,128,1024]{2,1,0:T(8,128)(2,1)}, bf16[4,128,1024]{2,1,0:T(8,128)(2,1)}, u32[]{:S(2)}, u32[]{:S(2)}) collective-permute-start(bf16[4,128,1024]{2,1,0:T(8,128)(2,1)} %get-tuple-element.70.refs_3_.refs_12_.refs_21_), channel_id=1, source_target_pairs={{0,1},{1,0},{2,3},{3,2},{4,5},{5,4},{6,7},{7,6},{8,9},{9,8},{10,11... | collective-permute-start | bytes 3145736 | tf_op jit(solution)/shard_map/ppermute | solution.py:853
  45.7 17.2 %collective-permute-start.4 = (bf16[4,128,1024]{2,1,0:T(8,128)(2,1)}, bf16[4,128,1024]{2,1,0:T(8,128)(2,1)}, u32[]{:S(2)}, u32[]{:S(2)}) collective-permute-start(bf16[4,128,1024]{2,1,0:T(8,128)(2,1)} %get-tuple-element.70.refs_3_.refs_12_.refs_21_), channel_id=1, source_target_pairs={{0,8},{1,5},{2,10},{3,7},{4,0},{5,13},{6,2},{7,15},{8,16},{9,1},{1... | collective-permute-start | bytes 3145736 | tf_op jit(solution)/shard_map/ppermute | solution.py:853
  49.3 13.6 %collective-permute-start.15 = (bf16[2,128,1024]{2,1,0:T(8,128)(2,1)}, bf16[2,128,1024]{2,1,0:T(8,128)(2,1)}, u32[]{:S(2)}, u32[]{:S(2)}) collective-permute-start(bf16[2,128,1024]{2,1,0:T(8,128)(2,1)} %get-tuple-element.72.refs_3_.refs_12_), channel_id=1, source_target_pairs={{0,2},{1,3},{2,0},{3,1},{4,6},{5,7},{6,4},{7,5},{8,10},{9,11},{10,... | collective-permute-start | bytes 1572872 | tf_op jit(solution)/shard_map/ppermute | solution.py:853
  51.4 15.7 %collective-permute-start.13 = (bf16[2,128,1024]{2,1,0:T(8,128)(2,1)}, bf16[2,128,1024]{2,1,0:T(8,128)(2,1)S(1)}, u32[]{:S(2)}, u32[]{:S(2)}) collective-permute-start(bf16[2,128,1024]{2,1,0:T(8,128)(2,1)} %get-tuple-element.72.refs_3_.refs_12_), channel_id=1, source_target_pairs={{0,8},{1,5},{2,10},{3,7},{4,0},{5,13},{6,2},{7,15},{8,16},{9,1},{1... | collective-permute-start | bytes 1572872 | tf_op jit(solution)/shard_map/ppermute | solution.py:853
  53.0 14.2 %collective-permute-start.14 = (bf16[2,128,1024]{2,1,0:T(8,128)(2,1)}, bf16[2,128,1024]{2,1,0:T(8,128)(2,1)}, u32[]{:S(2)}, u32[]{:S(2)}) collective-permute-start(bf16[2,128,1024]{2,1,0:T(8,128)(2,1)} %get-tuple-element.72.refs_3_.refs_12_), channel_id=1, source_target_pairs={{0,1},{1,0},{2,3},{3,2},{4,5},{5,4},{6,7},{7,6},{8,9},{9,8},{10,11... | collective-permute-start | bytes 1572872 | tf_op jit(solution)/shard_map/ppermute | solution.py:853
  62.9 4.3 %collective-permute-start.16 = (bf16[2,128,1024]{2,1,0:T(8,128)(2,1)}, bf16[2,128,1024]{2,1,0:T(8,128)(2,1)}, u32[]{:S(2)}, u32[]{:S(2)}) collective-permute-start(bf16[2,128,1024]{2,1,0:T(8,128)(2,1)} %collective-permute-done.15.refs_21_), channel_id=1, source_target_pairs={{0,1},{1,0},{2,3},{3,2},{4,5},{5,4},{6,7},{7,6},{8,9},{9,8},{10,11... | collective-permute-start | bytes 1572872 | tf_op jit(solution)/shard_map/ppermute | solution.py:853
  65.3 9.5 %collective-permute-start.6 = (bf16[4,64,1024]{2,1,0:T(8,128)(2,1)}, bf16[4,64,1024]{2,1,0:T(8,128)(2,1)}, u32[]{:S(2)}, u32[]{:S(2)}) collective-permute-start(bf16[4,64,1024]{2,1,0:T(8,128)(2,1)} %constant_dynamic-slice_fusion.2), channel_id=1, source_target_pairs={{0,8},{1,5},{2,10},{3,7},{4,0},{5,13},{6,2},{7,15},{8,16},{9,1},{1... | collective-permute-start | bytes 1572872 | tf_op jit(solution)/shard_map/ppermute | solution.py:853
  67.0 17.8 %collective-permute-start.5 = (bf16[4,128,1024]{2,1,0:T(8,128)(2,1)}, bf16[4,128,1024]{2,1,0:T(8,128)(2,1)}, u32[]{:S(2)}, u32[]{:S(2)}) collective-permute-start(bf16[4,128,1024]{2,1,0:T(8,128)(2,1)} %get-tuple-element.71.refs_5_.refs_14_.refs_23_), channel_id=1, source_target_pairs={{0,1},{1,0},{2,3},{3,2},{4,5},{5,4},{6,7},{7,6},{8,9},{9,8},{10,11... | collective-permute-start | bytes 3145736 | tf_op jit(solution)/shard_map/ppermute | solution.py:853
  68.5 14.6 %collective-permute-start.21 = (bf16[2,128,1024]{2,1,0:T(8,128)(2,1)}, bf16[2,128,1024]{2,1,0:T(8,128)(2,1)}, u32[]{:S(2)}, u32[]{:S(2)}) collective-permute-start(bf16[2,128,1024]{2,1,0:T(8,128)(2,1)} %get-tuple-element.73.refs_5_.refs_14_), channel_id=1, source_target_pairs={{0,2},{1,3},{2,0},{3,1},{4,6},{5,7},{6,4},{7,5},{8,10},{9,11},{10,... | collective-permute-start | bytes 1572872 | tf_op jit(solution)/shard_map/ppermute | solution.py:853
  74.8 9.8 %collective-permute-start.7 = (bf16[4,64,1024]{2,1,0:T(8,128)(2,1)}, bf16[4,64,1024]{2,1,0:T(8,128)(2,1)}, u32[]{:S(2)}, u32[]{:S(2)}) collective-permute-start(bf16[4,64,1024]{2,1,0:T(8,128)(2,1)} %collective-permute-done.6.refs_1_.refs_7_.refs_16_.refs_25_), channel_id=1, source_target_pairs={{0,1},{1,0},{2,3},{3,2},{4,5},{5,4},{6,7},{7,6},{8,9},{9,8},{10,11... | collective-permute-start | bytes 1572872 | tf_op jit(solution)/shard_map/ppermute | solution.py:853
  75.8 6.5 %collective-permute-start.17 = (bf16[2,64,1024]{2,1,0:T(8,128)(2,1)S(1)}, bf16[2,64,1024]{2,1,0:T(8,128)(2,1)}, u32[]{:S(2)}, u32[]{:S(2)}) collective-permute-start(bf16[2,64,1024]{2,1,0:T(8,128)(2,1)S(1)} %constant_dynamic-slice_fusion.1), channel_id=1, source_target_pairs={{0,8},{1,5},{2,10},{3,7},{4,0},{5,13},{6,2},{7,15},{8,16},{9,1},{1... | collective-permute-start | bytes 786440 | tf_op jit(solution)/shard_map/ppermute | solution.py:853
  80.6 20.2 %collective-permute-start.19 = (bf16[2,128,1024]{2,1,0:T(8,128)(2,1)S(1)}, bf16[2,128,1024]{2,1,0:T(8,128)(2,1)}, u32[]{:S(2)}, u32[]{:S(2)}) collective-permute-start(bf16[2,128,1024]{2,1,0:T(8,128)(2,1)S(1)} %copy-done.1), channel_id=1, source_target_pairs={{0,1},{1,0},{2,3},{3,2},{4,5},{5,4},{6,7},{7,6},{8,9},{9,8},{10,11... | collective-permute-start | bytes 1572872 | tf_op jit(solution)/shard_map/ppermute | solution.py:853
  82.3 18.5 %collective-permute-start.20 = (bf16[2,64,1024]{2,1,0:T(8,128)(2,1)}, bf16[2,64,1024]{2,1,0:T(8,128)(2,1)}, u32[]{:S(2)}, u32[]{:S(2)}) collective-permute-start(bf16[2,64,1024]{2,1,0:T(8,128)(2,1)} %collective-permute-done.17.refs_2_.refs_7_.refs_16_), channel_id=1, source_target_pairs={{0,1},{1,0},{2,3},{3,2},{4,5},{5,4},{6,7},{7,6},{8,9},{9,8},{10,11... | collective-permute-start | bytes 786440 | tf_op jit(solution)/shard_map/ppermute | solution.py:853
  83.1 16.4 %collective-permute-start.23 = (bf16[2,64,1024]{2,1,0:T(8,128)(2,1)}, bf16[2,64,1024]{2,1,0:T(8,128)(2,1)S(1)}, u32[]{:S(2)}, u32[]{:S(2)}) collective-permute-start(bf16[2,64,1024]{2,1,0:T(8,128)(2,1)} %collective-permute-done.17.refs_2_.refs_7_.refs_16_), channel_id=1, source_target_pairs={{0,2},{1,3},{2,0},{3,1},{4,6},{5,7},{6,4},{7,5},{8,10},{9,11},{10,... | collective-permute-start | bytes 786440 | tf_op jit(solution)/shard_map/ppermute | solution.py:853
  84.6 16.2 %collective-permute-start.22 = (bf16[2,128,1024]{2,1,0:T(8,128)(2,1)}, bf16[2,128,1024]{2,1,0:T(8,128)(2,1)}, u32[]{:S(2)}, u32[]{:S(2)}) collective-permute-start(bf16[2,128,1024]{2,1,0:T(8,128)(2,1)} %collective-permute-done.21.refs_23_), channel_id=1, source_target_pairs={{0,1},{1,0},{2,3},{3,2},{4,5},{5,4},{6,7},{7,6},{8,9},{9,8},{10,11... | collective-permute-start | bytes 1572872 | tf_op jit(solution)/shard_map/ppermute | solution.py:853
  84.8 28.3 %collective-permute-start.18 = (bf16[8,128,1024]{2,1,0:T(8,128)(2,1)}, bf16[8,128,1024]{2,1,0:T(8,128)(2,1)}, u32[]{:S(2)}, u32[]{:S(2)}) collective-permute-start(bf16[8,128,1024]{2,1,0:T(8,128)(2,1)} %get-tuple-element.74.refs_27_), channel_id=1, source_target_pairs={{0,8},{1,5},{2,10},{3,7},{4,0},{5,13},{6,2},{7,15},{8,16},{9,1},{1... | collective-permute-start | bytes 6291464 | tf_op jit(solution)/shard_map/ppermute | solution.py:853
  113.7 33.3 %collective-permute-start.25 = (bf16[8,128,1024]{2,1,0:T(8,128)(2,1)}, bf16[8,128,1024]{2,1,0:T(8,128)(2,1)}, u32[]{:S(2)}, u32[]{:S(2)}) collective-permute-start(bf16[8,128,1024]{2,1,0:T(8,128)(2,1)} %get-tuple-element.80.refs_0_.refs_28_), channel_id=1, source_target_pairs={{0,8},{1,5},{2,10},{3,7},{4,0},{5,13},{6,2},{7,15},{8,16},{9,1},{1... | collective-permute-start | bytes 6291464 | tf_op jit(solution)/shard_map/ppermute | solution.py:853
  147.5 26.7 %collective-permute-start.26 = (bf16[8,128,1024]{2,1,0:T(8,128)(2,1)}, bf16[8,128,1024]{2,1,0:T(8,128)(2,1)}, u32[]{:S(2)}, u32[]{:S(2)}) collective-permute-start(bf16[8,128,1024]{2,1,0:T(8,128)(2,1)} %get-tuple-element.86.refs_27_.refs_30_), channel_id=1, source_target_pairs={{0,8},{1,5},{2,10},{3,7},{4,0},{5,13},{6,2},{7,15},{8,16},{9,1},{1... | collective-permute-start | bytes 6291464 | tf_op jit(solution)/shard_map/ppermute | solution.py:853
  177.0 15.6 %collective-permute-start.30 = (bf16[8,64,1024]{2,1,0:T(8,128)(2,1)}, bf16[8,64,1024]{2,1,0:T(8,128)(2,1)}, u32[]{:S(2)}, u32[]{:S(2)}) collective-permute-start(bf16[8,64,1024]{2,1,0:T(8,128)(2,1)} %constant_dynamic-slice_fusion), channel_id=1, source_target_pairs={{0,8},{1,5},{2,10},{3,7},{4,0},{5,13},{6,2},{7,15},{8,16},{9,1},{1... | collective-permute-start | bytes 3145736 | tf_op jit(solution)/shard_map/ppermute | solution.py:853
  178.0 15.1 %collective-permute-start.27 = (bf16[8,128,1024]{2,1,0:T(8,128)(2,1)}, bf16[8,128,1024]{2,1,0:T(8,128)(2,1)}, u32[]{:S(2)}, u32[]{:S(2)}) collective-permute-start(bf16[8,128,1024]{2,1,0:T(8,128)(2,1)} %get-tuple-element.80.refs_0_.refs_28_), channel_id=1, source_target_pairs={{0,1},{1,0},{2,3},{3,2},{4,5},{5,4},{6,7},{7,6},{8,9},{9,8},{10,11... | collective-permute-start | bytes 6291464 | tf_op jit(solution)/shard_map/ppermute | solution.py:853
  178.0 15.1 %collective-permute-start.28 = (bf16[8,128,1024]{2,1,0:T(8,128)(2,1)}, bf16[8,128,1024]{2,1,0:T(8,128)(2,1)}, u32[]{:S(2)}, u32[]{:S(2)}) collective-permute-start(bf16[8,128,1024]{2,1,0:T(8,128)(2,1)} %get-tuple-element.86.refs_27_.refs_30_), channel_id=1, source_target_pairs={{0,1},{1,0},{2,3},{3,2},{4,5},{5,4},{6,7},{7,6},{8,9},{9,8},{10,11... | collective-permute-start | bytes 6291464 | tf_op jit(solution)/shard_map/ppermute | solution.py:853
  178.5 17.6 %collective-permute-start.29 = (bf16[8,128,1024]{2,1,0:T(8,128)(2,1)}, bf16[8,128,1024]{2,1,0:T(8,128)(2,1)}, u32[]{:S(2)}, u32[]{:S(2)}) collective-permute-start(bf16[8,128,1024]{2,1,0:T(8,128)(2,1)} %get-tuple-element.95.refs_3_.refs_32_), channel_id=1, source_target_pairs={{0,1},{1,0},{2,3},{3,2},{4,5},{5,4},{6,7},{7,6},{8,9},{9,8},{10,11... | collective-permute-start | bytes 6291464 | tf_op jit(solution)/shard_map/ppermute | solution.py:853
  193.0 3.1 collective-permute-start.31
  (11 other events, 45.3 us)
Sparse Core Ops, SparseCore 0:
  242.0 140.2 all-reduce.2
where the time goes:
time: 412 us; the launch traced here: 404 us
  Pallas kernels  289 us (70%)
  waiting for transfers between devices  47.1 us (11%)
  starting transfers between devices  29.1 us (7%)
  between operations  15.5 us (4%)
  other arithmetic  12.1 us (3%)
  local copies, waits for them, and re-layouts  12 us (3%)
    pallas_call x2, Pallas kernels, attend_back(): pl.pallas_call(functools.partial(attend_back_kernel, causal), grid=(pairs...  72.3 us
    pallas_call x4, Pallas kernels, attend(): pl.pallas_call(functools.partial(attend_kernel, causal, q_at, k_at, start...  55 us
    ppermute x32, waiting for transfers between devices, send(): return lax.ppermute(values, AXES, pairs)  46.6 us
    pallas_call x1, Pallas kernels, feed(): pl.pallas_call(functools.partial(feed_kernel, (output_at,), len(feed_piec...  45.7 us
    pallas_call x1, Pallas kernels, feed_back(): pl.pallas_call(functools.partial(feed_back_kernel, (output_at,), len(feed...  35.7 us
    ppermute x32, starting transfers between devices, send(): return lax.ppermute(values, AXES, pairs)  29.1 us
    pallas_call x2, Pallas kernels, project(): pl.pallas_call(functools.partial(project_kernel, wanted, scale, squared,...  23 us
    pallas_call x1, Pallas kernels, after_cross_back(): pl.pallas_call(functools.partial(cross_back_kernel, wanted), grid=(tokens...  19.4 us
  transfers between devices with their start and end apart: 33, of which 13 were waited for; matrix products, arithmetic and copies ran while one was open for 1% of the time, Pallas kernels for 59%

commit v1 on v0

--- a/solution.py
+++ b/solution.py
@@ -23,7 +23,7 @@
 f32, bf16 = jnp.float32, jnp.bfloat16
 query_scale = HEAD_DIM ** (-0.5) * math.log2(math.e)
 forbidden = -(2.0**100)
-score_limit = 64.0
+least_sum, most_sum = 2.0**-40, 2.0**60
 
 params = pltpu.CompilerParams(vmem_limit_bytes=63 * 2**20)
 
@@ -116,18 +116,9 @@
     return u * below, below + u * bell
 
 
-def head_squares(values):
-    width = values.shape[1]
-    member = (
-        lax.broadcasted_iota(jnp.int32, (width, PAIR), 0) >> 6
-        == lax.broadcasted_iota(jnp.int32, (width, PAIR), 1)
-    ).astype(bf16)
-    return jnp.max(contract(values * values, member, 1, 0), axis=0, keepdims=True)
-
-
-def project_kernel(wanted, scale, squared, count, x_ref, table_ref, *refs):
+def project_kernel(wanted, scale, count, x_ref, table_ref, *refs):
     pieces = refs[:count]
-    out_ref, square_ref, store, sems = refs[-4:]
+    out_ref, store, sems = refs[-3:]
     step = pl.program_id(0)
 
     @pl.when(step == 0)
@@ -143,31 +134,17 @@
         loaded(store, sems, step)
         out_ref[0] = contract(x_ref[...], store[step], 1, 0).astype(bf16)
 
-    @pl.when(step < squared)
-    def squares():
-        square_ref[0] = jnp.broadcast_to(head_squares(out_ref[0]), square_ref.shape[1:])
-
-    @pl.when(step >= squared)
-    def no_squares():
-        square_ref[0] = jnp.zeros(square_ref.shape[1:], f32)
-
-
-def project(x, table, pieces, wanted, scale, squared, sooner=()):
+
+def project(x, table, pieces, wanted, scale, sooner=()):
     tokens, width = x.shape
     count = len(wanted)
     return pl.pallas_call(
-        functools.partial(project_kernel, wanted, scale, squared, len(pieces)),
+        functools.partial(project_kernel, wanted, scale, len(pieces)),
         grid=(count,),
         in_specs=[pl.BlockSpec((tokens, width), lambda i: (0, 0)), smem()]
         + [in_place() for piece in (*pieces, *sooner)],
-        out_specs=[
-            pl.BlockSpec((1, tokens, width), lambda i: (i, 0, 0)),
-            pl.BlockSpec((1, 8, PAIR), lambda i: (i, 0, 0)),
-        ],
-        out_shape=[
-            jax.ShapeDtypeStruct((count, tokens, width), bf16),
-            jax.ShapeDtypeStruct((count, 8, PAIR), f32),
-        ],
+        out_specs=pl.BlockSpec((1, tokens, width), lambda i: (i, 0, 0)),
+        out_shape=jax.ShapeDtypeStruct((count, tokens, width), bf16),
         scratch_shapes=stores(count, width),
         compiler_params=params,
         cost_estimate=cost(4 * count),
@@ -197,13 +174,12 @@
 
 
 def attend_kernel(
-    causal, q_at, k_at, start, bucket_ref, lengths_ref, qsq_ref, ksq_ref, q_ref, k_ref, v_ref, *refs
+    causal, bucket_ref, lengths_ref, q_ref, k_ref, v_ref, *refs
 ):
     out_ref, weight_ref, share_ref, done_ref, qmark, kmark = refs[-6:]
     done_ref[...] = jnp.zeros_like(done_ref)
     tokens = q_ref.shape[-2]
     low = low_half(tokens)
-    pair = pl.program_id(0) + start
 
     @pl.when(pl.program_id(0) == 0)
     def marks():
@@ -232,13 +208,8 @@
         out_ref[...] = out.astype(bf16).T
         share_ref[0, 0:1] = even_share[:1]
         share_ref[0, 1:2] = odd_share[:1]
-
-    bound = score_limit * score_limit
-    small = (
-        qsq_ref[q_at, 0, 2 * pair] * ksq_ref[k_at, 0, 2 * pair] <= bound
-    ) & (qsq_ref[q_at, 0, 2 * pair + 1] * ksq_ref[k_at, 0, 2 * pair + 1] <= bound)
-
-    @pl.when(small)
+        return even[HEAD_DIM : HEAD_DIM + 1], odd[:1]
+
     def direct():
         sums = []
         for head in range(2):
@@ -264,9 +235,12 @@
             weight_ref[head, step:, step:] = low_part
             rest = contract(values[step:], low_part, 0, 0)
             sums.append(jnp.concatenate([total[:, :step], total[:, step:] + rest], axis=1))
-        finish(sums)
-
-    @pl.when(jnp.logical_not(small))
+        return finish(sums)
+
+    totals = jnp.concatenate(direct(), axis=0)
+    sound = (jnp.min(totals) >= least_sum) & (jnp.max(totals) <= most_sum)
+
+    @pl.when(jnp.logical_not(sound))
     def shifted():
         sums = []
         for head in range(2):
@@ -285,15 +259,15 @@
 
 
 def attend(bucket, lengths, q_pack, k_pack, v_pack, causal, start, stop, so_far=(), sooner=()):
-    (q, q_squares, q_at), (k, k_squares, k_at), (v, unused, v_at) = q_pack, k_pack, v_pack
+    (q, q_at), (k, k_at), (v, v_at) = q_pack, k_pack, v_pack
     tokens, width = q.shape[1:]
     pairs = width // PAIR
     pair_spec = lambda at: pl.BlockSpec((1, tokens, PAIR), lambda j: (at, 0, start + j))
     flat_spec = pl.BlockSpec((tokens, PAIR), lambda j: (0, start + j))
     return pl.pallas_call(
-        functools.partial(attend_kernel, causal, q_at, k_at, start),
+        functools.partial(attend_kernel, causal),
         grid=(stop - start,),
-        in_specs=[smem(), smem(), smem(), smem(), pair_spec(q_at), pair_spec(k_at), pair_spec(v_at)]
+        in_specs=[smem(), smem(), pair_spec(q_at), pair_spec(k_at), pair_spec(v_at)]
         + [in_place() for array in (*so_far, *sooner)],
         out_specs=[
             flat_spec,
@@ -307,12 +281,12 @@
             jax.ShapeDtypeStruct((pairs, 2, tokens), f32),
             jax.ShapeDtypeStruct((8, PAIR), f32),
         ],
-        input_output_aliases={7 + i: i for i in range(len(so_far))},
+        input_output_aliases={5 + i: i for i in range(len(so_far))},
         scratch_shapes=[pltpu.VMEM((tokens, PAIR), bf16), pltpu.VMEM((tokens, PAIR), bf16)],
         compiler_params=params,
         cost_estimate=cost(0.05 * (stop - start)),
         name="attend",
-    )(bucket, lengths, q_squares, k_squares, q, k, v, *so_far, *sooner)
+    )(bucket, lengths, q, k, v, *so_far, *sooner)
 
 
 def attend_back_kernel(
@@ -363,7 +337,7 @@
 
 
 def attend_back(q_pack, k_pack, v_pack, grad, out, weight, causal):
-    (q, unused, q_at), (k, unused, k_at), (v, unused, v_at) = q_pack, k_pack, v_pack
+    (q, q_at), (k, k_at), (v, v_at) = q_pack, k_pack, v_pack
     tokens, width = q.shape[1:]
     pairs = width // PAIR
     pair_spec = lambda at: pl.BlockSpec((1, tokens, PAIR), lambda j: (at, 0, j))
@@ -389,7 +363,7 @@
 
 def first_kernel(wanted, count, table_ref, x_ref, out_ref, gains_ref, *refs):
     pieces = refs[:count]
-    first_ref, inverse_ref, q_ref, square_ref, store, sems = refs[-6:]
+    first_ref, inverse_ref, q_ref, store, sems = refs[-5:]
     step = pl.program_id(0)
 
     @pl.when(step == 0)
@@ -405,15 +379,6 @@
     loaded_once(store, sems, 1)
     q = (contract(first.astype(bf16), store[1], 1, 0) * query_scale).astype(bf16)
     q_ref[0] = q
-    squares = jnp.broadcast_to(head_squares(q), square_ref.shape[1:])
-
-    @pl.when(step == 0)
-    def begin():
-        square_ref[0] = squares
-
-    @pl.when(step > 0)
-    def more():
-        square_ref[0] = jnp.maximum(square_ref[0], squares)
 
 
 def after_self(x, out, gains, table, pieces, wanted, sooner):
@@ -429,13 +394,11 @@
             tile,
             pl.BlockSpec((rows, PAIR), lambda i: (i, 0)),
             pl.BlockSpec((1, rows, width), lambda i: (0, i, 0)),
-            pl.BlockSpec((1, 8, PAIR), lambda i: (0, 0, 0)),
         ],
         out_shape=[
             jax.ShapeDtypeStruct((tokens, width), f32),
             jax.ShapeDtypeStruct((tokens, PAIR), f32),
             jax.ShapeDtypeStruct((1, tokens, width), bf16),
-            jax.ShapeDtypeStruct((1, 8, PAIR), f32),
         ],
         scratch_shapes=stores(len(wanted), width),
         compiler_params=params,
@@ -718,15 +681,42 @@
     )(table, dq, dk, dv, pre, *pieces)
 
 
-def adamw(master, first_moment, second_moment, gradient):
-    first_new = beta_first * first_moment + (1.0 - beta_first) * gradient
-    second_new = beta_second * second_moment + (1.0 - beta_second) * gradient * gradient
-    first_hat = first_new / (1.0 - beta_first**STEP)
-    second_hat = second_new / (1.0 - beta_second**STEP)
-    master_new = master - learn_rate * (
-        first_hat / (jnp.sqrt(second_hat) + epsilon_adam) + weight_decay * master
-    )
-    return (first_new, second_new, master_new)
+def adamw_kernel(*refs):
+    for ins, outs in ((refs[0:4], refs[8:13]), (refs[4:8], refs[13:18])):
+        master, first_moment, second_moment, gradient = (ref[...] for ref in ins)
+        first_new = beta_first * first_moment + (1.0 - beta_first) * gradient
+        second_new = beta_second * second_moment + (1.0 - beta_second) * gradient * gradient
+        first_hat = first_new / (1.0 - beta_first**STEP)
+        second_hat = second_new / (1.0 - beta_second**STEP)
+        master_new = master - learn_rate * (
+            first_hat / (jnp.sqrt(second_hat) + epsilon_adam) + weight_decay * master
+        )
+        for ref, value in zip(outs, (gradient, first_new, second_new, master_new, master_new.astype(bf16))):
+            ref[...] = value
+
+
+def adamw(down, up):
+    steps = 2
+
+    def spec(array):
+        return pl.BlockSpec((array.shape[0] // steps, array.shape[1]), lambda i: (i, 0))
+
+    ins = (*down, *up)
+    shapes = [
+        jax.ShapeDtypeStruct(arrays[0].shape, kind)
+        for arrays in (down, up)
+        for kind in (f32, f32, f32, f32, bf16)
+    ]
+    return pl.pallas_call(
+        adamw_kernel,
+        grid=(steps,),
+        in_specs=[spec(array) for array in ins],
+        out_specs=[spec(shape) for shape in shapes],
+        out_shape=shapes,
+        compiler_params=params,
+        cost_estimate=cost(10),
+        name="adamw",
+    )(*ins)
 
 
 def pack_kernel(*refs):
@@ -902,35 +892,37 @@
     ck, cv, cq, co = (0, 0), (0, 1), (1, 0), (1, 1)
     one = Gather(links, pack((self_query, self_key, self_value, self_output)))
     two = Gather(links, *pack_pair(table, (cross_key, cross_value, cross_query, cross_output)))
-    two_own = two.moving
+    late = Gather(links, pack_feed(fc_first, fc_second))
+    two_own, late_own = two.moving, late.moving
     one.hop(chained=True)
     two.hop(chained=True)
-    one.hop(two_own, chained=True)
+    one.hop(two_own, late_own, chained=True)
     two.hop(chained=True)
-    for quarter in range(2):
-        one.hop(chained=True)
-        two.hop(chained=True)
+    one.hop(chained=True)
+    two.hop(chained=True)
+    one.hop(chained=True)
+    two.hop(chained=True)
+    fourth = one.moving
     one.share()
     two.share()
-    late = Gather(links, pack_feed(fc_first, fc_second))
-    late.hop(one.moving, two.moving)
-
-    qkv, squares = project(inputs, table, one.pieces * 3, (sq, sk, sv), query_scale, 2, (late.shared,))
-    two.hand_over(squares)
+    late.hop(fourth)
+
+    qkv = project(inputs, table, one.pieces * 3, (sq, sk, sv), query_scale, (late.shared,))
+    two.hand_over(qkv)
     pieces = one.pieces + two.pieces + two.rest
-    kv, kv_squares = project(encoder, table, two.pieces + two.pieces + two.rest, (ck, cv), 1.0, 1, (squares,))
-    self_packs = [(qkv, squares, 0), (qkv, squares, 1), (qkv, None, 2)]
+    kv = project(encoder, table, two.pieces + two.pieces + two.rest, (ck, cv), 1.0, (qkv,))
+    self_packs = [(qkv, 0), (qkv, 1), (qkv, 2)]
     half = width // PAIR // 2
-    late.hop(squares, kv_squares)
+    late.hop(qkv, kv)
     *self_half, done = attend(buckets, lengths, *self_packs, True, 0, half, (), (late.shared,))
     self_out, self_weight, self_share, done = attend(
         buckets, lengths, *self_packs, True, half, 2 * half, self_half
     )
     late.hop(done)
-    first, first_inverse, query_cross, query_squares = after_self(
+    first, first_inverse, query_cross = after_self(
         inputs, self_out, norm_gains, table, pieces, (so, cq), (late.shared,)
     )
-    cross_packs = [(query_cross, query_squares, 0), (kv, kv_squares, 0), (kv, None, 1)]
+    cross_packs = [(query_cross, 0), (kv, 0), (kv, 1)]
     *cross_half, done = attend(buckets, lengths, *cross_packs, False, 0, half)
     late.hop(done)
     cross_out, cross_weight, cross_share, done = attend(
@@ -955,10 +947,12 @@
     dq, dk, dv = attend_back(*self_packs, grad_self_out, self_out, self_weight, True)
     input_grad = input_gradient(dq, dk, dv, grad_self_pre, table, pieces, (sq, sk, sv))
 
-    down_first_new, down_second_new, down_master_new = adamw(
-        down_master, down_first, down_second, down_grad
-    )
-    up_first_new, up_second_new, up_master_new = adamw(up_master, up_first, up_second, up_grad)
+    (
+        down_grad, down_first_new, down_second_new, down_master_new, down_weight,
+        up_grad, up_first_new, up_second_new, up_master_new, up_weight,
+    ) = adamw(
+        (down_master, down_first, down_second, down_grad), (up_master, up_first, up_second, up_grad)
+    )
     return (
         outputs,
         input_grad,
@@ -971,8 +965,8 @@
         up_second_new,
         down_master_new,
         up_master_new,
-        down_master_new.astype(bf16),
-        up_master_new.astype(bf16),
+        down_weight,
+        up_weight,
     )
 
 

time: 412 us -> 401 us (0.973)
  other arithmetic: 12.1 us -> 0 us
  waiting for transfers between devices: 47.1 us -> 52.1 us
    convert_element_type x2 -> x0, other arithmetic: 12.1 us -> none  [the longest x1 7.85 us: body(): down_master_new.astype(bf16)]
    pallas_call x6 -> x7, Pallas kernels: 77.9 us -> 78.6 us  [the longest x4 45.8 us: attend(): pl.pallas_call(functools.partial(attend_kernel, causal), grid=(stop - sta...]
  transfers between devices with their start and end apart: 33 -> 33, of which waited for: 13 -> 14; matrix products, arithmetic and copies ran while one was open for 1% -> 1% of each run, Pallas kernels for 59% -> 57%
where the time goes in v1:
time: 401 us; the launch traced here: 394 us
  Pallas kernels  288 us (72%)
  waiting for transfers between devices  52.1 us (13%)
  starting transfers between devices  29.8 us (7%)
  between operations  15.4 us (4%)
  local copies, waits for them, and re-layouts  8.88 us (2%)
    pallas_call x2, Pallas kernels, attend_back(): pl.pallas_call(functools.partial(attend_back_kernel, causal), grid=(pairs...  72.2 us
    ppermute x32, waiting for transfers between devices, send(): return lax.ppermute(values, AXES, pairs)  49.9 us
    pallas_call x4, Pallas kernels, attend(): pl.pallas_call(functools.partial(attend_kernel, causal), grid=(stop - sta...  45.8 us
    pallas_call x1, Pallas kernels, feed(): pl.pallas_call(functools.partial(feed_kernel, (output_at,), len(feed_piec...  45.7 us
    pallas_call x1, Pallas kernels, feed_back(): pl.pallas_call(functools.partial(feed_back_kernel, (output_at,), len(feed...  35.6 us
    ppermute x32, starting transfers between devices, send(): return lax.ppermute(values, AXES, pairs)  29.8 us
    pallas_call x2, Pallas kernels, project(): pl.pallas_call(functools.partial(project_kernel, wanted, scale, len(piece...  20.7 us
    pallas_call x1, Pallas kernels, after_cross_back(): pl.pallas_call(functools.partial(cross_back_kernel, wanted), grid=(tokens...  19.5 us
  transfers between devices with their start and end apart: 33, of which 14 were waited for; matrix products, arithmetic and copies ran while one was open for 1% of the time, Pallas kernels for 57%

profile of v1, /device:TPU:0, one launch (start us, length us, event | category | flops | bytes accessed | tf_op | source)
XLA Modules:
  0.0 394.2 jit_solution(15143455432833481910)
XLA Ops:
  7.2 2.2 pack.1.refs_0_.refs_9_.refs_18_
  9.5 3.0 collective-permute-start
  13.8 2.3 pack_pair.1
  17.6 3.0 pack_feed.1.refs_2_.refs_0_
  20.6 4.9 %collective-permute-done.refs_0_ = bf16[4,128,1024]{2,1,0:T(8,128)(2,1)} collective-permute-done((bf16[4,128,1024]{2,1,0:T(8,128)(2,1)}, bf16[4,128,1024]{2,1,0:T(8,128)(2,1)}, u32[]{:S(2)}, u32[]{:S(2)}) %collective-permute-start) | collective-permute-done | bytes 1048608 | tf_op jit(solution)/shard_map/ppermute | solution.py:843
  26.1 2.2 collective-permute-start.2
  28.2 2.9 collective-permute-done.9.refs_1_.refs_10_
  31.1 2.1 collective-permute-start.12
  34.7 9.9 %collective-permute-done.12.refs_19_ = bf16[2,128,1024]{2,1,0:T(8,128)(2,1)} collective-permute-done((bf16[2,128,1024]{2,1,0:T(8,128)(2,1)}, bf16[2,128,1024]{2,1,0:T(8,128)(2,1)}, u32[]{:S(2)}, u32[]{:S(2)}) %collective-permute-start.12) | collective-permute-done | bytes 524320 | tf_op jit(solution)/shard_map/ppermute | solution.py:843
  52.2 10.5 %collective-permute-done.16.refs_21_ = bf16[2,128,1024]{2,1,0:T(8,128)(2,1)} collective-permute-done((bf16[2,128,1024]{2,1,0:T(8,128)(2,1)}, bf16[2,128,1024]{2,1,0:T(8,128)(2,1)}, u32[]{:S(2)}, u32[]{:S(2)}) %collective-permute-start.16) | collective-permute-done | bytes 524320 | tf_op jit(solution)/shard_map/ppermute | solution.py:843
  69.8 4.8 %collective-permute-done.6.refs_1_.refs_7_.refs_16_.refs_25_ = bf16[4,64,1024]{2,1,0:T(8,128)(2,1)} collective-permute-done((bf16[4,64,1024]{2,1,0:T(8,128)(2,1)}, bf16[4,64,1024]{2,1,0:T(8,128)(2,1)}, u32[]{:S(2)}, u32[]{:S(2)}) %collective-permute-start.6) | collective-permute-done | bytes 524320 | tf_op jit(solution)/shard_map/ppermute | solution.py:843
  77.4 4.7 %collective-permute-done.19.refs_7_.refs_16_ = bf16[2,64,1024]{2,1,0:T(8,128)(2,1)} collective-permute-done((bf16[2,64,1024]{2,1,0:T(8,128)(2,1)S(1)}, bf16[2,64,1024]{2,1,0:T(8,128)(2,1)}, u32[]{:S(2)}, u32[]{:S(2)}) %collective-permute-start.19) | collective-permute-done | bytes 262176 | tf_op jit(solution)/shard_map/ppermute | solution.py:843
  85.6 11.5 %project.2.refs_1_.refs_27_.q_ref.k_ref.v_ref = bf16[3,1024,1024]{2,1,0:T(8,128)(2,1)} custom-call(bf16[1024,1024]{1,0:T(8,128)(2,1)} %x_ref.5, s32[4,9]{1,0:T(4,128)} %dynamic-slice_bitcast_fusion.table_ref, bf16[4,128,1024]{2,1,0:T(8,128)(2,1)} %pack.1.refs_0_.refs_9_.refs_18_, bf16[4,128,1024]{2,1,0:T(8,128)(2,1)} %get-tuple-element.74.refs_1_.refs_10_.refs_19_, ...), custom_call_target="tpu_custom_call" | custom-call | flops 13799999488 | bytes 100000 | tf_op jit(solution)/shard_map/project/pallas_call | solution.py:141
  101.0 9.2 %project.3.refs_2_.k_ref.v_ref = bf16[2,1024,1024]{2,1,0:T(8,128)(2,1)} custom-call(bf16[1024,1024]{1,0:T(8,128)(2,1)} %x_ref.4, s32[4,9]{1,0:T(4,128)} %dynamic-slice_bitcast_fusion.table_ref, bf16[2,128,1024]{2,1,0:T(8,128)(2,1)} %get-tuple-element.73.refs_1_.refs_0_.refs_9_, bf16[2,128,1024]{2,1,0:T(8,128)(2,1)} %collective-permute-done.9.refs_1_.refs_10_, ...), custom_call_target="tpu_custom_call" | custom-call | flops 9200000000 | bytes 100000 | tf_op jit(solution)/shard_map/project/pallas_call | solution.py:141
  113.4 11.3 %attend.4 = (bf16[1024,1024]{1,0:T(8,128)(2,1)}, bf16[16,1024,1024]{2,1,0:T(8,128)(2,1)}, f32[8,2,1024]{2,1,0:T(2,128)}, f32[8,128]{1,0:T(8,128)}) custom-call(s32[1]{0:T(128)S(6)} %copy.72.bucket_ref, s32[1,4]{1,0:T(1,128)} %lengths_ref.9, bf16[3,1024,1024]{2,1,0:T(8,128)(2,1)} %project.2.refs_1_.refs_27_.q_ref.k_ref.v_ref, ...), custom_call_target="tpu_custom_call" | custom-call | flops 230000000 | bytes 100000 | tf_op jit(solution)/shard_map/attend/pallas_call | solution.py:267
  124.7 11.3 %attend.5 = (bf16[1024,1024]{1,0:T(8,128)(2,1)}, bf16[16,1024,1024]{2,1,0:T(8,128)(2,1)}, f32[8,2,1024]{2,1,0:T(2,128)}, f32[8,128]{1,0:T(8,128)}) custom-call(s32[1]{0:T(128)S(6)} %copy.72.bucket_ref, s32[1,4]{1,0:T(1,128)} %lengths_ref.9, ...), custom_call_target="tpu_custom_call", output_to_operand_aliasing={{0}: (5, {}), {1}: (6, {}), {2}: (7, {})} | custom-call | flops 230000000 | bytes 100000 | tf_op jit(solution)/shard_map/attend/pallas_call | solution.py:267
  136.0 2.0 collective-permute-done.25.refs_0_
  139.9 10.7 %after_self.1 = (f32[1024,1024]{1,0:T(8,128)}, f32[1024,128]{1,0:T(8,128)}, bf16[1,1024,1024]{2,1,0:T(8,128)(2,1)}) custom-call(s32[4,9]{1,0:T(4,128)} %dynamic-slice_bitcast_fusion.table_ref, bf16[1024,1024]{1,0:T(8,128)(2,1)} %x_ref.5, bf16[1024,1024]{1,0:T(8,128)(2,1)} %get-tuple-element.86.out_ref, f32[3,1024]{1,0:T(4,128)} %gains_ref.7, ...), custom_call_target="tpu_custom_call" | custom-call | flops 230000000 | bytes 100000 | tf_op jit(solution)/shard_map/after_self/pallas_call | solution.py:388
  150.6 11.6 %attend.6 = (bf16[1024,1024]{1,0:T(8,128)(2,1)}, bf16[16,1024,1024]{2,1,0:T(8,128)(2,1)}, f32[8,2,1024]{2,1,0:T(2,128)}, f32[8,128]{1,0:T(8,128)}) custom-call(s32[1]{0:T(128)S(6)} %copy.72.bucket_ref, s32[1,4]{1,0:T(1,128)} %lengths_ref.9, bf16[1,1024,1024]{2,1,0:T(8,128)(2,1)} %get-tuple-element.90.q_ref, ...), custom_call_target="tpu_custom_call" | custom-call | flops 230000000 | bytes 100000 | tf_op jit(solution)/shard_map/attend/pallas_call | solution.py:267
  162.1 3.0 collective-permute-done.26.refs_0_
  165.7 2.3 constant_dynamic-slice_fusion
  170.0 11.6 %attend.7 = (bf16[1024,1024]{1,0:T(8,128)(2,1)}, bf16[16,1024,1024]{2,1,0:T(8,128)(2,1)}, f32[8,2,1024]{2,1,0:T(2,128)}, f32[8,128]{1,0:T(8,128)}) custom-call(s32[1]{0:T(128)S(6)} %copy.72.bucket_ref, s32[1,4]{1,0:T(1,128)} %lengths_ref.9, ...), custom_call_target="tpu_custom_call", output_to_operand_aliasing={{0}: (5, {}), {1}: (6, {}), {2}: (7, {})} | custom-call | flops 230000000 | bytes 100000 | tf_op jit(solution)/shard_map/attend/pallas_call | solution.py:267
  181.6 1.9 collective-permute-done.30.refs_0_
  184.1 3.0 collective-permute-done.31.refs_35_
  187.1 45.7 %feed.1 = (bf16[1024,1024]{1,0:T(8,128)(2,1)}, f32[1024,1024]{1,0:T(8,128)}, bf16[4,1024,1024]{2,1,0:T(8,128)(2,1)}, bf16[1024,1024]{1,0:T(8,128)(2,1)}, f32[102...) custom-call(s32[1]{0:T(128)S(6)} %copy.72.bucket_ref, ...), custom_call_target="tpu_custom_call" | custom-call | flops 230000000 | bytes 100000 | tf_op jit(solution)/shard_map/feed/pallas_call | solution.py:495
  232.9 35.6 %feed_back.1 = (f32[1024,1024]{1,0:T(8,128)}, bf16[1024,1024]{1,0:T(8,128)(2,1)}) custom-call(s32[4,9]{1,0:T(4,128)} %dynamic-slice_bitcast_fusion.table_ref, f32[1024,1024]{1,0:T(8,128)} %get-tuple-element.100.third_ref, bf16[4,1024,1024]{2,1,0:T(8,128)(2,1)} %get-tuple-element.101.slope_ref, bf16[1024,1024]{1,0:T(8,128)(2,1)} %get-tuple-element.102.normal_ref, ...), custom_call_target="tpu_custom_call" | custom-call | flops 230000000 | bytes 100000 | tf_op jit(solution)/shard_map/feed_back/pallas_call | solution.py:572
  268.4 39.4 %attend_back.2 = (bf16[1024,1024]{1,0:T(8,128)(2,1)}, bf16[1024,1024]{1,0:T(8,128)(2,1)}, bf16[1024,1024]{1,0:T(8,128)(2,1)}) custom-call(bf16[1,1024,1024]{2,1,0:T(8,128)(2,1)} %get-tuple-element.90.q_ref, bf16[2,1024,1024]{2,1,0:T(8,128)(2,1)} %project.3.refs_2_.k_ref.v_ref, bf16[2,1024,1024]{2,1,0:T(8,128)(2,1)} %project.3.refs_2_.k_ref.v_ref, ...), custom_call_target="tpu_custom_call" | custom-call | flops 230000000 | bytes 100000 | tf_op jit(solution)/shard_map/attend_back/pallas_call | solution.py:345
  307.8 19.5 %after_cross_back.1 = (bf16[1024,1024]{1,0:T(8,128)(2,1)}, f32[1024,1024]{1,0:T(8,128)}, bf16[1024,1024]{1,0:T(8,128)(2,1)}) custom-call(s32[4,9]{1,0:T(4,128)} %dynamic-slice_bitcast_fusion.table_ref, bf16[1024,1024]{1,0:T(8,128)(2,1)} %get-tuple-element.108.dq_ref, bf16[1024,1024]{1,0:T(8,128)(2,1)} %get-tuple-element.109.dk_ref, ...), custom_call_target="tpu_custom_call" | custom-call | flops 230000000 | bytes 100000 | tf_op jit(solution)/shard_map/after_cross_back/pallas_call | solution.py:633
  327.3 32.8 %attend_back.3 = (bf16[1024,1024]{1,0:T(8,128)(2,1)}, bf16[1024,1024]{1,0:T(8,128)(2,1)}, bf16[1024,1024]{1,0:T(8,128)(2,1)}) custom-call(bf16[3,1024,1024]{2,1,0:T(8,128)(2,1)} %project.2.refs_1_.refs_27_.q_ref.k_ref.v_ref, bf16[3,1024,1024]{2,1,0:T(8,128)(2,1)} %project.2.refs_1_.refs_27_.q_ref.k_ref.v_ref, ...), custom_call_target="tpu_custom_call" | custom-call | flops 230000000 | bytes 100000 | tf_op jit(solution)/shard_map/attend_back/pallas_call | solution.py:345
  360.2 12.6 %input_gradient.1 = bf16[1024,1024]{1,0:T(8,128)(2,1)} custom-call(s32[4,9]{1,0:T(4,128)} %dynamic-slice_bitcast_fusion.table_ref, bf16[1024,1024]{1,0:T(8,128)(2,1)} %get-tuple-element.116.dq_ref, bf16[1024,1024]{1,0:T(8,128)(2,1)} %get-tuple-element.117.dk_ref, bf16[1024,1024]{1,0:T(8,128)(2,1)} %get-tuple-element.118.dv_ref, ...), custom_call_target="tpu_custom_call" | custom-call | flops 230000000 | bytes 100000 | tf_op jit(solution)/shard_map/input_gradient/pallas_call | solution.py:671
  372.8 2.1 all-reduce.3.cloned.1.call-done
  374.9 12.0 %adamw.1 = (f32[1024,512]{1,0:T(8,128)}, f32[1024,512]{1,0:T(8,128)}, f32[1024,512]{1,0:T(8,128)}, f32[1024,512]{1,0:T(8,128)}, bf16[1024,512]{1,0:T(8,128)(2,1)...) custom-call(f32[1024,512]{1,0:T(8,128)} %refs_0_.5, ...), custom_call_target="tpu_custom_call" | custom-call | flops 11500000256 | bytes 100000 | tf_op jit(solution)/shard_map/adamw/pallas_call | solution.py:710
  (77 shorter events, 37.4 us)
Async XLA Ops:
  7.2 367.7 %all-reduce.3.cloned.1.call-start = ((), (), s32[]{:S(2)}) async-start(), calls=%async_computation | async-start | bytes 8388608 | tf_op jit(solution)/shard_map/psum | solution.py:937
  9.5 16.0 %collective-permute-start = (bf16[4,128,1024]{2,1,0:T(8,128)(2,1)}, bf16[4,128,1024]{2,1,0:T(8,128)(2,1)}, u32[]{:S(2)}, u32[]{:S(2)}) collective-permute-start(bf16[4,128,1024]{2,1,0:T(8,128)(2,1)} %pack.1.refs_0_.refs_9_.refs_18_), channel_id=1, source_target_pairs={{0,8},{1,5},{2,10},{3,7},{4,0},{5,13},{6,2},{7,15},{8,16},{9,1},{1... | collective-permute-start | bytes 3145736 | tf_op jit(solution)/shard_map/ppermute | solution.py:843
  16.0 15.1 %collective-permute-start.9 = (bf16[2,128,1024]{2,1,0:T(8,128)(2,1)}, bf16[2,128,1024]{2,1,0:T(8,128)(2,1)}, u32[]{:S(2)}, u32[]{:S(2)}) collective-permute-start(bf16[2,128,1024]{2,1,0:T(8,128)(2,1)} %get-tuple-element.73.refs_1_.refs_0_.refs_9_), channel_id=1, source_target_pairs={{0,8},{1,5},{2,10},{3,7},{4,0},{5,13},{6,2},{7,15},{8,16},{9,1},{1... | collective-permute-start | bytes 1572872 | tf_op jit(solution)/shard_map/ppermute | solution.py:843
  26.0 18.6 %collective-permute-start.1 = (bf16[4,128,1024]{2,1,0:T(8,128)(2,1)}, bf16[4,128,1024]{2,1,0:T(8,128)(2,1)}, u32[]{:S(2)}, u32[]{:S(2)}) collective-permute-start(bf16[4,128,1024]{2,1,0:T(8,128)(2,1)} %get-tuple-element.74.refs_1_.refs_10_.refs_19_), channel_id=1, source_target_pairs={{0,1},{1,0},{2,3},{3,2},{4,5},{5,4},{6,7},{7,6},{8,9},{9,8},{10,11... | collective-permute-start | bytes 3145736 | tf_op jit(solution)/shard_map/ppermute | solution.py:843
  26.1 18.5 %collective-permute-start.2 = (bf16[4,128,1024]{2,1,0:T(8,128)(2,1)}, bf16[4,128,1024]{2,1,0:T(8,128)(2,1)}, u32[]{:S(2)}, u32[]{:S(2)}) collective-permute-start(bf16[4,128,1024]{2,1,0:T(8,128)(2,1)} %get-tuple-element.74.refs_1_.refs_10_.refs_19_), channel_id=1, source_target_pairs={{0,8},{1,5},{2,10},{3,7},{4,0},{5,13},{6,2},{7,15},{8,16},{9,1},{1... | collective-permute-start | bytes 3145736 | tf_op jit(solution)/shard_map/ppermute | solution.py:843
  31.1 13.5 %collective-permute-start.12 = (bf16[2,128,1024]{2,1,0:T(8,128)(2,1)}, bf16[2,128,1024]{2,1,0:T(8,128)(2,1)}, u32[]{:S(2)}, u32[]{:S(2)}) collective-permute-start(bf16[2,128,1024]{2,1,0:T(8,128)(2,1)} %collective-permute-done.9.refs_1_.refs_10_), channel_id=1, source_target_pairs={{0,2},{1,3},{2,0},{3,1},{4,6},{5,7},{6,4},{7,5},{8,10},{9,11},{10,... | collective-permute-start | bytes 1572872 | tf_op jit(solution)/shard_map/ppermute | solution.py:843
  33.2 14.3 %collective-permute-start.10 = (bf16[2,128,1024]{2,1,0:T(8,128)(2,1)}, bf16[2,128,1024]{2,1,0:T(8,128)(2,1)S(1)}, u32[]{:S(2)}, u32[]{:S(2)}) collective-permute-start(bf16[2,128,1024]{2,1,0:T(8,128)(2,1)} %collective-permute-done.9.refs_1_.refs_10_), channel_id=1, source_target_pairs={{0,1},{1,0},{2,3},{3,2},{4,5},{5,4},{6,7},{7,6},{8,9},{9,8},{10,11... | collective-permute-start | bytes 1572872 | tf_op jit(solution)/shard_map/ppermute | solution.py:843
  33.2 14.8 %collective-permute-start.11 = (bf16[2,128,1024]{2,1,0:T(8,128)(2,1)}, bf16[2,128,1024]{2,1,0:T(8,128)(2,1)}, u32[]{:S(2)}, u32[]{:S(2)}) collective-permute-start(bf16[2,128,1024]{2,1,0:T(8,128)(2,1)} %collective-permute-done.9.refs_1_.refs_10_), channel_id=1, source_target_pairs={{0,8},{1,5},{2,10},{3,7},{4,0},{5,13},{6,2},{7,15},{8,16},{9,1},{1... | collective-permute-start | bytes 1572872 | tf_op jit(solution)/shard_map/ppermute | solution.py:843
  44.6 3.4 collective-permute-start.13
  45.1 17.6 %collective-permute-start.3 = (bf16[4,128,1024]{2,1,0:T(8,128)(2,1)}, bf16[4,128,1024]{2,1,0:T(8,128)(2,1)}, u32[]{:S(2)}, u32[]{:S(2)}) collective-permute-start(bf16[4,128,1024]{2,1,0:T(8,128)(2,1)} %get-tuple-element.75.refs_3_.refs_12_.refs_21_), channel_id=1, source_target_pairs={{0,1},{1,0},{2,3},{3,2},{4,5},{5,4},{6,7},{7,6},{8,9},{9,8},{10,11... | collective-permute-start | bytes 3145736 | tf_op jit(solution)/shard_map/ppermute | solution.py:843
  45.7 17.0 %collective-permute-start.4 = (bf16[4,128,1024]{2,1,0:T(8,128)(2,1)}, bf16[4,128,1024]{2,1,0:T(8,128)(2,1)}, u32[]{:S(2)}, u32[]{:S(2)}) collective-permute-start(bf16[4,128,1024]{2,1,0:T(8,128)(2,1)} %get-tuple-element.75.refs_3_.refs_12_.refs_21_), channel_id=1, source_target_pairs={{0,8},{1,5},{2,10},{3,7},{4,0},{5,13},{6,2},{7,15},{8,16},{9,1},{1... | collective-permute-start | bytes 3145736 | tf_op jit(solution)/shard_map/ppermute | solution.py:843
  48.8 13.9 %collective-permute-start.16 = (bf16[2,128,1024]{2,1,0:T(8,128)(2,1)}, bf16[2,128,1024]{2,1,0:T(8,128)(2,1)}, u32[]{:S(2)}, u32[]{:S(2)}) collective-permute-start(bf16[2,128,1024]{2,1,0:T(8,128)(2,1)} %get-tuple-element.78.refs_3_.refs_12_), channel_id=1, source_target_pairs={{0,2},{1,3},{2,0},{3,1},{4,6},{5,7},{6,4},{7,5},{8,10},{9,11},{10,... | collective-permute-start | bytes 1572872 | tf_op jit(solution)/shard_map/ppermute | solution.py:843
  50.6 16.3 %collective-permute-start.14 = (bf16[2,128,1024]{2,1,0:T(8,128)(2,1)}, bf16[2,128,1024]{2,1,0:T(8,128)(2,1)}, u32[]{:S(2)}, u32[]{:S(2)}) collective-permute-start(bf16[2,128,1024]{2,1,0:T(8,128)(2,1)} %get-tuple-element.78.refs_3_.refs_12_), channel_id=1, source_target_pairs={{0,1},{1,0},{2,3},{3,2},{4,5},{5,4},{6,7},{7,6},{8,9},{9,8},{10,11... | collective-permute-start | bytes 1572872 | tf_op jit(solution)/shard_map/ppermute | solution.py:843
  50.6 16.3 %collective-permute-start.15 = (bf16[2,128,1024]{2,1,0:T(8,128)(2,1)}, bf16[2,128,1024]{2,1,0:T(8,128)(2,1)S(1)}, u32[]{:S(2)}, u32[]{:S(2)}) collective-permute-start(bf16[2,128,1024]{2,1,0:T(8,128)(2,1)} %get-tuple-element.78.refs_3_.refs_12_), channel_id=1, source_target_pairs={{0,8},{1,5},{2,10},{3,7},{4,0},{5,13},{6,2},{7,15},{8,16},{9,1},{1... | collective-permute-start | bytes 1572872 | tf_op jit(solution)/shard_map/ppermute | solution.py:843
  62.7 4.2 %collective-permute-start.17 = (bf16[2,128,1024]{2,1,0:T(8,128)(2,1)}, bf16[2,128,1024]{2,1,0:T(8,128)(2,1)}, u32[]{:S(2)}, u32[]{:S(2)}) collective-permute-start(bf16[2,128,1024]{2,1,0:T(8,128)(2,1)} %collective-permute-done.16.refs_21_), channel_id=1, source_target_pairs={{0,1},{1,0},{2,3},{3,2},{4,5},{5,4},{6,7},{7,6},{8,9},{9,8},{10,11... | collective-permute-start | bytes 1572872 | tf_op jit(solution)/shard_map/ppermute | solution.py:843
  65.1 9.5 %collective-permute-start.6 = (bf16[4,64,1024]{2,1,0:T(8,128)(2,1)}, bf16[4,64,1024]{2,1,0:T(8,128)(2,1)}, u32[]{:S(2)}, u32[]{:S(2)}) collective-permute-start(bf16[4,64,1024]{2,1,0:T(8,128)(2,1)} %constant_dynamic-slice_fusion.2), channel_id=1, source_target_pairs={{0,8},{1,5},{2,10},{3,7},{4,0},{5,13},{6,2},{7,15},{8,16},{9,1},{1... | collective-permute-start | bytes 1572872 | tf_op jit(solution)/shard_map/ppermute | solution.py:843
  66.2 18.3 %collective-permute-start.5 = (bf16[4,128,1024]{2,1,0:T(8,128)(2,1)}, bf16[4,128,1024]{2,1,0:T(8,128)(2,1)}, u32[]{:S(2)}, u32[]{:S(2)}) collective-permute-start(bf16[4,128,1024]{2,1,0:T(8,128)(2,1)} %get-tuple-element.76.refs_5_.refs_14_.refs_23_), channel_id=1, source_target_pairs={{0,1},{1,0},{2,3},{3,2},{4,5},{5,4},{6,7},{7,6},{8,9},{9,8},{10,11... | collective-permute-start | bytes 3145736 | tf_op jit(solution)/shard_map/ppermute | solution.py:843
  68.2 14.4 %collective-permute-start.21 = (bf16[2,128,1024]{2,1,0:T(8,128)(2,1)}, bf16[2,128,1024]{2,1,0:T(8,128)(2,1)S(1)}, u32[]{:S(2)}, u32[]{:S(2)}) collective-permute-start(bf16[2,128,1024]{2,1,0:T(8,128)(2,1)} %get-tuple-element.79.refs_5_.refs_14_), channel_id=1, source_target_pairs={{0,2},{1,3},{2,0},{3,1},{4,6},{5,7},{6,4},{7,5},{8,10},{9,11},{10,... | collective-permute-start | bytes 1572872 | tf_op jit(solution)/shard_map/ppermute | solution.py:843
  74.6 9.6 %collective-permute-start.7 = (bf16[4,64,1024]{2,1,0:T(8,128)(2,1)}, bf16[4,64,1024]{2,1,0:T(8,128)(2,1)}, u32[]{:S(2)}, u32[]{:S(2)}) collective-permute-start(bf16[4,64,1024]{2,1,0:T(8,128)(2,1)} %collective-permute-done.6.refs_1_.refs_7_.refs_16_.refs_25_), channel_id=1, source_target_pairs={{0,1},{1,0},{2,3},{3,2},{4,5},{5,4},{6,7},{7,6},{8,9},{9,8},{10,11... | collective-permute-start | bytes 1572872 | tf_op jit(solution)/shard_map/ppermute | solution.py:843
  75.6 6.5 %collective-permute-start.19 = (bf16[2,64,1024]{2,1,0:T(8,128)(2,1)S(1)}, bf16[2,64,1024]{2,1,0:T(8,128)(2,1)}, u32[]{:S(2)}, u32[]{:S(2)}) collective-permute-start(bf16[2,64,1024]{2,1,0:T(8,128)(2,1)S(1)} %constant_dynamic-slice_fusion.1), channel_id=1, source_target_pairs={{0,8},{1,5},{2,10},{3,7},{4,0},{5,13},{6,2},{7,15},{8,16},{9,1},{1... | collective-permute-start | bytes 786440 | tf_op jit(solution)/shard_map/ppermute | solution.py:843
  76.7 22.2 %collective-permute-start.18 = (bf16[2,128,1024]{2,1,0:T(8,128)(2,1)}, bf16[2,128,1024]{2,1,0:T(8,128)(2,1)}, u32[]{:S(2)}, u32[]{:S(2)}) collective-permute-start(bf16[2,128,1024]{2,1,0:T(8,128)(2,1)} %get-tuple-element.79.refs_5_.refs_14_), channel_id=1, source_target_pairs={{0,1},{1,0},{2,3},{3,2},{4,5},{5,4},{6,7},{7,6},{8,9},{9,8},{10,11... | collective-permute-start | bytes 1572872 | tf_op jit(solution)/shard_map/ppermute | solution.py:843
  82.1 16.8 %collective-permute-start.20 = (bf16[2,64,1024]{2,1,0:T(8,128)(2,1)}, bf16[2,64,1024]{2,1,0:T(8,128)(2,1)}, u32[]{:S(2)}, u32[]{:S(2)}) collective-permute-start(bf16[2,64,1024]{2,1,0:T(8,128)(2,1)} %collective-permute-done.19.refs_7_.refs_16_), channel_id=1, source_target_pairs={{0,1},{1,0},{2,3},{3,2},{4,5},{5,4},{6,7},{7,6},{8,9},{9,8},{10,11... | collective-permute-start | bytes 786440 | tf_op jit(solution)/shard_map/ppermute | solution.py:843
  82.7 14.5 %collective-permute-start.23 = (bf16[2,64,1024]{2,1,0:T(8,128)(2,1)}, bf16[2,64,1024]{2,1,0:T(8,128)(2,1)S(1)}, u32[]{:S(2)}, u32[]{:S(2)}) collective-permute-start(bf16[2,64,1024]{2,1,0:T(8,128)(2,1)} %collective-permute-done.19.refs_7_.refs_16_), channel_id=1, source_target_pairs={{0,2},{1,3},{2,0},{3,1},{4,6},{5,7},{6,4},{7,5},{8,10},{9,11},{10,... | collective-permute-start | bytes 786440 | tf_op jit(solution)/shard_map/ppermute | solution.py:843
  84.2 14.7 %collective-permute-start.22 = (bf16[2,128,1024]{2,1,0:T(8,128)(2,1)S(1)}, bf16[2,128,1024]{2,1,0:T(8,128)(2,1)}, u32[]{:S(2)}, u32[]{:S(2)}) collective-permute-start(bf16[2,128,1024]{2,1,0:T(8,128)(2,1)S(1)} %collective-permute-done.21.refs_23_), channel_id=1, source_target_pairs={{0,1},{1,0},{2,3},{3,2},{4,5},{5,4},{6,7},{7,6},{8,9},{9,8},{10,11... | collective-permute-start | bytes 1572872 | tf_op jit(solution)/shard_map/ppermute | solution.py:843
  84.5 26.4 %collective-permute-start.8 = (bf16[8,128,1024]{2,1,0:T(8,128)(2,1)}, bf16[8,128,1024]{2,1,0:T(8,128)(2,1)}, u32[]{:S(2)}, u32[]{:S(2)}) collective-permute-start(bf16[8,128,1024]{2,1,0:T(8,128)(2,1)} %get-tuple-element.77.refs_27_), channel_id=1, source_target_pairs={{0,8},{1,5},{2,10},{3,7},{4,0},{5,13},{6,2},{7,15},{8,16},{9,1},{1... | collective-permute-start | bytes 6291464 | tf_op jit(solution)/shard_map/ppermute | solution.py:843
  111.4 26.6 %collective-permute-start.25 = (bf16[8,128,1024]{2,1,0:T(8,128)(2,1)}, bf16[8,128,1024]{2,1,0:T(8,128)(2,1)}, u32[]{:S(2)}, u32[]{:S(2)}) collective-permute-start(bf16[8,128,1024]{2,1,0:T(8,128)(2,1)} %get-tuple-element.82.refs_0_.refs_28_), channel_id=1, source_target_pairs={{0,8},{1,5},{2,10},{3,7},{4,0},{5,13},{6,2},{7,15},{8,16},{9,1},{1... | collective-permute-start | bytes 6291464 | tf_op jit(solution)/shard_map/ppermute | solution.py:843
  138.5 26.7 %collective-permute-start.26 = (bf16[8,128,1024]{2,1,0:T(8,128)(2,1)}, bf16[8,128,1024]{2,1,0:T(8,128)(2,1)}, u32[]{:S(2)}, u32[]{:S(2)}) collective-permute-start(bf16[8,128,1024]{2,1,0:T(8,128)(2,1)} %get-tuple-element.88.refs_27_.refs_30_), channel_id=1, source_target_pairs={{0,8},{1,5},{2,10},{3,7},{4,0},{5,13},{6,2},{7,15},{8,16},{9,1},{1... | collective-permute-start | bytes 6291464 | tf_op jit(solution)/shard_map/ppermute | solution.py:843
  167.9 15.6 %collective-permute-start.30 = (bf16[8,64,1024]{2,1,0:T(8,128)(2,1)}, bf16[8,64,1024]{2,1,0:T(8,128)(2,1)}, u32[]{:S(2)}, u32[]{:S(2)}) collective-permute-start(bf16[8,64,1024]{2,1,0:T(8,128)(2,1)} %constant_dynamic-slice_fusion), channel_id=1, source_target_pairs={{0,8},{1,5},{2,10},{3,7},{4,0},{5,13},{6,2},{7,15},{8,16},{9,1},{1... | collective-permute-start | bytes 3145736 | tf_op jit(solution)/shard_map/ppermute | solution.py:843
  169.5 14.6 %collective-permute-start.27 = (bf16[8,128,1024]{2,1,0:T(8,128)(2,1)}, bf16[8,128,1024]{2,1,0:T(8,128)(2,1)}, u32[]{:S(2)}, u32[]{:S(2)}) collective-permute-start(bf16[8,128,1024]{2,1,0:T(8,128)(2,1)} %get-tuple-element.82.refs_0_.refs_28_), channel_id=1, source_target_pairs={{0,1},{1,0},{2,3},{3,2},{4,5},{5,4},{6,7},{7,6},{8,9},{9,8},{10,11... | collective-permute-start | bytes 6291464 | tf_op jit(solution)/shard_map/ppermute | solution.py:843
  169.5 14.6 %collective-permute-start.28 = (bf16[8,128,1024]{2,1,0:T(8,128)(2,1)}, bf16[8,128,1024]{2,1,0:T(8,128)(2,1)}, u32[]{:S(2)}, u32[]{:S(2)}) collective-permute-start(bf16[8,128,1024]{2,1,0:T(8,128)(2,1)} %get-tuple-element.88.refs_27_.refs_30_), channel_id=1, source_target_pairs={{0,1},{1,0},{2,3},{3,2},{4,5},{5,4},{6,7},{7,6},{8,9},{9,8},{10,11... | collective-permute-start | bytes 6291464 | tf_op jit(solution)/shard_map/ppermute | solution.py:843
  170.0 17.1 %collective-permute-start.29 = (bf16[8,128,1024]{2,1,0:T(8,128)(2,1)}, bf16[8,128,1024]{2,1,0:T(8,128)(2,1)}, u32[]{:S(2)}, u32[]{:S(2)}) collective-permute-start(bf16[8,128,1024]{2,1,0:T(8,128)(2,1)} %get-tuple-element.95.refs_3_.refs_32_), channel_id=1, source_target_pairs={{0,1},{1,0},{2,3},{3,2},{4,5},{5,4},{6,7},{7,6},{8,9},{9,8},{10,11... | collective-permute-start | bytes 6291464 | tf_op jit(solution)/shard_map/ppermute | solution.py:843
  184.0 3.1 collective-permute-start.31
  (6 other events, 19.4 us)
Sparse Core Ops, SparseCore 0:
  233.0 141.8 all-reduce.2

commit v2 on v1

--- a/solution.py
+++ b/solution.py
@@ -21,7 +21,8 @@
 epsilon_adam = 1e-08
 
 f32, bf16 = jnp.float32, jnp.bfloat16
-query_scale = HEAD_DIM ** (-0.5) * math.log2(math.e)
+query_scale = HEAD_DIM ** (-0.5)
+log2_e = math.log2(math.e)
 forbidden = -(2.0**100)
 least_sum, most_sum = 2.0**-40, 2.0**60
 
@@ -176,7 +177,7 @@
 def attend_kernel(
     causal, bucket_ref, lengths_ref, q_ref, k_ref, v_ref, *refs
 ):
-    out_ref, weight_ref, share_ref, done_ref, qmark, kmark = refs[-6:]
+    out_ref, rest_ref, weight_ref, share_ref, done_ref, qmark, kmark = refs[-7:]
     done_ref[...] = jnp.zeros_like(done_ref)
     tokens = q_ref.shape[-2]
     low = low_half(tokens)
@@ -205,7 +206,9 @@
         out = jnp.concatenate(
             [even[:HEAD_DIM] * even_share[:1], odd[HEAD_DIM:] * odd_share[:1]], axis=0
         )
-        out_ref[...] = out.astype(bf16).T
+        high = out.astype(bf16)
+        out_ref[...] = high.T
+        rest_ref[...] = (out - high.astype(f32)).astype(bf16).T
         share_ref[0, 0:1] = even_share[:1]
         share_ref[0, 1:2] = odd_share[:1]
         return even[HEAD_DIM : HEAD_DIM + 1], odd[:1]
@@ -215,7 +218,7 @@
         for head in range(2):
             queries, keys, values = operands(head)
             if not causal:
-                weight = jnp.exp2(contract(keys, queries, 1, 1)).astype(bf16)
+                weight = jnp.exp2(contract(keys, queries, 1, 1) * log2_e).astype(bf16)
                 weight_ref[head] = weight
                 sums.append(contract(values, weight, 0, 0))
                 continue
@@ -224,13 +227,13 @@
                 jnp.int32, (step, step), 1
             )
             nothing = jnp.zeros((), bf16)
-            top = jnp.exp2(contract(keys[:step], queries, 1, 1)).astype(bf16)
+            top = jnp.exp2(contract(keys[:step], queries, 1, 1) * log2_e).astype(bf16)
             top = jnp.concatenate(
                 [jnp.where(before, top[:, :step], nothing), top[:, step:]], axis=1
             )
             weight_ref[head, :step] = top
             total = contract(values[:step], top, 0, 0)
-            low_part = jnp.exp2(contract(keys[step:], queries[step:], 1, 1)).astype(bf16)
+            low_part = jnp.exp2(contract(keys[step:], queries[step:], 1, 1) * log2_e).astype(bf16)
             low_part = jnp.where(before, low_part, nothing)
             weight_ref[head, step:, step:] = low_part
             rest = contract(values[step:], low_part, 0, 0)
@@ -252,7 +255,7 @@
                 ) <= lax.broadcasted_iota(jnp.int32, scores.shape, 1)
                 scores = jnp.where(before, scores, forbidden)
             scores = scores - jnp.max(scores, axis=0, keepdims=True)
-            weight = jnp.exp2(scores).astype(bf16)
+            weight = jnp.exp2(scores * log2_e).astype(bf16)
             weight_ref[head] = weight
             sums.append(contract(values, weight, 0, 0))
         finish(sums)
@@ -271,11 +274,13 @@
         + [in_place() for array in (*so_far, *sooner)],
         out_specs=[
             flat_spec,
+            flat_spec,
             pl.BlockSpec((2, tokens, tokens), lambda j: (start + j, 0, 0)),
             pl.BlockSpec((1, 2, tokens), lambda j: (start + j, 0, 0)),
             pl.BlockSpec((8, PAIR), lambda j: (0, 0)),
         ],
         out_shape=[
+            jax.ShapeDtypeStruct((tokens, width), bf16),
             jax.ShapeDtypeStruct((tokens, width), bf16),
             jax.ShapeDtypeStruct((2 * pairs, tokens, tokens), bf16),
             jax.ShapeDtypeStruct((pairs, 2, tokens), f32),
@@ -290,7 +295,7 @@
 
 
 def attend_back_kernel(
-    causal, q_ref, k_ref, v_ref, grad_ref, out_ref, weight_ref, dq_ref, dk_ref, dv_ref
+    causal, q_ref, k_ref, v_ref, grad_ref, out_ref, rest_ref, weight_ref, dq_ref, dk_ref, dv_ref
 ):
     tokens = q_ref.shape[-2]
     low = low_half(tokens)
@@ -301,7 +306,7 @@
         (lax.broadcasted_iota(jnp.int32, (PAIR, PAIR), 0) < HEAD_DIM)
         != (lax.broadcasted_iota(jnp.int32, (PAIR, PAIR), 1) < HEAD_DIM)
     ).astype(bf16)
-    product = grad.astype(f32) * out_ref[...].astype(f32)
+    product = grad.astype(f32) * (out_ref[...].astype(f32) + rest_ref[...].astype(f32))
     high = product.astype(bf16)
     centre = contract(high, swap, 1, 0) + contract((product - high.astype(f32)).astype(bf16), swap, 1, 0)
     high = centre.astype(bf16)
@@ -327,7 +332,7 @@
             dk = dk_own if head == 0 else dk + dk_own
             turned.append(contract(k[rows], dscore, 0, 0)[head * HEAD_DIM : (head + 1) * HEAD_DIM])
         dv_ref[rows] = dv.astype(bf16)
-        dk_ref[rows] = (dk * math.log(2.0)).astype(bf16)
+        dk_ref[rows] = dk.astype(bf16)
         turned = jnp.concatenate(turned, axis=0)
         if tile == 0:
             dq_turned = turned
@@ -336,7 +341,7 @@
     dq_ref[...] = (dq_turned * HEAD_DIM ** (-0.5)).T.astype(bf16)
 
 
-def attend_back(q_pack, k_pack, v_pack, grad, out, weight, causal):
+def attend_back(q_pack, k_pack, v_pack, grad, out, rest, weight, causal):
     (q, q_at), (k, k_at), (v, v_at) = q_pack, k_pack, v_pack
     tokens, width = q.shape[1:]
     pairs = width // PAIR
@@ -351,6 +356,7 @@
             pair_spec(v_at),
             flat_spec,
             flat_spec,
+            flat_spec,
             pl.BlockSpec((2, tokens, tokens), lambda j: (j, 0, 0)),
         ],
         out_specs=[flat_spec] * 3,
@@ -358,7 +364,7 @@
         compiler_params=params,
         cost_estimate=cost(0.2),
         name="attend_back",
-    )(q, k, v, grad, out, weight)
+    )(q, k, v, grad, out, rest, weight)
 
 
 def first_kernel(wanted, count, table_ref, x_ref, out_ref, gains_ref, *refs):
@@ -915,7 +921,7 @@
     half = width // PAIR // 2
     late.hop(qkv, kv)
     *self_half, done = attend(buckets, lengths, *self_packs, True, 0, half, (), (late.shared,))
-    self_out, self_weight, self_share, done = attend(
+    self_out, self_rest, self_weight, self_share, done = attend(
         buckets, lengths, *self_packs, True, half, 2 * half, self_half
     )
     late.hop(done)
@@ -925,7 +931,7 @@
     cross_packs = [(query_cross, 0), (kv, 0), (kv, 1)]
     *cross_half, done = attend(buckets, lengths, *cross_packs, False, 0, half)
     late.hop(done)
-    cross_out, cross_weight, cross_share, done = attend(
+    cross_out, cross_rest, cross_weight, cross_share, done = attend(
         buckets, lengths, *cross_packs, False, half, 2 * half, cross_half, (late.shared,)
     )
     late.share(done)
@@ -940,11 +946,11 @@
         table, grad_third, slope, second_normal, second_inverse, adapter, cross_share, norm_gains, down_master,
         pieces, co, late.pieces,
     )
-    dq, dk, dv = attend_back(*cross_packs, grad_cross_out, cross_out, cross_weight, False)
+    dq, dk, dv = attend_back(*cross_packs, grad_cross_out, cross_out, cross_rest, cross_weight, False)
     encoder_grad, grad_self_pre, grad_self_out = after_cross_back(
         dq, dk, dv, grad_cross_pre, first, first_inverse, self_share, norm_gains, table, pieces, (cq, ck, cv, so)
     )
-    dq, dk, dv = attend_back(*self_packs, grad_self_out, self_out, self_weight, True)
+    dq, dk, dv = attend_back(*self_packs, grad_self_out, self_out, self_rest, self_weight, True)
     input_grad = input_gradient(dq, dk, dv, grad_self_pre, table, pieces, (sq, sk, sv))
 
     (

time: 401 us -> 401 us (level)
  transfers between devices with their start and end apart: 33 -> 33, of which waited for: 14 -> 14; matrix products, arithmetic and copies ran while one was open for 1% -> 1% of each run, Pallas kernels for 57% -> 58%
where the time goes in v2:
time: 401 us; the launch traced here: 394 us
  Pallas kernels  291 us (73%)
  waiting for transfers between devices  49.5 us (12%)
  starting transfers between devices  29.8 us (7%)
  between operations  15.4 us (4%)
  local copies, waits for them, and re-layouts  8.94 us (2%)
    pallas_call x2, Pallas kernels, attend_back(): pl.pallas_call(functools.partial(attend_back_kernel, causal), grid=(pairs...  72.4 us
    pallas_call x4, Pallas kernels, attend(): pl.pallas_call(functools.partial(attend_kernel, causal), grid=(stop - sta...  48.1 us
    ppermute x32, waiting for transfers between devices, send(): return lax.ppermute(values, AXES, pairs)  47.5 us
    pallas_call x1, Pallas kernels, feed(): pl.pallas_call(functools.partial(feed_kernel, (output_at,), len(feed_piec...  45.7 us
    pallas_call x1, Pallas kernels, feed_back(): pl.pallas_call(functools.partial(feed_back_kernel, (output_at,), len(feed...  35.6 us
    ppermute x32, starting transfers between devices, send(): return lax.ppermute(values, AXES, pairs)  29.8 us
    pallas_call x2, Pallas kernels, project(): pl.pallas_call(functools.partial(project_kernel, wanted, scale, len(piece...  20.7 us
    pallas_call x1, Pallas kernels, after_cross_back(): pl.pallas_call(functools.partial(cross_back_kernel, wanted), grid=(tokens...  19.5 us
  transfers between devices with their start and end apart: 33, of which 14 were waited for; matrix products, arithmetic and copies ran while one was open for 1% of the time, Pallas kernels for 58%

profile of v2, /device:TPU:0, one launch (start us, length us, event | category | flops | bytes accessed | tf_op | source)
XLA Modules:
  0.0 394.2 jit_solution(6005567565246037025)
XLA Ops:
  7.2 2.2 pack.1.refs_0_.refs_9_.refs_18_
  9.5 3.0 collective-permute-start
  13.7 2.3 pack_pair.1
  17.6 3.0 pack_feed.1.refs_2_.refs_0_
  20.6 4.9 %collective-permute-done.refs_0_ = bf16[4,128,1024]{2,1,0:T(8,128)(2,1)} collective-permute-done((bf16[4,128,1024]{2,1,0:T(8,128)(2,1)}, bf16[4,128,1024]{2,1,0:T(8,128)(2,1)}, u32[]{:S(2)}, u32[]{:S(2)}) %collective-permute-start) | collective-permute-done | bytes 1048608 | tf_op jit(solution)/shard_map/ppermute | solution.py:849
  26.1 2.2 collective-permute-start.2
  28.2 2.9 collective-permute-done.9.refs_1_.refs_10_
  31.1 2.1 collective-permute-start.12
  34.7 9.9 %collective-permute-done.12.refs_19_ = bf16[2,128,1024]{2,1,0:T(8,128)(2,1)} collective-permute-done((bf16[2,128,1024]{2,1,0:T(8,128)(2,1)}, bf16[2,128,1024]{2,1,0:T(8,128)(2,1)}, u32[]{:S(2)}, u32[]{:S(2)}) %collective-permute-start.12) | collective-permute-done | bytes 524320 | tf_op jit(solution)/shard_map/ppermute | solution.py:849
  48.8 1.8 collective-permute-start.16
  52.2 10.5 %collective-permute-done.16.refs_21_ = bf16[2,128,1024]{2,1,0:T(8,128)(2,1)} collective-permute-done((bf16[2,128,1024]{2,1,0:T(8,128)(2,1)}, bf16[2,128,1024]{2,1,0:T(8,128)(2,1)}, u32[]{:S(2)}, u32[]{:S(2)}) %collective-permute-start.16) | collective-permute-done | bytes 524320 | tf_op jit(solution)/shard_map/ppermute | solution.py:849
  63.2 1.9 constant_dynamic-slice_fusion.2
  69.9 4.7 %collective-permute-done.6.refs_1_.refs_7_.refs_16_.refs_25_ = bf16[4,64,1024]{2,1,0:T(8,128)(2,1)} collective-permute-done((bf16[4,64,1024]{2,1,0:T(8,128)(2,1)}, bf16[4,64,1024]{2,1,0:T(8,128)(2,1)}, u32[]{:S(2)}, u32[]{:S(2)}) %collective-permute-start.6) | collective-permute-done | bytes 524320 | tf_op jit(solution)/shard_map/ppermute | solution.py:849
  77.4 4.7 %collective-permute-done.19.refs_7_.refs_16_ = bf16[2,64,1024]{2,1,0:T(8,128)(2,1)} collective-permute-done((bf16[2,64,1024]{2,1,0:T(8,128)(2,1)S(1)}, bf16[2,64,1024]{2,1,0:T(8,128)(2,1)}, u32[]{:S(2)}, u32[]{:S(2)}) %collective-permute-start.19) | collective-permute-done | bytes 262176 | tf_op jit(solution)/shard_map/ppermute | solution.py:849
  85.6 11.5 %project.2.refs_1_.refs_27_.q_ref.k_ref.v_ref = bf16[3,1024,1024]{2,1,0:T(8,128)(2,1)} custom-call(bf16[1024,1024]{1,0:T(8,128)(2,1)} %x_ref.5, s32[4,9]{1,0:T(4,128)} %dynamic-slice_bitcast_fusion.table_ref, bf16[4,128,1024]{2,1,0:T(8,128)(2,1)} %pack.1.refs_0_.refs_9_.refs_18_, bf16[4,128,1024]{2,1,0:T(8,128)(2,1)} %get-tuple-element.78.refs_1_.refs_10_.refs_19_, ...), custom_call_target="tpu_custom_call" | custom-call | flops 13799999488 | bytes 100000 | tf_op jit(solution)/shard_map/project/pallas_call | solution.py:142
  101.0 9.2 %project.3.refs_2_.k_ref.v_ref = bf16[2,1024,1024]{2,1,0:T(8,128)(2,1)} custom-call(bf16[1024,1024]{1,0:T(8,128)(2,1)} %x_ref.4, s32[4,9]{1,0:T(4,128)} %dynamic-slice_bitcast_fusion.table_ref, bf16[2,128,1024]{2,1,0:T(8,128)(2,1)} %get-tuple-element.77.refs_1_.refs_0_.refs_9_, bf16[2,128,1024]{2,1,0:T(8,128)(2,1)} %collective-permute-done.9.refs_1_.refs_10_, ...), custom_call_target="tpu_custom_call" | custom-call | flops 9200000000 | bytes 100000 | tf_op jit(solution)/shard_map/project/pallas_call | solution.py:142
  113.4 12.0 %attend.4 = (bf16[1024,1024]{1,0:T(8,128)(2,1)}, bf16[1024,1024]{1,0:T(8,128)(2,1)}, bf16[16,1024,1024]{2,1,0:T(8,128)(2,1)}, f32[8,2,1024]{2,1,0:T(2,128)}, f32[8,128]{1,0:T(8,128)}) custom-call(s32[1]{0:T(128)S(6)} %copy.76.bucket_ref, s32[1,4]{1,0:T(1,128)} %lengths_ref.9, bf16[3,1024,1024]{2,1,0:T(8,128)(2,1)} %project.2.refs_1_.refs_27_.q_ref.k_ref.v_ref, ...), custom_call_target="tpu_custom_call" | custom-call | flops 230000000 | bytes 100000 | tf_op jit(solution)/shard_map/attend/pallas_call | solution.py:270
  125.3 12.0 %attend.5 = (bf16[1024,1024]{1,0:T(8,128)(2,1)}, bf16[1024,1024]{1,0:T(8,128)(2,1)}, bf16[16,1024,1024]{2,1,0:T(8,128)(2,1)}, f32[8,2,1024]{2,1,0:T(2,128)}, f32[8,128]{1,0:T(8,128)}) custom-call(s32[1]{0:T(128)S(6)} %copy.76.bucket_ref, s32[1,4]{1,0:T(1,128)} %lengths_ref.9, ...), custom_call_target="tpu_custom_call", output_to_operand_aliasing={{0}: (5, {}), {1}: (6, {}), {2}: (7, {}), {3}: (8, {})} | custom-call | flops 230000000 | bytes 100000 | tf_op jit(solution)/shard_map/attend/pallas_call | solution.py:270
  139.9 10.7 %after_self.1 = (f32[1024,1024]{1,0:T(8,128)}, f32[1024,128]{1,0:T(8,128)}, bf16[1,1024,1024]{2,1,0:T(8,128)(2,1)}) custom-call(s32[4,9]{1,0:T(4,128)} %dynamic-slice_bitcast_fusion.table_ref, bf16[1024,1024]{1,0:T(8,128)(2,1)} %x_ref.5, bf16[1024,1024]{1,0:T(8,128)(2,1)} %get-tuple-element.91.out_ref, f32[3,1024]{1,0:T(4,128)} %gains_ref.7, ...), custom_call_target="tpu_custom_call" | custom-call | flops 230000000 | bytes 100000 | tf_op jit(solution)/shard_map/after_self/pallas_call | solution.py:394
  150.6 12.1 %attend.6 = (bf16[1024,1024]{1,0:T(8,128)(2,1)}, bf16[1024,1024]{1,0:T(8,128)(2,1)}, bf16[16,1024,1024]{2,1,0:T(8,128)(2,1)}, f32[8,2,1024]{2,1,0:T(2,128)}, f32[8,128]{1,0:T(8,128)}) custom-call(s32[1]{0:T(128)S(6)} %copy.76.bucket_ref, s32[1,4]{1,0:T(1,128)} %lengths_ref.9, bf16[1,1024,1024]{2,1,0:T(8,128)(2,1)} %get-tuple-element.95.q_ref, ...), custom_call_target="tpu_custom_call" | custom-call | flops 230000000 | bytes 100000 | tf_op jit(solution)/shard_map/attend/pallas_call | solution.py:270
  162.6 2.5 collective-permute-done.26.refs_0_
  165.7 2.3 constant_dynamic-slice_fusion
  170.0 12.1 %attend.7 = (bf16[1024,1024]{1,0:T(8,128)(2,1)}, bf16[1024,1024]{1,0:T(8,128)(2,1)}, bf16[16,1024,1024]{2,1,0:T(8,128)(2,1)}, f32[8,2,1024]{2,1,0:T(2,128)}, f32[8,128]{1,0:T(8,128)}) custom-call(s32[1]{0:T(128)S(6)} %copy.76.bucket_ref, s32[1,4]{1,0:T(1,128)} %lengths_ref.9, ...), custom_call_target="tpu_custom_call", output_to_operand_aliasing={{0}: (5, {}), {1}: (6, {}), {2}: (7, {}), {3}: (8, {})} | custom-call | flops 230000000 | bytes 100000 | tf_op jit(solution)/shard_map/attend/pallas_call | solution.py:270
  184.1 3.0 collective-permute-done.31.refs_35_
  187.1 45.7 %feed.1 = (bf16[1024,1024]{1,0:T(8,128)(2,1)}, f32[1024,1024]{1,0:T(8,128)}, bf16[4,1024,1024]{2,1,0:T(8,128)(2,1)}, bf16[1024,1024]{1,0:T(8,128)(2,1)}, f32[102...) custom-call(s32[1]{0:T(128)S(6)} %copy.76.bucket_ref, ...), custom_call_target="tpu_custom_call" | custom-call | flops 230000000 | bytes 100000 | tf_op jit(solution)/shard_map/feed/pallas_call | solution.py:501
  232.9 35.6 %feed_back.1 = (f32[1024,1024]{1,0:T(8,128)}, bf16[1024,1024]{1,0:T(8,128)(2,1)}) custom-call(s32[4,9]{1,0:T(4,128)} %dynamic-slice_bitcast_fusion.table_ref, f32[1024,1024]{1,0:T(8,128)} %get-tuple-element.106.third_ref, bf16[4,1024,1024]{2,1,0:T(8,128)(2,1)} %get-tuple-element.107.slope_ref, bf16[1024,1024]{1,0:T(8,128)(2,1)} %get-tuple-element.108.normal_ref, ...), custom_call_target="tpu_custom_call" | custom-call | flops 230000000 | bytes 100000 | tf_op jit(solution)/shard_map/feed_back/pallas_call | solution.py:578
  268.4 39.5 %attend_back.2 = (bf16[1024,1024]{1,0:T(8,128)(2,1)}, bf16[1024,1024]{1,0:T(8,128)(2,1)}, bf16[1024,1024]{1,0:T(8,128)(2,1)}) custom-call(bf16[1,1024,1024]{2,1,0:T(8,128)(2,1)} %get-tuple-element.95.q_ref, bf16[2,1024,1024]{2,1,0:T(8,128)(2,1)} %project.3.refs_2_.k_ref.v_ref, bf16[2,1024,1024]{2,1,0:T(8,128)(2,1)} %project.3.refs_2_.k_ref.v_ref, ...), custom_call_target="tpu_custom_call" | custom-call | flops 230000000 | bytes 100000 | tf_op jit(solution)/shard_map/attend_back/pallas_call | solution.py:350
  307.9 19.5 %after_cross_back.1 = (bf16[1024,1024]{1,0:T(8,128)(2,1)}, f32[1024,1024]{1,0:T(8,128)}, bf16[1024,1024]{1,0:T(8,128)(2,1)}) custom-call(s32[4,9]{1,0:T(4,128)} %dynamic-slice_bitcast_fusion.table_ref, bf16[1024,1024]{1,0:T(8,128)(2,1)} %get-tuple-element.115.dq_ref, bf16[1024,1024]{1,0:T(8,128)(2,1)} %get-tuple-element.116.dk_ref, ...), custom_call_target="tpu_custom_call" | custom-call | flops 230000000 | bytes 100000 | tf_op jit(solution)/shard_map/after_cross_back/pallas_call | solution.py:639
  327.4 32.9 %attend_back.3 = (bf16[1024,1024]{1,0:T(8,128)(2,1)}, bf16[1024,1024]{1,0:T(8,128)(2,1)}, bf16[1024,1024]{1,0:T(8,128)(2,1)}) custom-call(bf16[3,1024,1024]{2,1,0:T(8,128)(2,1)} %project.2.refs_1_.refs_27_.q_ref.k_ref.v_ref, bf16[3,1024,1024]{2,1,0:T(8,128)(2,1)} %project.2.refs_1_.refs_27_.q_ref.k_ref.v_ref, ...), custom_call_target="tpu_custom_call" | custom-call | flops 230000000 | bytes 100000 | tf_op jit(solution)/shard_map/attend_back/pallas_call | solution.py:350
  360.3 12.6 %input_gradient.1 = bf16[1024,1024]{1,0:T(8,128)(2,1)} custom-call(s32[4,9]{1,0:T(4,128)} %dynamic-slice_bitcast_fusion.table_ref, bf16[1024,1024]{1,0:T(8,128)(2,1)} %get-tuple-element.124.dq_ref, bf16[1024,1024]{1,0:T(8,128)(2,1)} %get-tuple-element.125.dk_ref, bf16[1024,1024]{1,0:T(8,128)(2,1)} %get-tuple-element.126.dv_ref, ...), custom_call_target="tpu_custom_call" | custom-call | flops 230000000 | bytes 100000 | tf_op jit(solution)/shard_map/input_gradient/pallas_call | solution.py:677
  372.9 1.9 all-reduce.3.cloned.1.call-done
  374.9 12.0 %adamw.1 = (f32[1024,512]{1,0:T(8,128)}, f32[1024,512]{1,0:T(8,128)}, f32[1024,512]{1,0:T(8,128)}, f32[1024,512]{1,0:T(8,128)}, bf16[1024,512]{1,0:T(8,128)(2,1)...) custom-call(f32[1024,512]{1,0:T(8,128)} %refs_0_.5, ...), custom_call_target="tpu_custom_call" | custom-call | flops 11500000256 | bytes 100000 | tf_op jit(solution)/shard_map/adamw/pallas_call | solution.py:716
  (77 shorter events, 35.8 us)
Async XLA Ops:
  7.2 367.7 %all-reduce.3.cloned.1.call-start = ((), (), s32[]{:S(2)}) async-start(), calls=%async_computation | async-start | bytes 8388608 | tf_op jit(solution)/shard_map/psum | solution.py:943
  9.5 16.0 %collective-permute-start = (bf16[4,128,1024]{2,1,0:T(8,128)(2,1)}, bf16[4,128,1024]{2,1,0:T(8,128)(2,1)}, u32[]{:S(2)}, u32[]{:S(2)}) collective-permute-start(bf16[4,128,1024]{2,1,0:T(8,128)(2,1)} %pack.1.refs_0_.refs_9_.refs_18_), channel_id=1, source_target_pairs={{0,8},{1,5},{2,10},{3,7},{4,0},{5,13},{6,2},{7,15},{8,16},{9,1},{1... | collective-permute-start | bytes 3145736 | tf_op jit(solution)/shard_map/ppermute | solution.py:849
  16.0 15.1 %collective-permute-start.9 = (bf16[2,128,1024]{2,1,0:T(8,128)(2,1)}, bf16[2,128,1024]{2,1,0:T(8,128)(2,1)}, u32[]{:S(2)}, u32[]{:S(2)}) collective-permute-start(bf16[2,128,1024]{2,1,0:T(8,128)(2,1)} %get-tuple-element.77.refs_1_.refs_0_.refs_9_), channel_id=1, source_target_pairs={{0,8},{1,5},{2,10},{3,7},{4,0},{5,13},{6,2},{7,15},{8,16},{9,1},{1... | collective-permute-start | bytes 1572872 | tf_op jit(solution)/shard_map/ppermute | solution.py:849
  26.0 18.6 %collective-permute-start.1 = (bf16[4,128,1024]{2,1,0:T(8,128)(2,1)}, bf16[4,128,1024]{2,1,0:T(8,128)(2,1)}, u32[]{:S(2)}, u32[]{:S(2)}) collective-permute-start(bf16[4,128,1024]{2,1,0:T(8,128)(2,1)} %get-tuple-element.78.refs_1_.refs_10_.refs_19_), channel_id=1, source_target_pairs={{0,1},{1,0},{2,3},{3,2},{4,5},{5,4},{6,7},{7,6},{8,9},{9,8},{10,11... | collective-permute-start | bytes 3145736 | tf_op jit(solution)/shard_map/ppermute | solution.py:849
  26.1 18.5 %collective-permute-start.2 = (bf16[4,128,1024]{2,1,0:T(8,128)(2,1)}, bf16[4,128,1024]{2,1,0:T(8,128)(2,1)}, u32[]{:S(2)}, u32[]{:S(2)}) collective-permute-start(bf16[4,128,1024]{2,1,0:T(8,128)(2,1)} %get-tuple-element.78.refs_1_.refs_10_.refs_19_), channel_id=1, source_target_pairs={{0,8},{1,5},{2,10},{3,7},{4,0},{5,13},{6,2},{7,15},{8,16},{9,1},{1... | collective-permute-start | bytes 3145736 | tf_op jit(solution)/shard_map/ppermute | solution.py:849
  31.1 13.5 %collective-permute-start.12 = (bf16[2,128,1024]{2,1,0:T(8,128)(2,1)}, bf16[2,128,1024]{2,1,0:T(8,128)(2,1)}, u32[]{:S(2)}, u32[]{:S(2)}) collective-permute-start(bf16[2,128,1024]{2,1,0:T(8,128)(2,1)} %collective-permute-done.9.refs_1_.refs_10_), channel_id=1, source_target_pairs={{0,2},{1,3},{2,0},{3,1},{4,6},{5,7},{6,4},{7,5},{8,10},{9,11},{10,... | collective-permute-start | bytes 1572872 | tf_op jit(solution)/shard_map/ppermute | solution.py:849
  33.2 14.3 %collective-permute-start.10 = (bf16[2,128,1024]{2,1,0:T(8,128)(2,1)}, bf16[2,128,1024]{2,1,0:T(8,128)(2,1)S(1)}, u32[]{:S(2)}, u32[]{:S(2)}) collective-permute-start(bf16[2,128,1024]{2,1,0:T(8,128)(2,1)} %collective-permute-done.9.refs_1_.refs_10_), channel_id=1, source_target_pairs={{0,1},{1,0},{2,3},{3,2},{4,5},{5,4},{6,7},{7,6},{8,9},{9,8},{10,11... | collective-permute-start | bytes 1572872 | tf_op jit(solution)/shard_map/ppermute | solution.py:849
  33.2 14.8 %collective-permute-start.11 = (bf16[2,128,1024]{2,1,0:T(8,128)(2,1)}, bf16[2,128,1024]{2,1,0:T(8,128)(2,1)}, u32[]{:S(2)}, u32[]{:S(2)}) collective-permute-start(bf16[2,128,1024]{2,1,0:T(8,128)(2,1)} %collective-permute-done.9.refs_1_.refs_10_), channel_id=1, source_target_pairs={{0,8},{1,5},{2,10},{3,7},{4,0},{5,13},{6,2},{7,15},{8,16},{9,1},{1... | collective-permute-start | bytes 1572872 | tf_op jit(solution)/shard_map/ppermute | solution.py:849
  44.6 3.4 collective-permute-start.13
  45.1 17.6 %collective-permute-start.3 = (bf16[4,128,1024]{2,1,0:T(8,128)(2,1)}, bf16[4,128,1024]{2,1,0:T(8,128)(2,1)}, u32[]{:S(2)}, u32[]{:S(2)}) collective-permute-start(bf16[4,128,1024]{2,1,0:T(8,128)(2,1)} %get-tuple-element.79.refs_3_.refs_12_.refs_21_), channel_id=1, source_target_pairs={{0,1},{1,0},{2,3},{3,2},{4,5},{5,4},{6,7},{7,6},{8,9},{9,8},{10,11... | collective-permute-start | bytes 3145736 | tf_op jit(solution)/shard_map/ppermute | solution.py:849
  45.7 17.0 %collective-permute-start.4 = (bf16[4,128,1024]{2,1,0:T(8,128)(2,1)}, bf16[4,128,1024]{2,1,0:T(8,128)(2,1)}, u32[]{:S(2)}, u32[]{:S(2)}) collective-permute-start(bf16[4,128,1024]{2,1,0:T(8,128)(2,1)} %get-tuple-element.79.refs_3_.refs_12_.refs_21_), channel_id=1, source_target_pairs={{0,8},{1,5},{2,10},{3,7},{4,0},{5,13},{6,2},{7,15},{8,16},{9,1},{1... | collective-permute-start | bytes 3145736 | tf_op jit(solution)/shard_map/ppermute | solution.py:849
  48.8 13.9 %collective-permute-start.16 = (bf16[2,128,1024]{2,1,0:T(8,128)(2,1)}, bf16[2,128,1024]{2,1,0:T(8,128)(2,1)}, u32[]{:S(2)}, u32[]{:S(2)}) collective-permute-start(bf16[2,128,1024]{2,1,0:T(8,128)(2,1)} %get-tuple-element.82.refs_3_.refs_12_), channel_id=1, source_target_pairs={{0,2},{1,3},{2,0},{3,1},{4,6},{5,7},{6,4},{7,5},{8,10},{9,11},{10,... | collective-permute-start | bytes 1572872 | tf_op jit(solution)/shard_map/ppermute | solution.py:849
  50.6 16.3 %collective-permute-start.14 = (bf16[2,128,1024]{2,1,0:T(8,128)(2,1)}, bf16[2,128,1024]{2,1,0:T(8,128)(2,1)}, u32[]{:S(2)}, u32[]{:S(2)}) collective-permute-start(bf16[2,128,1024]{2,1,0:T(8,128)(2,1)} %get-tuple-element.82.refs_3_.refs_12_), channel_id=1, source_target_pairs={{0,1},{1,0},{2,3},{3,2},{4,5},{5,4},{6,7},{7,6},{8,9},{9,8},{10,11... | collective-permute-start | bytes 1572872 | tf_op jit(solution)/shard_map/ppermute | solution.py:849
  50.6 16.3 %collective-permute-start.15 = (bf16[2,128,1024]{2,1,0:T(8,128)(2,1)}, bf16[2,128,1024]{2,1,0:T(8,128)(2,1)S(1)}, u32[]{:S(2)}, u32[]{:S(2)}) collective-permute-start(bf16[2,128,1024]{2,1,0:T(8,128)(2,1)} %get-tuple-element.82.refs_3_.refs_12_), channel_id=1, source_target_pairs={{0,8},{1,5},{2,10},{3,7},{4,0},{5,13},{6,2},{7,15},{8,16},{9,1},{1... | collective-permute-start | bytes 1572872 | tf_op jit(solution)/shard_map/ppermute | solution.py:849
  62.7 4.2 %collective-permute-start.17 = (bf16[2,128,1024]{2,1,0:T(8,128)(2,1)}, bf16[2,128,1024]{2,1,0:T(8,128)(2,1)}, u32[]{:S(2)}, u32[]{:S(2)}) collective-permute-start(bf16[2,128,1024]{2,1,0:T(8,128)(2,1)} %collective-permute-done.16.refs_21_), channel_id=1, source_target_pairs={{0,1},{1,0},{2,3},{3,2},{4,5},{5,4},{6,7},{7,6},{8,9},{9,8},{10,11... | collective-permute-start | bytes 1572872 | tf_op jit(solution)/shard_map/ppermute | solution.py:849
  65.1 9.5 %collective-permute-start.6 = (bf16[4,64,1024]{2,1,0:T(8,128)(2,1)}, bf16[4,64,1024]{2,1,0:T(8,128)(2,1)}, u32[]{:S(2)}, u32[]{:S(2)}) collective-permute-start(bf16[4,64,1024]{2,1,0:T(8,128)(2,1)} %constant_dynamic-slice_fusion.2), channel_id=1, source_target_pairs={{0,8},{1,5},{2,10},{3,7},{4,0},{5,13},{6,2},{7,15},{8,16},{9,1},{1... | collective-permute-start | bytes 1572872 | tf_op jit(solution)/shard_map/ppermute | solution.py:849
  66.2 18.3 %collective-permute-start.5 = (bf16[4,128,1024]{2,1,0:T(8,128)(2,1)}, bf16[4,128,1024]{2,1,0:T(8,128)(2,1)}, u32[]{:S(2)}, u32[]{:S(2)}) collective-permute-start(bf16[4,128,1024]{2,1,0:T(8,128)(2,1)} %get-tuple-element.80.refs_5_.refs_14_.refs_23_), channel_id=1, source_target_pairs={{0,1},{1,0},{2,3},{3,2},{4,5},{5,4},{6,7},{7,6},{8,9},{9,8},{10,11... | collective-permute-start | bytes 3145736 | tf_op jit(solution)/shard_map/ppermute | solution.py:849
  68.3 14.4 %collective-permute-start.21 = (bf16[2,128,1024]{2,1,0:T(8,128)(2,1)}, bf16[2,128,1024]{2,1,0:T(8,128)(2,1)S(1)}, u32[]{:S(2)}, u32[]{:S(2)}) collective-permute-start(bf16[2,128,1024]{2,1,0:T(8,128)(2,1)} %get-tuple-element.83.refs_5_.refs_14_), channel_id=1, source_target_pairs={{0,2},{1,3},{2,0},{3,1},{4,6},{5,7},{6,4},{7,5},{8,10},{9,11},{10,... | collective-permute-start | bytes 1572872 | tf_op jit(solution)/shard_map/ppermute | solution.py:849
  74.6 9.6 %collective-permute-start.7 = (bf16[4,64,1024]{2,1,0:T(8,128)(2,1)}, bf16[4,64,1024]{2,1,0:T(8,128)(2,1)}, u32[]{:S(2)}, u32[]{:S(2)}) collective-permute-start(bf16[4,64,1024]{2,1,0:T(8,128)(2,1)} %collective-permute-done.6.refs_1_.refs_7_.refs_16_.refs_25_), channel_id=1, source_target_pairs={{0,1},{1,0},{2,3},{3,2},{4,5},{5,4},{6,7},{7,6},{8,9},{9,8},{10,11... | collective-permute-start | bytes 1572872 | tf_op jit(solution)/shard_map/ppermute | solution.py:849
  75.6 6.5 %collective-permute-start.19 = (bf16[2,64,1024]{2,1,0:T(8,128)(2,1)S(1)}, bf16[2,64,1024]{2,1,0:T(8,128)(2,1)}, u32[]{:S(2)}, u32[]{:S(2)}) collective-permute-start(bf16[2,64,1024]{2,1,0:T(8,128)(2,1)S(1)} %constant_dynamic-slice_fusion.1), channel_id=1, source_target_pairs={{0,8},{1,5},{2,10},{3,7},{4,0},{5,13},{6,2},{7,15},{8,16},{9,1},{1... | collective-permute-start | bytes 786440 | tf_op jit(solution)/shard_map/ppermute | solution.py:849
  76.7 22.2 %collective-permute-start.18 = (bf16[2,128,1024]{2,1,0:T(8,128)(2,1)}, bf16[2,128,1024]{2,1,0:T(8,128)(2,1)}, u32[]{:S(2)}, u32[]{:S(2)}) collective-permute-start(bf16[2,128,1024]{2,1,0:T(8,128)(2,1)} %get-tuple-element.83.refs_5_.refs_14_), channel_id=1, source_target_pairs={{0,1},{1,0},{2,3},{3,2},{4,5},{5,4},{6,7},{7,6},{8,9},{9,8},{10,11... | collective-permute-start | bytes 1572872 | tf_op jit(solution)/shard_map/ppermute | solution.py:849
  82.1 16.8 %collective-permute-start.20 = (bf16[2,64,1024]{2,1,0:T(8,128)(2,1)}, bf16[2,64,1024]{2,1,0:T(8,128)(2,1)}, u32[]{:S(2)}, u32[]{:S(2)}) collective-permute-start(bf16[2,64,1024]{2,1,0:T(8,128)(2,1)} %collective-permute-done.19.refs_7_.refs_16_), channel_id=1, source_target_pairs={{0,1},{1,0},{2,3},{3,2},{4,5},{5,4},{6,7},{7,6},{8,9},{9,8},{10,11... | collective-permute-start | bytes 786440 | tf_op jit(solution)/shard_map/ppermute | solution.py:849
  82.7 14.5 %collective-permute-start.23 = (bf16[2,64,1024]{2,1,0:T(8,128)(2,1)}, bf16[2,64,1024]{2,1,0:T(8,128)(2,1)S(1)}, u32[]{:S(2)}, u32[]{:S(2)}) collective-permute-start(bf16[2,64,1024]{2,1,0:T(8,128)(2,1)} %collective-permute-done.19.refs_7_.refs_16_), channel_id=1, source_target_pairs={{0,2},{1,3},{2,0},{3,1},{4,6},{5,7},{6,4},{7,5},{8,10},{9,11},{10,... | collective-permute-start | bytes 786440 | tf_op jit(solution)/shard_map/ppermute | solution.py:849
  84.2 14.7 %collective-permute-start.22 = (bf16[2,128,1024]{2,1,0:T(8,128)(2,1)S(1)}, bf16[2,128,1024]{2,1,0:T(8,128)(2,1)}, u32[]{:S(2)}, u32[]{:S(2)}) collective-permute-start(bf16[2,128,1024]{2,1,0:T(8,128)(2,1)S(1)} %collective-permute-done.21.refs_23_), channel_id=1, source_target_pairs={{0,1},{1,0},{2,3},{3,2},{4,5},{5,4},{6,7},{7,6},{8,9},{9,8},{10,11... | collective-permute-start | bytes 1572872 | tf_op jit(solution)/shard_map/ppermute | solution.py:849
  84.5 26.4 %collective-permute-start.8 = (bf16[8,128,1024]{2,1,0:T(8,128)(2,1)}, bf16[8,128,1024]{2,1,0:T(8,128)(2,1)}, u32[]{:S(2)}, u32[]{:S(2)}) collective-permute-start(bf16[8,128,1024]{2,1,0:T(8,128)(2,1)} %get-tuple-element.81.refs_27_), channel_id=1, source_target_pairs={{0,8},{1,5},{2,10},{3,7},{4,0},{5,13},{6,2},{7,15},{8,16},{9,1},{1... | collective-permute-start | bytes 6291464 | tf_op jit(solution)/shard_map/ppermute | solution.py:849
  111.3 26.6 %collective-permute-start.25 = (bf16[8,128,1024]{2,1,0:T(8,128)(2,1)}, bf16[8,128,1024]{2,1,0:T(8,128)(2,1)}, u32[]{:S(2)}, u32[]{:S(2)}) collective-permute-start(bf16[8,128,1024]{2,1,0:T(8,128)(2,1)} %get-tuple-element.86.refs_0_.refs_28_), channel_id=1, source_target_pairs={{0,8},{1,5},{2,10},{3,7},{4,0},{5,13},{6,2},{7,15},{8,16},{9,1},{1... | collective-permute-start | bytes 6291464 | tf_op jit(solution)/shard_map/ppermute | solution.py:849
  138.5 26.7 %collective-permute-start.26 = (bf16[8,128,1024]{2,1,0:T(8,128)(2,1)}, bf16[8,128,1024]{2,1,0:T(8,128)(2,1)}, u32[]{:S(2)}, u32[]{:S(2)}) collective-permute-start(bf16[8,128,1024]{2,1,0:T(8,128)(2,1)} %get-tuple-element.93.refs_27_.refs_30_), channel_id=1, source_target_pairs={{0,8},{1,5},{2,10},{3,7},{4,0},{5,13},{6,2},{7,15},{8,16},{9,1},{1... | collective-permute-start | bytes 6291464 | tf_op jit(solution)/shard_map/ppermute | solution.py:849
  167.9 15.6 %collective-permute-start.30 = (bf16[8,64,1024]{2,1,0:T(8,128)(2,1)}, bf16[8,64,1024]{2,1,0:T(8,128)(2,1)}, u32[]{:S(2)}, u32[]{:S(2)}) collective-permute-start(bf16[8,64,1024]{2,1,0:T(8,128)(2,1)} %constant_dynamic-slice_fusion), channel_id=1, source_target_pairs={{0,8},{1,5},{2,10},{3,7},{4,0},{5,13},{6,2},{7,15},{8,16},{9,1},{1... | collective-permute-start | bytes 3145736 | tf_op jit(solution)/shard_map/ppermute | solution.py:849
  169.5 14.6 %collective-permute-start.27 = (bf16[8,128,1024]{2,1,0:T(8,128)(2,1)}, bf16[8,128,1024]{2,1,0:T(8,128)(2,1)}, u32[]{:S(2)}, u32[]{:S(2)}) collective-permute-start(bf16[8,128,1024]{2,1,0:T(8,128)(2,1)} %get-tuple-element.86.refs_0_.refs_28_), channel_id=1, source_target_pairs={{0,1},{1,0},{2,3},{3,2},{4,5},{5,4},{6,7},{7,6},{8,9},{9,8},{10,11... | collective-permute-start | bytes 6291464 | tf_op jit(solution)/shard_map/ppermute | solution.py:849
  169.5 14.6 %collective-permute-start.28 = (bf16[8,128,1024]{2,1,0:T(8,128)(2,1)}, bf16[8,128,1024]{2,1,0:T(8,128)(2,1)}, u32[]{:S(2)}, u32[]{:S(2)}) collective-permute-start(bf16[8,128,1024]{2,1,0:T(8,128)(2,1)} %get-tuple-element.93.refs_27_.refs_30_), channel_id=1, source_target_pairs={{0,1},{1,0},{2,3},{3,2},{4,5},{5,4},{6,7},{7,6},{8,9},{9,8},{10,11... | collective-permute-start | bytes 6291464 | tf_op jit(solution)/shard_map/ppermute | solution.py:849
  170.0 17.1 %collective-permute-start.29 = (bf16[8,128,1024]{2,1,0:T(8,128)(2,1)}, bf16[8,128,1024]{2,1,0:T(8,128)(2,1)}, u32[]{:S(2)}, u32[]{:S(2)}) collective-permute-start(bf16[8,128,1024]{2,1,0:T(8,128)(2,1)} %get-tuple-element.101.refs_4_.refs_32_), channel_id=1, source_target_pairs={{0,1},{1,0},{2,3},{3,2},{4,5},{5,4},{6,7},{7,6},{8,9},{9,8},{10,11... | collective-permute-start | bytes 6291464 | tf_op jit(solution)/shard_map/ppermute | solution.py:849
  184.0 3.1 collective-permute-start.31
  (6 other events, 19.5 us)
Sparse Core Ops, SparseCore 0:
  233.0 141.8 all-reduce.2

commit v3 on v2

--- a/solution.py
+++ b/solution.py
@@ -879,11 +879,14 @@
         while self.count < self.quarter * links.hops // 4:
             if chained and len(self.pieces) > 1:
                 sooner = (*sooner, self.pieces[-1], *self.rest[2:][-1:])
-            self.share(*sooner)
+            final = self.count + 1 == links.hops
+            half = links.last(self.moving) if final and self.rest else None
+            self.share(*sooner, *(() if half is None else (half,)))
             sooner = ()
             self.count += 1
-            moving = links.last(self.moving) if self.count == links.hops else self.moving
-            self.moving = links.send(moving, links.onward)
+            if half is None:
+                half = links.last(self.moving) if final else self.moving
+            self.moving = links.send(half, links.onward)
 
 
 def body(

time: 401 us -> 401 us (level)
  no operation moved by 1% of the time
where the time goes in v3:
time: 401 us; the launch traced here: 394 us
  Pallas kernels  291 us (73%)
  waiting for transfers between devices  50.3 us (13%)
  starting transfers between devices  29.3 us (7%)
  between operations  15.4 us (4%)
  local copies, waits for them, and re-layouts  8.06 us (2%)
    pallas_call x2, Pallas kernels, attend_back(): pl.pallas_call(functools.partial(attend_back_kernel, causal), grid=(pairs...  72.4 us
    ppermute x32, waiting for transfers between devices, send(): return lax.ppermute(values, AXES, pairs)  48.4 us
    pallas_call x4, Pallas kernels, attend(): pl.pallas_call(functools.partial(attend_kernel, causal), grid=(stop - sta...  48.1 us
    pallas_call x1, Pallas kernels, feed(): pl.pallas_call(functools.partial(feed_kernel, (output_at,), len(feed_piec...  45.7 us
    pallas_call x1, Pallas kernels, feed_back(): pl.pallas_call(functools.partial(feed_back_kernel, (output_at,), len(feed...  35.6 us
    ppermute x32, starting transfers between devices, send(): return lax.ppermute(values, AXES, pairs)  29.3 us
    pallas_call x2, Pallas kernels, project(): pl.pallas_call(functools.partial(project_kernel, wanted, scale, len(piece...  20.7 us
    pallas_call x1, Pallas kernels, after_cross_back(): pl.pallas_call(functools.partial(cross_back_kernel, wanted), grid=(tokens...  19.5 us
  transfers between devices with their start and end apart: 33, of which 14 were waited for; matrix products, arithmetic and copies ran while one was open for 1% of the time, Pallas kernels for 58%

profile of v3, /device:TPU:0, one launch (start us, length us, event | category | flops | bytes accessed | tf_op | source)
XLA Modules:
  0.0 393.6 jit_solution(9397067858544383230)
XLA Ops:
  7.2 2.2 pack.1.refs_0_.refs_9_.refs_18_
  9.5 3.0 collective-permute-start
  13.7 2.3 pack_pair.1
  17.6 3.0 pack_feed.1.refs_2_.refs_0_
  20.6 4.9 %collective-permute-done.refs_0_ = bf16[4,128,1024]{2,1,0:T(8,128)(2,1)} collective-permute-done((bf16[4,128,1024]{2,1,0:T(8,128)(2,1)}, bf16[4,128,1024]{2,1,0:T(8,128)(2,1)}, u32[]{:S(2)}, u32[]{:S(2)}) %collective-permute-start) | collective-permute-done | bytes 1048608 | tf_op jit(solution)/shard_map/ppermute | solution.py:849
  26.1 2.2 collective-permute-start.2
  28.2 2.9 collective-permute-done.9.refs_1_.refs_10_
  31.1 2.1 collective-permute-start.12
  34.7 9.9 %collective-permute-done.12.refs_19_ = bf16[2,128,1024]{2,1,0:T(8,128)(2,1)} collective-permute-done((bf16[2,128,1024]{2,1,0:T(8,128)(2,1)}, bf16[2,128,1024]{2,1,0:T(8,128)(2,1)}, u32[]{:S(2)}, u32[]{:S(2)}) %collective-permute-start.12) | collective-permute-done | bytes 524320 | tf_op jit(solution)/shard_map/ppermute | solution.py:849
  48.8 1.8 collective-permute-start.16
  52.2 10.5 %collective-permute-done.16.refs_21_ = bf16[2,128,1024]{2,1,0:T(8,128)(2,1)} collective-permute-done((bf16[2,128,1024]{2,1,0:T(8,128)(2,1)}, bf16[2,128,1024]{2,1,0:T(8,128)(2,1)}, u32[]{:S(2)}, u32[]{:S(2)}) %collective-permute-start.16) | collective-permute-done | bytes 524320 | tf_op jit(solution)/shard_map/ppermute | solution.py:849
  63.2 1.9 constant_dynamic-slice_fusion.2
  70.0 4.6 %collective-permute-done.6.refs_1_.refs_7_.refs_16_.refs_25_ = bf16[4,64,1024]{2,1,0:T(8,128)(2,1)} collective-permute-done((bf16[4,64,1024]{2,1,0:T(8,128)(2,1)}, bf16[4,64,1024]{2,1,0:T(8,128)(2,1)}, u32[]{:S(2)}, u32[]{:S(2)}) %collective-permute-start.6) | collective-permute-done | bytes 524320 | tf_op jit(solution)/shard_map/ppermute | solution.py:849
  75.7 5.6 %collective-permute-done.19.refs_7_.refs_16_ = bf16[2,64,1024]{2,1,0:T(8,128)(2,1)} collective-permute-done((bf16[2,64,1024]{2,1,0:T(8,128)(2,1)}, bf16[2,64,1024]{2,1,0:T(8,128)(2,1)}, u32[]{:S(2)}, u32[]{:S(2)}) %collective-permute-start.19) | collective-permute-done | bytes 262176 | tf_op jit(solution)/shard_map/ppermute | solution.py:849
  85.0 11.5 %project.2.refs_1_.refs_27_.q_ref.k_ref.v_ref = bf16[3,1024,1024]{2,1,0:T(8,128)(2,1)} custom-call(bf16[1024,1024]{1,0:T(8,128)(2,1)} %x_ref.5, s32[4,9]{1,0:T(4,128)} %dynamic-slice_bitcast_fusion.table_ref, bf16[4,128,1024]{2,1,0:T(8,128)(2,1)} %pack.1.refs_0_.refs_9_.refs_18_, bf16[4,128,1024]{2,1,0:T(8,128)(2,1)} %get-tuple-element.78.refs_1_.refs_10_.refs_19_, ...), custom_call_target="tpu_custom_call" | custom-call | flops 13799999488 | bytes 100000 | tf_op jit(solution)/shard_map/project/pallas_call | solution.py:142
  100.4 9.2 %project.3.refs_2_.k_ref.v_ref = bf16[2,1024,1024]{2,1,0:T(8,128)(2,1)} custom-call(bf16[1024,1024]{1,0:T(8,128)(2,1)} %x_ref.4, s32[4,9]{1,0:T(4,128)} %dynamic-slice_bitcast_fusion.table_ref, bf16[2,128,1024]{2,1,0:T(8,128)(2,1)} %get-tuple-element.77.refs_1_.refs_0_.refs_9_, bf16[2,128,1024]{2,1,0:T(8,128)(2,1)} %collective-permute-done.9.refs_1_.refs_10_, ...), custom_call_target="tpu_custom_call" | custom-call | flops 9200000000 | bytes 100000 | tf_op jit(solution)/shard_map/project/pallas_call | solution.py:142
  112.8 12.0 %attend.4 = (bf16[1024,1024]{1,0:T(8,128)(2,1)}, bf16[1024,1024]{1,0:T(8,128)(2,1)}, bf16[16,1024,1024]{2,1,0:T(8,128)(2,1)}, f32[8,2,1024]{2,1,0:T(2,128)}, f32[8,128]{1,0:T(8,128)}) custom-call(s32[1]{0:T(128)S(6)} %copy.76.bucket_ref, s32[1,4]{1,0:T(1,128)} %lengths_ref.9, bf16[3,1024,1024]{2,1,0:T(8,128)(2,1)} %project.2.refs_1_.refs_27_.q_ref.k_ref.v_ref, ...), custom_call_target="tpu_custom_call" | custom-call | flops 230000000 | bytes 100000 | tf_op jit(solution)/shard_map/attend/pallas_call | solution.py:270
  124.8 12.0 %attend.5 = (bf16[1024,1024]{1,0:T(8,128)(2,1)}, bf16[1024,1024]{1,0:T(8,128)(2,1)}, bf16[16,1024,1024]{2,1,0:T(8,128)(2,1)}, f32[8,2,1024]{2,1,0:T(2,128)}, f32[8,128]{1,0:T(8,128)}) custom-call(s32[1]{0:T(128)S(6)} %copy.76.bucket_ref, s32[1,4]{1,0:T(1,128)} %lengths_ref.9, ...), custom_call_target="tpu_custom_call", output_to_operand_aliasing={{0}: (5, {}), {1}: (6, {}), {2}: (7, {}), {3}: (8, {})} | custom-call | flops 230000000 | bytes 100000 | tf_op jit(solution)/shard_map/attend/pallas_call | solution.py:270
  139.4 10.7 %after_self.1 = (f32[1024,1024]{1,0:T(8,128)}, f32[1024,128]{1,0:T(8,128)}, bf16[1,1024,1024]{2,1,0:T(8,128)(2,1)}) custom-call(s32[4,9]{1,0:T(4,128)} %dynamic-slice_bitcast_fusion.table_ref, bf16[1024,1024]{1,0:T(8,128)(2,1)} %x_ref.5, bf16[1024,1024]{1,0:T(8,128)(2,1)} %get-tuple-element.91.out_ref, f32[3,1024]{1,0:T(4,128)} %gains_ref.7, ...), custom_call_target="tpu_custom_call" | custom-call | flops 230000000 | bytes 100000 | tf_op jit(solution)/shard_map/after_self/pallas_call | solution.py:394
  150.0 12.1 %attend.6 = (bf16[1024,1024]{1,0:T(8,128)(2,1)}, bf16[1024,1024]{1,0:T(8,128)(2,1)}, bf16[16,1024,1024]{2,1,0:T(8,128)(2,1)}, f32[8,2,1024]{2,1,0:T(2,128)}, f32[8,128]{1,0:T(8,128)}) custom-call(s32[1]{0:T(128)S(6)} %copy.76.bucket_ref, s32[1,4]{1,0:T(1,128)} %lengths_ref.9, bf16[1,1024,1024]{2,1,0:T(8,128)(2,1)} %get-tuple-element.95.q_ref, ...), custom_call_target="tpu_custom_call" | custom-call | flops 230000000 | bytes 100000 | tf_op jit(solution)/shard_map/attend/pallas_call | solution.py:270
  162.1 2.5 collective-permute-done.26.refs_0_
  165.1 2.3 constant_dynamic-slice_fusion
  169.5 12.1 %attend.7 = (bf16[1024,1024]{1,0:T(8,128)(2,1)}, bf16[1024,1024]{1,0:T(8,128)(2,1)}, bf16[16,1024,1024]{2,1,0:T(8,128)(2,1)}, f32[8,2,1024]{2,1,0:T(2,128)}, f32[8,128]{1,0:T(8,128)}) custom-call(s32[1]{0:T(128)S(6)} %copy.76.bucket_ref, s32[1,4]{1,0:T(1,128)} %lengths_ref.9, ...), custom_call_target="tpu_custom_call", output_to_operand_aliasing={{0}: (5, {}), {1}: (6, {}), {2}: (7, {}), {3}: (8, {})} | custom-call | flops 230000000 | bytes 100000 | tf_op jit(solution)/shard_map/attend/pallas_call | solution.py:270
  183.6 3.0 collective-permute-done.31.refs_35_
  186.6 45.7 %feed.1 = (bf16[1024,1024]{1,0:T(8,128)(2,1)}, f32[1024,1024]{1,0:T(8,128)}, bf16[4,1024,1024]{2,1,0:T(8,128)(2,1)}, bf16[1024,1024]{1,0:T(8,128)(2,1)}, f32[102...) custom-call(s32[1]{0:T(128)S(6)} %copy.76.bucket_ref, ...), custom_call_target="tpu_custom_call" | custom-call | flops 230000000 | bytes 100000 | tf_op jit(solution)/shard_map/feed/pallas_call | solution.py:501
  232.3 35.6 %feed_back.1 = (f32[1024,1024]{1,0:T(8,128)}, bf16[1024,1024]{1,0:T(8,128)(2,1)}) custom-call(s32[4,9]{1,0:T(4,128)} %dynamic-slice_bitcast_fusion.table_ref, f32[1024,1024]{1,0:T(8,128)} %get-tuple-element.106.third_ref, bf16[4,1024,1024]{2,1,0:T(8,128)(2,1)} %get-tuple-element.107.slope_ref, bf16[1024,1024]{1,0:T(8,128)(2,1)} %get-tuple-element.108.normal_ref, ...), custom_call_target="tpu_custom_call" | custom-call | flops 230000000 | bytes 100000 | tf_op jit(solution)/shard_map/feed_back/pallas_call | solution.py:578
  267.9 39.5 %attend_back.2 = (bf16[1024,1024]{1,0:T(8,128)(2,1)}, bf16[1024,1024]{1,0:T(8,128)(2,1)}, bf16[1024,1024]{1,0:T(8,128)(2,1)}) custom-call(bf16[1,1024,1024]{2,1,0:T(8,128)(2,1)} %get-tuple-element.95.q_ref, bf16[2,1024,1024]{2,1,0:T(8,128)(2,1)} %project.3.refs_2_.k_ref.v_ref, bf16[2,1024,1024]{2,1,0:T(8,128)(2,1)} %project.3.refs_2_.k_ref.v_ref, ...), custom_call_target="tpu_custom_call" | custom-call | flops 230000000 | bytes 100000 | tf_op jit(solution)/shard_map/attend_back/pallas_call | solution.py:350
  307.4 19.5 %after_cross_back.1 = (bf16[1024,1024]{1,0:T(8,128)(2,1)}, f32[1024,1024]{1,0:T(8,128)}, bf16[1024,1024]{1,0:T(8,128)(2,1)}) custom-call(s32[4,9]{1,0:T(4,128)} %dynamic-slice_bitcast_fusion.table_ref, bf16[1024,1024]{1,0:T(8,128)(2,1)} %get-tuple-element.115.dq_ref, bf16[1024,1024]{1,0:T(8,128)(2,1)} %get-tuple-element.116.dk_ref, ...), custom_call_target="tpu_custom_call" | custom-call | flops 230000000 | bytes 100000 | tf_op jit(solution)/shard_map/after_cross_back/pallas_call | solution.py:639
  326.9 32.9 %attend_back.3 = (bf16[1024,1024]{1,0:T(8,128)(2,1)}, bf16[1024,1024]{1,0:T(8,128)(2,1)}, bf16[1024,1024]{1,0:T(8,128)(2,1)}) custom-call(bf16[3,1024,1024]{2,1,0:T(8,128)(2,1)} %project.2.refs_1_.refs_27_.q_ref.k_ref.v_ref, bf16[3,1024,1024]{2,1,0:T(8,128)(2,1)} %project.2.refs_1_.refs_27_.q_ref.k_ref.v_ref, ...), custom_call_target="tpu_custom_call" | custom-call | flops 230000000 | bytes 100000 | tf_op jit(solution)/shard_map/attend_back/pallas_call | solution.py:350
  359.8 12.6 %input_gradient.1 = bf16[1024,1024]{1,0:T(8,128)(2,1)} custom-call(s32[4,9]{1,0:T(4,128)} %dynamic-slice_bitcast_fusion.table_ref, bf16[1024,1024]{1,0:T(8,128)(2,1)} %get-tuple-element.124.dq_ref, bf16[1024,1024]{1,0:T(8,128)(2,1)} %get-tuple-element.125.dk_ref, bf16[1024,1024]{1,0:T(8,128)(2,1)} %get-tuple-element.126.dv_ref, ...), custom_call_target="tpu_custom_call" | custom-call | flops 230000000 | bytes 100000 | tf_op jit(solution)/shard_map/input_gradient/pallas_call | solution.py:677
  372.4 1.9 all-reduce.3.cloned.1.call-done
  374.3 12.0 %adamw.1 = (f32[1024,512]{1,0:T(8,128)}, f32[1024,512]{1,0:T(8,128)}, f32[1024,512]{1,0:T(8,128)}, f32[1024,512]{1,0:T(8,128)}, bf16[1024,512]{1,0:T(8,128)(2,1)...) custom-call(f32[1024,512]{1,0:T(8,128)} %refs_0_.5, ...), custom_call_target="tpu_custom_call" | custom-call | flops 11500000256 | bytes 100000 | tf_op jit(solution)/shard_map/adamw/pallas_call | solution.py:716
  (77 shorter events, 34.5 us)
Async XLA Ops:
  7.2 367.1 %all-reduce.3.cloned.1.call-start = ((), (), s32[]{:S(2)}) async-start(), calls=%async_computation | async-start | bytes 8388608 | tf_op jit(solution)/shard_map/psum | solution.py:946
  9.5 16.0 %collective-permute-start = (bf16[4,128,1024]{2,1,0:T(8,128)(2,1)}, bf16[4,128,1024]{2,1,0:T(8,128)(2,1)}, u32[]{:S(2)}, u32[]{:S(2)}) collective-permute-start(bf16[4,128,1024]{2,1,0:T(8,128)(2,1)} %pack.1.refs_0_.refs_9_.refs_18_), channel_id=1, source_target_pairs={{0,8},{1,5},{2,10},{3,7},{4,0},{5,13},{6,2},{7,15},{8,16},{9,1},{1... | collective-permute-start | bytes 3145736 | tf_op jit(solution)/shard_map/ppermute | solution.py:849
  16.0 15.1 %collective-permute-start.9 = (bf16[2,128,1024]{2,1,0:T(8,128)(2,1)}, bf16[2,128,1024]{2,1,0:T(8,128)(2,1)}, u32[]{:S(2)}, u32[]{:S(2)}) collective-permute-start(bf16[2,128,1024]{2,1,0:T(8,128)(2,1)} %get-tuple-element.77.refs_1_.refs_0_.refs_9_), channel_id=1, source_target_pairs={{0,8},{1,5},{2,10},{3,7},{4,0},{5,13},{6,2},{7,15},{8,16},{9,1},{1... | collective-permute-start | bytes 1572872 | tf_op jit(solution)/shard_map/ppermute | solution.py:849
  26.0 18.6 %collective-permute-start.1 = (bf16[4,128,1024]{2,1,0:T(8,128)(2,1)}, bf16[4,128,1024]{2,1,0:T(8,128)(2,1)}, u32[]{:S(2)}, u32[]{:S(2)}) collective-permute-start(bf16[4,128,1024]{2,1,0:T(8,128)(2,1)} %get-tuple-element.78.refs_1_.refs_10_.refs_19_), channel_id=1, source_target_pairs={{0,1},{1,0},{2,3},{3,2},{4,5},{5,4},{6,7},{7,6},{8,9},{9,8},{10,11... | collective-permute-start | bytes 3145736 | tf_op jit(solution)/shard_map/ppermute | solution.py:849
  26.1 18.5 %collective-permute-start.2 = (bf16[4,128,1024]{2,1,0:T(8,128)(2,1)}, bf16[4,128,1024]{2,1,0:T(8,128)(2,1)}, u32[]{:S(2)}, u32[]{:S(2)}) collective-permute-start(bf16[4,128,1024]{2,1,0:T(8,128)(2,1)} %get-tuple-element.78.refs_1_.refs_10_.refs_19_), channel_id=1, source_target_pairs={{0,8},{1,5},{2,10},{3,7},{4,0},{5,13},{6,2},{7,15},{8,16},{9,1},{1... | collective-permute-start | bytes 3145736 | tf_op jit(solution)/shard_map/ppermute | solution.py:849
  31.1 13.5 %collective-permute-start.12 = (bf16[2,128,1024]{2,1,0:T(8,128)(2,1)}, bf16[2,128,1024]{2,1,0:T(8,128)(2,1)}, u32[]{:S(2)}, u32[]{:S(2)}) collective-permute-start(bf16[2,128,1024]{2,1,0:T(8,128)(2,1)} %collective-permute-done.9.refs_1_.refs_10_), channel_id=1, source_target_pairs={{0,2},{1,3},{2,0},{3,1},{4,6},{5,7},{6,4},{7,5},{8,10},{9,11},{10,... | collective-permute-start | bytes 1572872 | tf_op jit(solution)/shard_map/ppermute | solution.py:849
  33.2 14.3 %collective-permute-start.10 = (bf16[2,128,1024]{2,1,0:T(8,128)(2,1)}, bf16[2,128,1024]{2,1,0:T(8,128)(2,1)S(1)}, u32[]{:S(2)}, u32[]{:S(2)}) collective-permute-start(bf16[2,128,1024]{2,1,0:T(8,128)(2,1)} %collective-permute-done.9.refs_1_.refs_10_), channel_id=1, source_target_pairs={{0,1},{1,0},{2,3},{3,2},{4,5},{5,4},{6,7},{7,6},{8,9},{9,8},{10,11... | collective-permute-start | bytes 1572872 | tf_op jit(solution)/shard_map/ppermute | solution.py:849
  33.2 14.8 %collective-permute-start.11 = (bf16[2,128,1024]{2,1,0:T(8,128)(2,1)}, bf16[2,128,1024]{2,1,0:T(8,128)(2,1)}, u32[]{:S(2)}, u32[]{:S(2)}) collective-permute-start(bf16[2,128,1024]{2,1,0:T(8,128)(2,1)} %collective-permute-done.9.refs_1_.refs_10_), channel_id=1, source_target_pairs={{0,8},{1,5},{2,10},{3,7},{4,0},{5,13},{6,2},{7,15},{8,16},{9,1},{1... | collective-permute-start | bytes 1572872 | tf_op jit(solution)/shard_map/ppermute | solution.py:849
  44.6 3.4 collective-permute-start.13
  45.1 17.6 %collective-permute-start.3 = (bf16[4,128,1024]{2,1,0:T(8,128)(2,1)}, bf16[4,128,1024]{2,1,0:T(8,128)(2,1)}, u32[]{:S(2)}, u32[]{:S(2)}) collective-permute-start(bf16[4,128,1024]{2,1,0:T(8,128)(2,1)} %get-tuple-element.79.refs_3_.refs_12_.refs_21_), channel_id=1, source_target_pairs={{0,1},{1,0},{2,3},{3,2},{4,5},{5,4},{6,7},{7,6},{8,9},{9,8},{10,11... | collective-permute-start | bytes 3145736 | tf_op jit(solution)/shard_map/ppermute | solution.py:849
  45.7 17.0 %collective-permute-start.4 = (bf16[4,128,1024]{2,1,0:T(8,128)(2,1)}, bf16[4,128,1024]{2,1,0:T(8,128)(2,1)}, u32[]{:S(2)}, u32[]{:S(2)}) collective-permute-start(bf16[4,128,1024]{2,1,0:T(8,128)(2,1)} %get-tuple-element.79.refs_3_.refs_12_.refs_21_), channel_id=1, source_target_pairs={{0,8},{1,5},{2,10},{3,7},{4,0},{5,13},{6,2},{7,15},{8,16},{9,1},{1... | collective-permute-start | bytes 3145736 | tf_op jit(solution)/shard_map/ppermute | solution.py:849
  48.8 13.9 %collective-permute-start.16 = (bf16[2,128,1024]{2,1,0:T(8,128)(2,1)}, bf16[2,128,1024]{2,1,0:T(8,128)(2,1)}, u32[]{:S(2)}, u32[]{:S(2)}) collective-permute-start(bf16[2,128,1024]{2,1,0:T(8,128)(2,1)} %get-tuple-element.82.refs_3_.refs_12_), channel_id=1, source_target_pairs={{0,2},{1,3},{2,0},{3,1},{4,6},{5,7},{6,4},{7,5},{8,10},{9,11},{10,... | collective-permute-start | bytes 1572872 | tf_op jit(solution)/shard_map/ppermute | solution.py:849
  50.6 17.1 %collective-permute-start.14 = (bf16[2,128,1024]{2,1,0:T(8,128)(2,1)}, bf16[2,128,1024]{2,1,0:T(8,128)(2,1)}, u32[]{:S(2)}, u32[]{:S(2)}) collective-permute-start(bf16[2,128,1024]{2,1,0:T(8,128)(2,1)} %get-tuple-element.82.refs_3_.refs_12_), channel_id=1, source_target_pairs={{0,1},{1,0},{2,3},{3,2},{4,5},{5,4},{6,7},{7,6},{8,9},{9,8},{10,11... | collective-permute-start | bytes 1572872 | tf_op jit(solution)/shard_map/ppermute | solution.py:849
  50.6 16.3 %collective-permute-start.15 = (bf16[2,128,1024]{2,1,0:T(8,128)(2,1)}, bf16[2,128,1024]{2,1,0:T(8,128)(2,1)S(1)}, u32[]{:S(2)}, u32[]{:S(2)}) collective-permute-start(bf16[2,128,1024]{2,1,0:T(8,128)(2,1)} %get-tuple-element.82.refs_3_.refs_12_), channel_id=1, source_target_pairs={{0,8},{1,5},{2,10},{3,7},{4,0},{5,13},{6,2},{7,15},{8,16},{9,1},{1... | collective-permute-start | bytes 1572872 | tf_op jit(solution)/shard_map/ppermute | solution.py:849
  62.7 5.0 %collective-permute-start.17 = (bf16[2,128,1024]{2,1,0:T(8,128)(2,1)}, bf16[2,128,1024]{2,1,0:T(8,128)(2,1)}, u32[]{:S(2)}, u32[]{:S(2)}) collective-permute-start(bf16[2,128,1024]{2,1,0:T(8,128)(2,1)} %collective-permute-done.16.refs_21_), channel_id=1, source_target_pairs={{0,1},{1,0},{2,3},{3,2},{4,5},{5,4},{6,7},{7,6},{8,9},{9,8},{10,11... | collective-permute-start | bytes 1572872 | tf_op jit(solution)/shard_map/ppermute | solution.py:849
  65.1 9.5 %collective-permute-start.6 = (bf16[4,64,1024]{2,1,0:T(8,128)(2,1)}, bf16[4,64,1024]{2,1,0:T(8,128)(2,1)}, u32[]{:S(2)}, u32[]{:S(2)}) collective-permute-start(bf16[4,64,1024]{2,1,0:T(8,128)(2,1)} %constant_dynamic-slice_fusion.2), channel_id=1, source_target_pairs={{0,8},{1,5},{2,10},{3,7},{4,0},{5,13},{6,2},{7,15},{8,16},{9,1},{1... | collective-permute-start | bytes 1572872 | tf_op jit(solution)/shard_map/ppermute | solution.py:849
  66.2 17.7 %collective-permute-start.5 = (bf16[4,128,1024]{2,1,0:T(8,128)(2,1)}, bf16[4,128,1024]{2,1,0:T(8,128)(2,1)}, u32[]{:S(2)}, u32[]{:S(2)}) collective-permute-start(bf16[4,128,1024]{2,1,0:T(8,128)(2,1)} %get-tuple-element.80.refs_5_.refs_14_.refs_23_), channel_id=1, source_target_pairs={{0,1},{1,0},{2,3},{3,2},{4,5},{5,4},{6,7},{7,6},{8,9},{9,8},{10,11... | collective-permute-start | bytes 3145736 | tf_op jit(solution)/shard_map/ppermute | solution.py:849
  68.4 15.0 %collective-permute-start.21 = (bf16[2,128,1024]{2,1,0:T(8,128)(2,1)}, bf16[2,128,1024]{2,1,0:T(8,128)(2,1)}, u32[]{:S(2)}, u32[]{:S(2)}) collective-permute-start(bf16[2,128,1024]{2,1,0:T(8,128)(2,1)} %get-tuple-element.83.refs_5_.refs_14_), channel_id=1, source_target_pairs={{0,2},{1,3},{2,0},{3,1},{4,6},{5,7},{6,4},{7,5},{8,10},{9,11},{10,... | collective-permute-start | bytes 1572872 | tf_op jit(solution)/shard_map/ppermute | solution.py:849
  74.6 9.1 %collective-permute-start.7 = (bf16[4,64,1024]{2,1,0:T(8,128)(2,1)}, bf16[4,64,1024]{2,1,0:T(8,128)(2,1)}, u32[]{:S(2)}, u32[]{:S(2)}) collective-permute-start(bf16[4,64,1024]{2,1,0:T(8,128)(2,1)} %collective-permute-done.6.refs_1_.refs_7_.refs_16_.refs_25_), channel_id=1, source_target_pairs={{0,1},{1,0},{2,3},{3,2},{4,5},{5,4},{6,7},{7,6},{8,9},{9,8},{10,11... | collective-permute-start | bytes 1572872 | tf_op jit(solution)/shard_map/ppermute | solution.py:849
  74.6 6.7 %collective-permute-start.19 = (bf16[2,64,1024]{2,1,0:T(8,128)(2,1)}, bf16[2,64,1024]{2,1,0:T(8,128)(2,1)}, u32[]{:S(2)}, u32[]{:S(2)}) collective-permute-start(bf16[2,64,1024]{2,1,0:T(8,128)(2,1)} %constant_dynamic-slice_fusion.1.refs_3_), channel_id=1, source_target_pairs={{0,8},{1,5},{2,10},{3,7},{4,0},{5,13},{6,2},{7,15},{8,16},{9,1},{1... | collective-permute-start | bytes 786440 | tf_op jit(solution)/shard_map/ppermute | solution.py:849
  81.3 17.0 %collective-permute-start.20 = (bf16[2,64,1024]{2,1,0:T(8,128)(2,1)}, bf16[2,64,1024]{2,1,0:T(8,128)(2,1)}, u32[]{:S(2)}, u32[]{:S(2)}) collective-permute-start(bf16[2,64,1024]{2,1,0:T(8,128)(2,1)} %collective-permute-done.19.refs_7_.refs_16_), channel_id=1, source_target_pairs={{0,1},{1,0},{2,3},{3,2},{4,5},{5,4},{6,7},{7,6},{8,9},{9,8},{10,11... | collective-permute-start | bytes 786440 | tf_op jit(solution)/shard_map/ppermute | solution.py:849
  81.3 15.3 %collective-permute-start.23 = (bf16[2,64,1024]{2,1,0:T(8,128)(2,1)}, bf16[2,64,1024]{2,1,0:T(8,128)(2,1)S(1)}, u32[]{:S(2)}, u32[]{:S(2)}) collective-permute-start(bf16[2,64,1024]{2,1,0:T(8,128)(2,1)} %collective-permute-done.19.refs_7_.refs_16_), channel_id=1, source_target_pairs={{0,2},{1,3},{2,0},{3,1},{4,6},{5,7},{6,4},{7,5},{8,10},{9,11},{10,... | collective-permute-start | bytes 786440 | tf_op jit(solution)/shard_map/ppermute | solution.py:849
  83.4 15.0 %collective-permute-start.18 = (bf16[2,128,1024]{2,1,0:T(8,128)(2,1)S(1)}, bf16[2,128,1024]{2,1,0:T(8,128)(2,1)}, u32[]{:S(2)}, u32[]{:S(2)}) collective-permute-start(bf16[2,128,1024]{2,1,0:T(8,128)(2,1)S(1)} %copy-done.1), channel_id=1, source_target_pairs={{0,1},{1,0},{2,3},{3,2},{4,5},{5,4},{6,7},{7,6},{8,9},{9,8},{10,11... | collective-permute-start | bytes 1572872 | tf_op jit(solution)/shard_map/ppermute | solution.py:849
  83.7 14.7 %collective-permute-start.22 = (bf16[2,128,1024]{2,1,0:T(8,128)(2,1)}, bf16[2,128,1024]{2,1,0:T(8,128)(2,1)}, u32[]{:S(2)}, u32[]{:S(2)}) collective-permute-start(bf16[2,128,1024]{2,1,0:T(8,128)(2,1)} %collective-permute-done.21.refs_23_), channel_id=1, source_target_pairs={{0,1},{1,0},{2,3},{3,2},{4,5},{5,4},{6,7},{7,6},{8,9},{9,8},{10,11... | collective-permute-start | bytes 1572872 | tf_op jit(solution)/shard_map/ppermute | solution.py:849
  83.9 26.4 %collective-permute-start.8 = (bf16[8,128,1024]{2,1,0:T(8,128)(2,1)}, bf16[8,128,1024]{2,1,0:T(8,128)(2,1)}, u32[]{:S(2)}, u32[]{:S(2)}) collective-permute-start(bf16[8,128,1024]{2,1,0:T(8,128)(2,1)} %get-tuple-element.81.refs_27_), channel_id=1, source_target_pairs={{0,8},{1,5},{2,10},{3,7},{4,0},{5,13},{6,2},{7,15},{8,16},{9,1},{1... | collective-permute-start | bytes 6291464 | tf_op jit(solution)/shard_map/ppermute | solution.py:849
  110.8 26.6 %collective-permute-start.25 = (bf16[8,128,1024]{2,1,0:T(8,128)(2,1)}, bf16[8,128,1024]{2,1,0:T(8,128)(2,1)}, u32[]{:S(2)}, u32[]{:S(2)}) collective-permute-start(bf16[8,128,1024]{2,1,0:T(8,128)(2,1)} %get-tuple-element.86.refs_0_.refs_28_), channel_id=1, source_target_pairs={{0,8},{1,5},{2,10},{3,7},{4,0},{5,13},{6,2},{7,15},{8,16},{9,1},{1... | collective-permute-start | bytes 6291464 | tf_op jit(solution)/shard_map/ppermute | solution.py:849
  138.0 26.7 %collective-permute-start.26 = (bf16[8,128,1024]{2,1,0:T(8,128)(2,1)}, bf16[8,128,1024]{2,1,0:T(8,128)(2,1)}, u32[]{:S(2)}, u32[]{:S(2)}) collective-permute-start(bf16[8,128,1024]{2,1,0:T(8,128)(2,1)} %get-tuple-element.93.refs_27_.refs_30_), channel_id=1, source_target_pairs={{0,8},{1,5},{2,10},{3,7},{4,0},{5,13},{6,2},{7,15},{8,16},{9,1},{1... | collective-permute-start | bytes 6291464 | tf_op jit(solution)/shard_map/ppermute | solution.py:849
  167.4 15.6 %collective-permute-start.30 = (bf16[8,64,1024]{2,1,0:T(8,128)(2,1)}, bf16[8,64,1024]{2,1,0:T(8,128)(2,1)}, u32[]{:S(2)}, u32[]{:S(2)}) collective-permute-start(bf16[8,64,1024]{2,1,0:T(8,128)(2,1)} %constant_dynamic-slice_fusion), channel_id=1, source_target_pairs={{0,8},{1,5},{2,10},{3,7},{4,0},{5,13},{6,2},{7,15},{8,16},{9,1},{1... | collective-permute-start | bytes 3145736 | tf_op jit(solution)/shard_map/ppermute | solution.py:849
  169.0 14.6 %collective-permute-start.27 = (bf16[8,128,1024]{2,1,0:T(8,128)(2,1)}, bf16[8,128,1024]{2,1,0:T(8,128)(2,1)}, u32[]{:S(2)}, u32[]{:S(2)}) collective-permute-start(bf16[8,128,1024]{2,1,0:T(8,128)(2,1)} %get-tuple-element.86.refs_0_.refs_28_), channel_id=1, source_target_pairs={{0,1},{1,0},{2,3},{3,2},{4,5},{5,4},{6,7},{7,6},{8,9},{9,8},{10,11... | collective-permute-start | bytes 6291464 | tf_op jit(solution)/shard_map/ppermute | solution.py:849
  169.0 14.6 %collective-permute-start.28 = (bf16[8,128,1024]{2,1,0:T(8,128)(2,1)}, bf16[8,128,1024]{2,1,0:T(8,128)(2,1)}, u32[]{:S(2)}, u32[]{:S(2)}) collective-permute-start(bf16[8,128,1024]{2,1,0:T(8,128)(2,1)} %get-tuple-element.93.refs_27_.refs_30_), channel_id=1, source_target_pairs={{0,1},{1,0},{2,3},{3,2},{4,5},{5,4},{6,7},{7,6},{8,9},{9,8},{10,11... | collective-permute-start | bytes 6291464 | tf_op jit(solution)/shard_map/ppermute | solution.py:849
  169.5 17.1 %collective-permute-start.29 = (bf16[8,128,1024]{2,1,0:T(8,128)(2,1)}, bf16[8,128,1024]{2,1,0:T(8,128)(2,1)}, u32[]{:S(2)}, u32[]{:S(2)}) collective-permute-start(bf16[8,128,1024]{2,1,0:T(8,128)(2,1)} %get-tuple-element.101.refs_4_.refs_32_), channel_id=1, source_target_pairs={{0,1},{1,0},{2,3},{3,2},{4,5},{5,4},{6,7},{7,6},{8,9},{9,8},{10,11... | collective-permute-start | bytes 6291464 | tf_op jit(solution)/shard_map/ppermute | solution.py:849
  183.5 3.1 collective-permute-start.31
  (6 other events, 20.0 us)
Sparse Core Ops, SparseCore 0:
  232.4 141.8 all-reduce.2
